TPU v7x, 128 devices: a whole 4x4x4 slice. The times are simulated.
128 devices in a mesh: grp: 4 (over z_lo, core), ctx: 32 (over x, z_hi, y).
Axes of the slice: x: 4, y: 4, z: 4 (z_hi: 2, z_lo: 2; z = z_hi * 2 + z_lo), core: 2. Of those that a mesh axis runs over, the one named last changes fastest.
Arguments:
- patches: bfloat16 [4, 4096, 1024], P('grp', 'ctx'), may hold values from -6 to 6
- gain: float32 [1024], replicated, may hold values from 0.5 to 1.5
- w_qkv: bfloat16 [1024, 3072], replicated, as said below
- w_out: bfloat16 [1024, 1024], replicated, may hold values from -0.1875 to 0.1875
- image_ids: int32 [4, 4096], P('grp', 'ctx'), may hold values from 0 to 15, never falling along the last dimension, each value on 1 to 2048 neighbouring positions
- grad_out: bfloat16 [4, 4096, 1024], P('grp', 'ctx'), may hold values from -6 to 6
Outputs:
- out: bfloat16 [4, 4096, 1024], P('grp', 'ctx')
- grad_patches: bfloat16 [4, 4096, 1024], P('grp', 'ctx')
- grad_w_qkv: float32 [1024, 3072], P('ctx')
- grad_w_out: float32 [1024, 1024], P('ctx')
Inputs may be any that keep to these rules, and one draw needn't show every extreme that they name: `image_ids`: along each sequence the ids never fall and take every value from 0 to 15; each image holds at most 2048 patches, and some image in every sequence draw holds exactly 2048. `w_qkv`: every entry lies within plus or minus 6 / sqrt(1024).
All inputs are finite; a program needn't handle non-finite values.
Results may differ from a plain program's by a relative error of at most 0.04.
Values may be sent and summed in bfloat16 or wider, within the bound.
No kernel may reach another device: no remote copies, remote signals or barrier semaphores. Data moves between devices by JAX's collectives and lax.ppermute only.
A program may use at most 256 MiB of HBM per device.

v0:
```python
import math

import jax
import jax.numpy as jnp
from jax import lax
from jax.sharding import PartitionSpec as P

HEADS = 16
HEAD_DIM = 64


EPSILON = 1e-06
NEGATIVE = -1e30


def shards(patches, gain, w_qkv, w_out, image_ids, grad_out):
    tokens = patches[0]
    ident = image_ids[0]
    cotangent = grad_out[0]
    local_rows, model_width = tokens.shape
    head_count = HEADS
    head_size = HEAD_DIM
    score_scale = 1.0 / math.sqrt(head_size)
    values_f = tokens.astype(jnp.float32)
    average = jnp.mean(values_f, axis=1, keepdims=True)
    centered = values_f - average
    variance = jnp.mean(centered * centered, axis=1, keepdims=True)
    inv_std = lax.rsqrt(variance + EPSILON)
    x_hat = centered * inv_std
    normed = (x_hat * gain).astype(jnp.bfloat16)
    qkv = jnp.dot(normed, w_qkv, preferred_element_type=jnp.float32).astype(jnp.bfloat16)
    query = qkv[:, :model_width].reshape(local_rows, head_count, head_size)
    key_value = qkv[:, model_width:]
    own_keys = key_value[:, :model_width].reshape(local_rows, head_count, head_size)
    own_values = key_value[:, model_width:].reshape(local_rows, head_count, head_size)
    kv_all, ids_all = (
        lax.all_gather(key_value, "ctx", axis=0, tiled=True),
        lax.all_gather(ident, "ctx", axis=0, tiled=True),
    )
    seq_len = kv_all.shape[0]
    key_rows = math.gcd(seq_len, 512)
    block_count = seq_len // key_rows
    kv_blocks = kv_all.reshape(block_count, key_rows, 2, head_count, head_size)
    id_blocks = ids_all.reshape(block_count, key_rows)

    def scores_of(query_rows, key_rows_block):
        return (
            jnp.einsum(
                "qhd,khd->hqk", query_rows, key_rows_block, preferred_element_type=jnp.float32
            )
            * score_scale
        )

    def stat_step(running, block_data):
        kv_block, key_ids = block_data
        matches = (ident[:, None] == key_ids[None, :])[None]

        def compute(state):
            row_max, row_sum = state
            masked = jnp.where(matches, scores_of(query, kv_block[:, 0]), NEGATIVE)
            new_max = jnp.maximum(row_max, jnp.max(masked, axis=2))
            added = jnp.sum(jnp.where(matches, jnp.exp(masked - new_max[:, :, None]), 0.0), axis=2)
            return (new_max, row_sum * jnp.exp(row_max - new_max) + added)

        return (compute(running), None)

    start_stats = (
        jnp.full((head_count, local_rows), NEGATIVE, jnp.float32),
        jnp.zeros((head_count, local_rows), jnp.float32),
    )
    (row_max, row_sum), _ = lax.scan(stat_step, start_stats, (kv_blocks, id_blocks))
    log_total = row_max + jnp.log(row_sum)

    def out_step(running, block_data):
        kv_block, key_ids = block_data
        matches = (ident[:, None] == key_ids[None, :])[None]

        def compute(accum):
            masked = jnp.where(matches, scores_of(query, kv_block[:, 0]), NEGATIVE)
            rounded = jnp.where(matches, jnp.exp(masked - log_total[:, :, None]), 0.0).astype(
                jnp.bfloat16
            )
            return accum + jnp.einsum(
                "hqk,khd->qhd", rounded, kv_block[:, 1], preferred_element_type=jnp.float32
            )

        return (compute(running), None)

    zero_rows = jnp.zeros((local_rows, head_count, head_size), jnp.float32)
    attended_f, _ = lax.scan(out_step, zero_rows, (kv_blocks, id_blocks))
    attended = attended_f.reshape(local_rows, model_width).astype(jnp.bfloat16)
    result = jnp.dot(attended, w_out, preferred_element_type=jnp.float32).astype(jnp.bfloat16)
    grad_attended = jnp.einsum(
        "te,de->td", cotangent, w_out, preferred_element_type=jnp.float32
    ).astype(jnp.bfloat16)
    out_part = jnp.einsum("td,te->de", attended, cotangent, preferred_element_type=jnp.float32)
    grad_heads = grad_attended.reshape(local_rows, head_count, head_size)
    attended_heads = attended.reshape(local_rows, head_count, head_size)
    delta = jnp.sum(grad_heads.astype(jnp.float32) * attended_heads.astype(jnp.float32), axis=2).T

    def query_step(running, block_data):
        kv_block, key_ids = block_data
        matches = (ident[:, None] == key_ids[None, :])[None]

        def compute(accum):
            masked = jnp.where(matches, scores_of(query, kv_block[:, 0]), NEGATIVE)
            weights = jnp.where(matches, jnp.exp(masked - log_total[:, :, None]), 0.0)
            prob_grad = jnp.einsum(
                "qhd,khd->hqk", grad_heads, kv_block[:, 1], preferred_element_type=jnp.float32
            )
            score_grad = (weights * (prob_grad - delta[:, :, None]) * score_scale).astype(
                jnp.bfloat16
            )
            return accum + jnp.einsum(
                "hqk,khd->qhd", score_grad, kv_block[:, 0], preferred_element_type=jnp.float32
            )

        return (compute(running), None)

    query_grad, _ = lax.scan(query_step, zero_rows, (kv_blocks, id_blocks))
    stats = jnp.concatenate([log_total.T, delta.T], axis=1)
    stats_all = lax.all_gather(stats, "ctx", axis=0, tiled=True)
    piece_query = lax.all_gather(qkv[:, :model_width], "ctx", axis=0, tiled=True)
    piece_grad = lax.all_gather(grad_attended, "ctx", axis=0, tiled=True)
    extent = piece_query.shape[0]
    matches = (ids_all[:, None] == ident[None, :])[None]

    def compute(state):
        query_rows = piece_query.reshape(extent, head_count, head_size)
        grad_rows = piece_grad.reshape(extent, head_count, head_size)
        masked = jnp.where(matches, scores_of(query_rows, own_keys), NEGATIVE)
        weights = jnp.where(matches, jnp.exp(masked - stats_all[:, :head_count].T[:, :, None]), 0.0)
        rounded = weights.astype(jnp.bfloat16)
        prob_grad = jnp.einsum(
            "qhd,khd->hqk", grad_rows, own_values, preferred_element_type=jnp.float32
        )
        score_grad = (
            weights * (prob_grad - stats_all[:, head_count:].T[:, :, None]) * score_scale
        ).astype(jnp.bfloat16)
        key_grad = jnp.einsum(
            "hqk,qhd->khd", score_grad, query_rows, preferred_element_type=jnp.float32
        )
        value_grad = jnp.einsum(
            "hqk,qhd->khd", rounded, grad_rows, preferred_element_type=jnp.float32
        )
        return (key_grad, value_grad)

    key_grad, value_grad = compute((zero_rows, zero_rows))
    key_grad = key_grad.reshape(local_rows, model_width)
    value_grad = value_grad.reshape(local_rows, model_width)
    grad_qkv = jnp.concatenate(
        [query_grad.reshape(local_rows, model_width), key_grad, value_grad], axis=1
    ).astype(jnp.bfloat16)
    qkv_part = jnp.einsum("td,te->de", normed, grad_qkv, preferred_element_type=jnp.float32)
    grad_normed = (
        jnp.einsum("te,de->td", grad_qkv, w_qkv, preferred_element_type=jnp.float32) * gain
    )
    grad_tokens = inv_std * (
        grad_normed
        - jnp.mean(grad_normed, axis=1, keepdims=True)
        - x_hat * jnp.mean(grad_normed * x_hat, axis=1, keepdims=True)
    )
    qkv_share, out_share = (
        lax.psum_scatter(
            qkv_part.astype(jnp.bfloat16), "ctx", scatter_dimension=0, tiled=True
        ).astype(jnp.float32),
        lax.psum_scatter(
            out_part.astype(jnp.bfloat16), "ctx", scatter_dimension=0, tiled=True
        ).astype(jnp.float32),
    )
    qkv_grad, out_grad = (
        lax.psum(qkv_share.astype(jnp.bfloat16), "grp").astype(jnp.float32),
        lax.psum(out_share.astype(jnp.bfloat16), "grp").astype(jnp.float32),
    )
    factor = 1.0 / math.sqrt(lax.axis_size("grp") * seq_len)
    return (
        result[None],
        grad_tokens.astype(jnp.bfloat16)[None],
        qkv_grad * factor,
        out_grad * factor,
    )


def solution(mesh):
    in_specs = (P("grp", "ctx", None), P(), P(), P(), P("grp", "ctx"), P("grp", "ctx", None))
    out_specs = (P("grp", "ctx", None), P("grp", "ctx", None), P("ctx", None), P("ctx", None))
    return jax.shard_map(shards, mesh=mesh, in_specs=in_specs, out_specs=out_specs, check_vma=False)
```

profile of v0, /device:TPU:1, one launch (start us, length us, event | category | flops | bytes accessed | tf_op | source)
XLA Modules:
  0.0 1293.6 jit_solution(1969812044111071228)
XLA Ops:
  18.7 82.3 %all-gather = s32[1,4096]{1,0:T(1,128)S(1)} all-gather(s32[1,128]{1,0:T(1,128)S(1)} %copy-done.11), channel_id=2, replica_groups=mesh['grp'=4,'ctx'=32] {'ctx'}, dimensions={1}, use_global_device_ids=true | all-gather | bytes 16896 | tf_op jit(solution)/shard_map/all_gather | solution.py:38
  109.2 13.5 %all-gather.7.cloned.1.call-done = bf16[4096,1024]{1,0:T(8,128)(2,1)} async-done(((bf16[128,1024]{1,0:T(8,128)(2,1)}), bf16[4096,1024]{1,0:T(8,128)(2,1)}) %all-gather.7.cloned.1.call-update) | async-done | bytes 8388624 | tf_op jit(solution)/shard_map/all_gather | solution.py:123
  122.7 11.3 copy.28
  134.0 95.1 %all-gather.9.cloned.1.call-done = bf16[4096,1024]{1,0:T(8,128)(2,1)} async-done(((bf16[128,1024]{1,0:T(8,128)(2,1)}), bf16[4096,1024]{1,0:T(8,128)(2,1)}) %all-gather.9.cloned.1.call-update) | async-done | bytes 8388624 | tf_op jit(solution)/shard_map/all_gather | solution.py:124
  229.2 11.3 copy.30
  240.5 16.0 %fusion.70 = f32[16,4096,128]{2,1,0:T(8,128)} fusion(bf16[4096,16,64]{0,2,1:T(8,128)(2,1)} %bitcast.219, bf16[128,16,64]{0,2,1:T(8,128)(2,1)S(1)} %bitcast.226), kind=kOutput, calls=%fused_computation.106 | convolution fusion | flops 1073741824 | bytes 42205184 | tf_op jit(solution)/shard_map/qhd,khd->hqk/dot_general | solution.py:48
  256.5 130.0 %all-gather.5.cloned.1.call-done = bf16[4096,2048]{1,0:T(8,128)(2,1)} async-done(((bf16[128,2048]{1,0:T(8,128)(2,1)}), bf16[4096,2048]{1,0:T(8,128)(2,1)}) %all-gather.5.cloned.1.call-update) | async-done | bytes 16777232 | tf_op jit(solution)/shard_map/all_gather | solution.py:37
  386.5 47.8 %reshape.207 = bf16[8,512,2,16,64]{4,3,2,1,0:T(8,128)(2,1)} reshape(bf16[4096,2048]{1,0:T(8,128)(2,1)} %all-gather.5.cloned.1.call-done) | data formatting | bytes 33554432 | tf_op jit(solution)/shard_map/reshape | solution.py:43
  434.2 35.5 %copy.22 = bf16[8,512,2,16,64]{1,4,3,2,0:T(8,128)(2,1)} copy(bf16[8,512,2,16,64]{4,3,2,1,0:T(8,128)(2,1)} %reshape.207) | data formatting | bytes 33554432
  469.7 65.9 %while.35 = (s32[]{:T(128)}, f32[16,128]{1,0:T(8,128)S(1)}, f32[16,128]{1,0:T(8,128)S(1)}, s32[1,128]{1,0:T(1,128)S(1)}, s32[8,512]{1,0:T(8,128)S(1)}, /*index=5...) while((s32[]{:T(128)}, f32[16,128]{1,0:T(8,128)S(1)}, ...), condition=%wide.region_5.6_spmd.clone, body=%wide.region_2.5_spmd.clone.sunk | while | flops 142682112 | bytes 14203504 | solution.py:71
  535.7 61.5 %while.36 = (s32[]{:T(128)}, f32[128,16,64]{0,2,1:T(8,128)}, bf16[8,512,2,16,64]{1,4,3,2,0:T(8,128)(2,1)}, s32[1,128]{1,0:T(1,128)S(1)}, s32[8,512]{1,0:T(8,128)...) while((s32[]{:T(128)}, f32[128,16,64]{0,2,1:T(8,128)}, ...), condition=%wide.region_7.8_spmd.clone, body=%wide.region_6.7_spmd.clone.sunk | while | flops 274006016 | bytes 7748207 | solution.py:90
  561.9 4.4 fusion.105
  569.6 4.4 fusion.105
  585.0 4.4 fusion.105
  598.3 97.1 %while.37 = (s32[]{:T(128)}, f32[128,16,64]{0,2,1:T(8,128)}, bf16[8,512,2,16,64]{1,4,3,2,0:T(8,128)(2,1)}, s32[1,128]{1,0:T(1,128)S(1)}, s32[8,512]{1,0:T(8,128)...) while((s32[]{:T(128)}, f32[128,16,64]{0,2,1:T(8,128)}, ...), condition=%wide.region_10.11_spmd.clone, body=%wide.region_9.10_spmd.clone.sunk | while | flops 411369472 | bytes 27155124 | solution.py:120
  604.6 6.0 fusion.109
  616.7 6.0 fusion.109
  628.8 6.0 fusion.109
  640.9 6.0 fusion.109
  653.0 6.0 fusion.109
  665.1 6.0 fusion.109
  677.2 6.0 fusion.109
  689.3 6.0 fusion.109
  696.5 79.1 %all_gather.18 = f32[4096,32]{0,1:T(8,128)S(1)} all-gather(f32[128,32]{0,1:T(8,128)S(1)} %pad_maximum_fusion.3), channel_id=1, replica_groups=mesh['grp'=4,'ctx'=32] {'ctx'}, dimensions={0}, use_global_device_ids=true | all-gather | bytes 540672 | tf_op jit(solution)/shard_map/all_gather | solution.py:122
  776.3 27.9 %multiply_convert_fusion.6 = bf16[16,4096,128]{2,1,0:T(8,128)(2,1)} fusion(f32[16,4096,128]{2,1,0:T(8,128)} %fusion.70, f32[16,4096]{1,0:T(8,128)S(1)} %get-tuple-element.311, f32[16,4096]{1,0:T(8,128)S(1)} %get-tuple-element.312, pred[4096,128]{1,0:T(8,128)(4,1)} %broadcast_compare_fusion.3, bf16[4096,16,64]{0,2,1:T(8,128)(2,1)} %bitcast.221, ...), kind=kOutput, calls=%fused_computation.49.clone.clone.clone.clone.1 | convolution fusion | flops 1140850688 | bytes 60030976 | tf_op jit(solution)/shard_map/qhd,khd->hqk/dot_general | solution.py:134
  804.2 11.2 fusion.38
  817.6 17.8 %fusion.39 = bf16[16,64,128]{2,1,0:T(8,128)(2,1)S(1)} fusion(bf16[4096,16,64]{0,2,1:T(8,128)(2,1)} %bitcast.222, f32[16,4096,128]{2,1,0:T(8,128)} %fusion.70, f32[16,4096]{1,0:T(8,128)} %copy-done.10, pred[4096,128]{1,0:T(8,128)(4,1)} %broadcast_compare_fusion.3), kind=kOutput, calls=%fused_computation.64 | convolution fusion | flops 1115815936 | bytes 42991616 | tf_op jit(solution)/shard_map/hqk,qhd->khd/dot_general | solution.py:143
  835.5 4.6 convolution_convert_fusion
  841.6 5.8 fusion.68
  847.4 142.2 %reduce-scatter.5.cloned.1.call-done = bf16[32,1024]{1,0:T(8,128)(2,1)} async-done(((bf16[1024,1024]{1,0:T(8,128)(2,1)}), bf16[32,1024]{1,0:T(8,128)(2,1)}) %reduce-scatter.5.cloned.1.call-update) | async-done | bytes 65552 | tf_op jit(solution)/shard_map/reduce_scatter | solution.py:167
  989.6 255.2 %reduce-scatter.3.cloned.1.call-done = bf16[32,3072]{1,0:T(8,128)(2,1)} async-done(((bf16[1024,3072]{1,0:T(8,128)(2,1)}), bf16[32,3072]{1,0:T(8,128)(2,1)}) %reduce-scatter.3.cloned.1.call-update) | async-done | bytes 196624 | tf_op jit(solution)/shard_map/reduce_scatter | solution.py:164
  1246.7 36.8 %all-reduce.3.cloned.1.call-done = (bf16[32,3072]{1,0:T(8,128)(2,1)}, bf16[32,1024]{1,0:T(8,128)(2,1)}) async-done(((bf16[32,3072]{1,0:T(8,128)(2,1)}, bf16[32,1024]{1,0:T(8,128)(2,1)}), (bf16[32,3072]{1,0:T(8,128)(2,1)}, bf16[32,1024]{1,0:T(8,128)(2,1)})) %all-reduce.3.cloned.1.call-update) | async-done | bytes 262160 | tf_op jit(solution)/shard_map/psum | solution.py:172
  (230 shorter events, 193.2 us)
Async XLA Ops:
  7.2 7.5 copy-start
  7.2 115.5 %all-gather.7.cloned.1.call-start = ((), (), s32[]{:S(2)}) async-start(), calls=%async_computation.3 | async-start | bytes 8650752 | tf_op jit(solution)/shard_map/all_gather | solution.py:123
  8.4 5.2 copy-start.12
  9.6 4.0 copy-start.14
  9.6 5.0 copy-start.4
  13.7 5.0 copy-start.11
  14.6 2.6 copy-start.3
  14.6 214.5 %all-gather.9.cloned.1.call-start = ((), (), s32[]{:S(2)}) async-start(), calls=%async_computation.4 | async-start | bytes 8650752 | tf_op jit(solution)/shard_map/all_gather | solution.py:124
  16.2 370.2 %all-gather.5.cloned.1.call-start = ((), (), s32[]{:S(2)}) async-start(), calls=%async_computation.2 | async-start | bytes 17301504 | tf_op jit(solution)/shard_map/all_gather | solution.py:37
  17.2 972.4 %reduce-scatter.5.cloned.1.call-start = ((), (), s32[]{:S(2)}) async-start(), calls=%async_computation.6 | async-start | bytes 2162688 | tf_op jit(solution)/shard_map/reduce_scatter | solution.py:167
  17.4 86.3 %copy-start.6 = (bf16[128,1024]{0,1:T(8,128)(2,1)}, bf16[128,1024]{0,1:T(8,128)(2,1)S(1)}, u32[]{:S(2)}) copy-start(bf16[128,1024]{0,1:T(8,128)(2,1)S(1)} %copy.20) | copy-start | bytes 786436
  434.2 35.5 %copy-start.7 = (bf16[128,1024]{0,1:T(8,128)(2,1)S(1)}, bf16[128,1024]{0,1:T(8,128)(2,1)}, u32[]{:S(2)}) copy-start(bf16[128,1024]{0,1:T(8,128)(2,1)} %copy-done.6) | copy-start | bytes 786436
  598.5 6.1 copy-start.8
  600.4 1.3 copy-start.1
  610.6 6.1 copy-start.8
  612.5 1.3 copy-start.1
  622.7 6.1 copy-start.8
  624.6 1.3 copy-start.1
  634.8 6.1 copy-start.8
  636.7 1.3 copy-start.1
  646.9 6.1 copy-start.8
  648.8 1.3 copy-start.1
  659.0 6.1 copy-start.8
  671.1 6.1 copy-start.8
  683.2 6.1 copy-start.8
  804.2 11.2 copy-start.5
  817.5 17.9 %copy-start.2 = (bf16[1,128,1024]{2,1,0:T(8,128)(2,1)S(1)}, bf16[1,128,1024]{2,1,0:T(8,128)(2,1)}, u32[]{:S(2)}) copy-start(bf16[1,128,1024]{2,1,0:T(8,128)(2,1)} %param.12) | copy-start | bytes 786436
  817.5 17.9 %copy-start.9 = (f32[1024]{0:T(1024)S(1)}, f32[1024]{0:T(1024)}, u32[]{:S(2)}) copy-start(f32[1024]{0:T(1024)} %param.13) | copy-start | bytes 12292
  817.5 17.9 %copy-start.13 = (f32[128]{0:T(128)S(1)}, f32[128]{0:T(128)}, u32[]{:S(2)}) copy-start(f32[128]{0:T(128)} %copy-done.12) | copy-start | bytes 1540
  817.5 17.9 %copy-start.15 = (f32[128]{0:T(128)S(1)}, f32[128]{0:T(128)}, u32[]{:S(2)}) copy-start(f32[128]{0:T(128)} %copy-done.14) | copy-start | bytes 1540
  817.5 427.2 %reduce-scatter.3.cloned.1.call-start = ((), (), s32[]{:S(2)}) async-start(), calls=%async_computation.5 | async-start | bytes 6488064 | tf_op jit(solution)/shard_map/reduce_scatter | solution.py:164
  840.1 443.5 %all-reduce.3.cloned.1.call-start = ((), (), s32[]{:S(2)}) async-start(), calls=%async_computation.7 | async-start | bytes 524288 | tf_op jit(solution)/shard_map/psum | solution.py:172
  (4 other events, 4.6 us)
Sparse Core Ops, SparseCore 0:
  14.7 107.9 all-gather.6
  126.4 102.7 all-gather.8
  232.2 154.1 all-gather.4
  817.6 171.9 reduce-scatter.4
  995.4 249.3 reduce-scatter.2
  1247.3 36.2 all-reduce.2
where the time goes:
time: 1300 us; the launch traced here: 1290 us
  waiting for transfers between devices  673 us (52%)
  matrix products  222 us (17%)
  local copies, waits for them, and re-layouts  180 us (14%)
  blocking collectives  161 us (12%)
  other arithmetic  41.2 us (3%)
  between operations  14.4 us (1%)
    reduce_scatter x1, waiting for transfers between devices, shards(): lax.psum_scatter(qkv_part.astype(jnp.bfloat16), 'ctx', scatter_dimension=...  255 us
    reduce_scatter x1, waiting for transfers between devices, shards(): lax.psum_scatter(out_part.astype(jnp.bfloat16), 'ctx', scatter_dimension=...  142 us
    all_gather x1, waiting for transfers between devices, shards(): lax.all_gather(key_value, 'ctx', axis=0, tiled=True)  130 us
    all_gather x1, waiting for transfers between devices, shards(): piece_grad = lax.all_gather(grad_attended, 'ctx', axis=0, tiled=True)  95.1 us
    all_gather x1, blocking collectives, shards(): lax.all_gather(ident, 'ctx', axis=0, tiled=True)  82.3 us
    all_gather x1, blocking collectives, shards(): stats_all = lax.all_gather(stats, 'ctx', axis=0, tiled=True)  79.1 us
    dot_general x17, matrix products, scores_of(): jnp.einsum('qhd,khd->hqk', query_rows, key_rows_block, preferred_element_...  62.4 us
    squeeze x24, local copies, waits for them, and re-layouts, shards(): lax.scan(stat_step, start_stats, (kv_blocks, id_blocks))  54.6 us
  transfers between devices with their start and end apart: 6, of which 6 were waited for; matrix products, arithmetic and copies ran while one was open for 6% of the time, Pallas kernels for 0%

commit v1 on v0

v1 whole, which is shorter than its diff:
```python
import functools
import math

import jax
import jax.numpy as jnp
from jax import lax
from jax.experimental import pallas as pl
from jax.experimental.pallas import tpu as pltpu
from jax.sharding import PartitionSpec as P

HEADS = 16
HEAD_DIM = 64
D = HEADS * HEAD_DIM
TOK = 128
HALF = TOK // 2
N_CTX = 32
N_GRP = 4
SEQ = TOK * N_CTX
ID_ROWS = 16
IN_ROWS = TOK + HALF + ID_ROWS
OUT_ROWS = TOK + HALF
TQ = 256
TK = 512
Q_SRC = TQ // HALF
N_QB = N_CTX // Q_SRC
EPSILON = 1e-06
MASK = -1e30
VMEM = 56 * 1024 * 1024
F32 = jnp.float32
BF16 = jnp.bfloat16


def dot_nn(a, b):
    return jnp.dot(a, b, preferred_element_type=F32)


def dot_nt(a, b):
    return lax.dot_general(a, b, (((1,), (1,)), ((), ())), preferred_element_type=F32)


def dot_tn(a, b):
    return lax.dot_general(a, b, (((0,), (0,)), ((), ())), preferred_element_type=F32)


def lanes(shape):
    return lax.broadcasted_iota(jnp.int32, shape, 1)


def project_kernel(x_ref, cot_ref, gain_ref, ids_ref, wq_ref, wk_ref, wv_ref, wo_ref, send_ref, normed_ref):
    @pl.when(pl.program_id(0) == 0)
    def _():
        x = x_ref[...].astype(F32)
        cen = x - jnp.mean(x, axis=1, keepdims=True)
        inv = lax.rsqrt(jnp.mean(cen * cen, axis=1, keepdims=True) + EPSILON)
        normed_ref[...] = (cen * inv * gain_ref[...]).astype(BF16)

    n = normed_ref[...]
    q = dot_nn(n, wq_ref[...])
    k = dot_nn(n, wk_ref[...])
    v = dot_nn(n, wv_ref[...])
    g = dot_nt(cot_ref[...], wo_ref[...])
    ids = ids_ref[...].astype(F32)
    rolled = jnp.concatenate([ids[:, HALF:], ids[:, :HALF]], axis=1)
    for h in range(4):
        cols = slice(h * HEAD_DIM, (h + 1) * HEAD_DIM)
        kv = jnp.concatenate([k[:, cols], v[:, cols]], axis=1).astype(BF16)
        qg = jnp.concatenate([q[:, cols], g[:, cols]], axis=1).astype(BF16)
        for p in range(2):
            own = ids if p == 0 else rolled
            rows = jnp.concatenate(
                [jnp.broadcast_to(ids, (8, TOK)), jnp.broadcast_to(own, (8, TOK))], axis=0
            )
            send_ref[2 * h + p, :TOK, :] = kv
            send_ref[2 * h + p, TOK:OUT_ROWS, :] = qg[p * HALF:(p + 1) * HALF, :]
            send_ref[2 * h + p, OUT_ROWS:, :] = rows.astype(BF16)


def project(x, cot, gain, ids, w_qkv, w_out):
    whole = lambda shape: pl.BlockSpec(shape, lambda j: (0, 0))
    return pl.pallas_call(
        project_kernel,
        grid=(4,),
        in_specs=[
            whole((TOK, D)),
            whole((TOK, D)),
            whole((1, D)),
            whole((1, TOK)),
            pl.BlockSpec((D, 256), lambda j: (0, j)),
            pl.BlockSpec((D, 256), lambda j: (0, 4 + j)),
            pl.BlockSpec((D, 256), lambda j: (0, 8 + j)),
            pl.BlockSpec((256, D), lambda j: (j, 0)),
        ],
        out_specs=[pl.BlockSpec((8, IN_ROWS, TOK), lambda j: (j, 0, 0)), whole((TOK, D))],
        out_shape=[
            jax.ShapeDtypeStruct((N_CTX, IN_ROWS, TOK), BF16),
            jax.ShapeDtypeStruct((TOK, D), BF16),
        ],
        compiler_params=pltpu.CompilerParams(vmem_limit_bytes=VMEM),
        name="project",
    )(x, cot, gain, ids, w_qkv, w_qkv, w_qkv, w_out)


def attend_kernel(recv_ref, send_ref, kx, kvt, idm, sc, acc):
    lane = lanes((TOK, TOK))

    def prepare(c, carry):
        kv = recv_ref[c, :TOK, :].astype(F32)
        idrow = recv_ref[c, OUT_ROWS:, :].astype(F32)[:1]
        idm[pl.ds(c, 1), :] = idrow
        idcol = jnp.broadcast_to(idrow, (TOK, TOK)).T
        onehot = jnp.where(lane.astype(F32) - HEAD_DIM == idcol, 1.0, 0.0)
        rows = pl.ds(pl.multiple_of(c * TOK, TOK), TOK)
        kx[rows, :] = jnp.where(lane < HEAD_DIM, kv, onehot).astype(BF16)
        kvt[:, rows] = kv.T.astype(BF16)
        acc[rows, :] = jnp.zeros((TOK, TOK), F32)
        return carry

    lax.fori_loop(0, N_CTX, prepare, 0, unroll=4)

    lane_q = lanes((TQ, TOK))

    def fold(tile, op):
        out = tile[0:8]
        for r in range(8, tile.shape[0], 8):
            out = op(out, tile[r:r + 8])
        return out

    def query_block(i, carry):
        c0 = i * Q_SRC
        qd = recv_ref[pl.ds(c0, Q_SRC), TOK:OUT_ROWS, :].reshape(TQ, TOK).astype(F32)
        idcols = []
        lowest, highest = None, None
        for a in range(Q_SRC):
            both = recv_ref[c0 + a, OUT_ROWS:, :].astype(F32)
            idcols.append(jnp.broadcast_to(both[8:9], (TOK, TOK)).T[:HALF])
            lowest = both if lowest is None else jnp.minimum(lowest, both)
            highest = both if highest is None else jnp.maximum(highest, both)
        idcol = jnp.concatenate(idcols, axis=0)
        every = idm[...]
        below = jnp.sum(jnp.where(every < jnp.min(lowest), 1.0, 0.0)).astype(jnp.int32)
        upto = jnp.sum(jnp.where(every <= jnp.max(highest), 1.0, 0.0)).astype(jnp.int32)
        first = below // TK
        last = (upto + (TK - 1)) // TK

        other = jnp.where(
            (lane_q < HEAD_DIM + HEADS) & (lane_q.astype(F32) - HEAD_DIM != idcol), MASK, 0.0
        )
        qx = jnp.where(lane_q < HEAD_DIM, qd * 0.125, other)
        qxt = qx.T.astype(BF16)
        gz = jnp.where(lane_q >= HEAD_DIM, qd, 0.0)
        gzt_f = gz.T
        gzt = gzt_f.astype(BF16)

        def at(kb):
            return pl.ds(pl.multiple_of(kb * TK, TK), TK)

        def score_step(kb, top):
            s = dot_nn(kx[at(kb), :], qxt)
            sc[at(kb), :] = s
            return jnp.maximum(top, fold(s, jnp.maximum))

        top = lax.fori_loop(first, last, score_step, jnp.full((8, TQ), MASK, F32))
        top = jnp.max(top, axis=0, keepdims=True)

        def value_step(kb, state):
            total, ot = state
            e = jnp.exp(sc[at(kb), :] - top)
            sc[at(kb), :] = e
            return (
                total + fold(e, jnp.add),
                ot + dot_nn(kvt[HEAD_DIM:, at(kb)], e.astype(BF16)),
            )

        total, ot = lax.fori_loop(
            first, last, value_step, (jnp.zeros((8, TQ), F32), jnp.zeros((HEAD_DIM, TQ), F32))
        )
        inv = 1.0 / jnp.sum(total, axis=0, keepdims=True)
        ot = (ot * inv).astype(BF16).astype(F32)
        delta = jnp.sum(ot * gzt_f[HEAD_DIM:], axis=0, keepdims=True)

        scaled = (qd.T * inv).T
        right_q = jnp.where(lane_q < HEAD_DIM, scaled * 0.125, 0.0).astype(BF16)
        right_g = jnp.where(lane_q >= HEAD_DIM, scaled, 0.0).astype(BF16)

        def grad_step(kb, dqt):
            rows = recv_ref[pl.ds(kb * (TK // TOK), TK // TOK), :TOK, :].reshape(TK, TOK)
            dp = dot_nn(rows, gzt)
            e = sc[at(kb), :]
            ds = (e * (dp - delta)).astype(BF16)
            acc[at(kb), :] += dot_nn(ds, right_q) + dot_nn(e.astype(BF16), right_g)
            return dqt + dot_nn(kvt[:HEAD_DIM, at(kb)], ds)

        dqt = lax.fori_loop(first, last, grad_step, jnp.zeros((HEAD_DIM, TQ), F32))
        both = jnp.concatenate([ot, dqt * (inv * 0.125)], axis=0).T.astype(BF16)
        for a in range(Q_SRC):
            send_ref[c0 + a, TOK:, :] = both[a * HALF:(a + 1) * HALF]
        return carry

    lax.fori_loop(0, N_QB, query_block, 0)

    def finish(c, carry):
        rows = pl.ds(pl.multiple_of(c * TOK, TOK), TOK)
        send_ref[c, :TOK, :] = acc[rows, :].astype(BF16)
        return carry

    lax.fori_loop(0, N_CTX, finish, 0, unroll=4)


def attend(recv):
    vmem = pl.BlockSpec(memory_space=pltpu.VMEM)
    return pl.pallas_call(
        attend_kernel,
        in_specs=[vmem],
        out_specs=vmem,
        out_shape=jax.ShapeDtypeStruct((N_CTX, OUT_ROWS, TOK), BF16),
        scratch_shapes=[
            pltpu.VMEM((SEQ, TOK), BF16),
            pltpu.VMEM((TOK, SEQ), BF16),
            pltpu.VMEM((N_CTX, TOK), F32),
            pltpu.VMEM((SEQ, TQ), F32),
            pltpu.VMEM((SEQ, TOK), F32),
        ],
        compiler_params=pltpu.CompilerParams(vmem_limit_bytes=VMEM),
        name="attend",
    )(recv)


def unproject_kernel(recv_ref, x_ref, gain_ref, wq_ref, wk_ref, wv_ref, wo_ref, out_ref, gx_ref, cols_ref, sum_out, sum_g, sum_sel):
    step = pl.program_id(0)

    @pl.when(step == 0)
    def _():
        sum_out[...] = jnp.zeros_like(sum_out)
        sum_g[...] = jnp.zeros_like(sum_g)
        sum_sel[...] = jnp.zeros_like(sum_sel)

    att, dq, dk, dv = [], [], [], []
    for h in range(4):
        lo, hi = recv_ref[2 * h].astype(F32), recv_ref[2 * h + 1].astype(F32)
        kv = lo[:TOK] + hi[:TOK]
        aq = jnp.concatenate([lo[TOK:], hi[TOK:]], axis=0)
        att.append(aq[:, :HEAD_DIM])
        dq.append(aq[:, HEAD_DIM:])
        dk.append(kv[:, :HEAD_DIM])
        dv.append(kv[:, HEAD_DIM:])
    att, dq, dk, dv = [jnp.concatenate(t, axis=1).astype(BF16) for t in (att, dq, dk, dv)]

    row = lax.broadcasted_iota(jnp.int32, (256, D), 0) + step * 256
    place = ((row % 32) // 8) * 256 + (row // 32) * 8 + row % 8
    chosen = jnp.where(lanes((256, D)) == place, 1.0, 0.0).astype(BF16)
    sum_sel[...] += dot_nn(att, chosen)
    sum_out[...] += dot_nn(att, wo_ref[...])
    sum_g[...] += dot_nt(dq, wq_ref[...]) + dot_nt(dk, wk_ref[...]) + dot_nt(dv, wv_ref[...])
    cols_ref[step, :, :256] = dq
    cols_ref[step, :, 256:512] = dk
    cols_ref[step, :, 512:768] = dv

    @pl.when(step == 3)
    def _():
        out_ref[...] = sum_out[...].astype(BF16)
        for j in range(N_GRP):
            cols_ref[j, :, 768:] = sum_sel[:, j * 256:(j + 1) * 256].astype(BF16)
        x = x_ref[...].astype(F32)
        cen = x - jnp.mean(x, axis=1, keepdims=True)
        inv = lax.rsqrt(jnp.mean(cen * cen, axis=1, keepdims=True) + EPSILON)
        x_hat = cen * inv
        g = sum_g[...] * gain_ref[...]
        gx = inv * (
            g - jnp.mean(g, axis=1, keepdims=True) - x_hat * jnp.mean(g * x_hat, axis=1, keepdims=True)
        )
        gx_ref[...] = gx.astype(BF16)


def unproject(recv, x, gain, w_qkv, w_out):
    whole = lambda shape: pl.BlockSpec(shape, lambda j: (0,) * len(shape))
    return pl.pallas_call(
        unproject_kernel,
        grid=(4,),
        in_specs=[
            pl.BlockSpec((8, OUT_ROWS, TOK), lambda j: (j, 0, 0)),
            whole((TOK, D)),
            whole((1, D)),
            pl.BlockSpec((D, 256), lambda j: (0, j)),
            pl.BlockSpec((D, 256), lambda j: (0, 4 + j)),
            pl.BlockSpec((D, 256), lambda j: (0, 8 + j)),
            pl.BlockSpec((256, D), lambda j: (j, 0)),
        ],
        out_specs=[whole((TOK, D)), whole((TOK, D)), whole((N_GRP, TOK, D))],
        out_shape=[
            jax.ShapeDtypeStruct((TOK, D), BF16),
            jax.ShapeDtypeStruct((TOK, D), BF16),
            jax.ShapeDtypeStruct((N_GRP, TOK, D), BF16),
        ],
        scratch_shapes=[pltpu.VMEM((TOK, D), F32)] * 3,
        compiler_params=pltpu.CompilerParams(vmem_limit_bytes=VMEM),
        name="unproject",
    )(recv, x, gain, w_qkv, w_qkv, w_qkv, w_out)


def weights_kernel(both_ref, cols_ref, send_ref):
    both = both_ref[...].reshape(N_GRP * TOK, 2 * D)
    cols = cols_ref[...].reshape(N_GRP * TOK, D)
    for m in range(4):
        part = dot_tn(both[:, m * 256:(m + 1) * 256], cols[:, :768])
        for c in range(8):
            send_ref[8 * m + c, :, :768] = part[32 * c:32 * c + 32].astype(BF16)
    part = dot_tn(cols[:, 768:], both[:, D:])
    for c in range(N_CTX):
        rows = part[8 * c:8 * c + 8]
        piece = jnp.concatenate([rows[:, q * 256:(q + 1) * 256] for q in range(4)], axis=0)
        send_ref[c, :, 768:] = piece.astype(BF16)


def weights(both, cols):
    vmem = pl.BlockSpec(memory_space=pltpu.VMEM)
    return pl.pallas_call(
        weights_kernel,
        in_specs=[vmem, vmem],
        out_specs=vmem,
        out_shape=jax.ShapeDtypeStruct((N_CTX, 32, D), BF16),
        compiler_params=pltpu.CompilerParams(vmem_limit_bytes=VMEM),
        name="weights",
    )(both, cols)


def shards(patches, gain, w_qkv, w_out, image_ids, grad_out):
    x, cot = patches[0], grad_out[0]
    gain_row = gain[None]
    send, normed = project(x, cot, gain_row, image_ids, w_qkv, w_out)
    recv = lax.all_to_all(send, "ctx", 0, 0, tiled=True)
    both = lax.all_gather(jnp.concatenate([normed, cot], axis=1), "grp", axis=0)
    back = lax.all_to_all(attend(recv), "ctx", 0, 0, tiled=True)
    out, grad_x, cols = unproject(back, x, gain_row, w_qkv, w_out)
    cols = lax.all_to_all(cols, "grp", 0, 0, tiled=True)
    parts = lax.all_to_all(weights(both, cols), "ctx", 0, 0, tiled=True)
    factor = 1.0 / math.sqrt(N_GRP * SEQ)
    share = (jnp.sum(parts.astype(F32), axis=0) * factor).astype(BF16)
    full = lax.all_gather(share, "grp", axis=0).astype(F32)
    grad_qkv = full[:, :, :768].reshape(N_GRP, 32, 3, 256).transpose(1, 2, 0, 3).reshape(32, 3 * D)
    grad_out_w = full[:, :, 768:].reshape(N_GRP, 4, 8, 256).transpose(0, 2, 1, 3).reshape(32, D)
    return out[None], grad_x[None], grad_qkv, grad_out_w


def solution(mesh):
    in_specs = (P("grp", "ctx", None), P(), P(), P(), P("grp", "ctx"), P("grp", "ctx", None))
    out_specs = (P("grp", "ctx", None), P("grp", "ctx", None), P("ctx", None), P("ctx", None))
    return jax.shard_map(shards, mesh=mesh, in_specs=in_specs, out_specs=out_specs, check_vma=False)
```

time: 1300 us -> 202 us (0.16)
  waiting for transfers between devices: 673 us -> 36.1 us
  matrix products: 222 us -> 0 us
  local copies, waits for them, and re-layouts: 180 us -> 4.26 us
  blocking collectives: 161 us -> 66.3 us
  Pallas kernels: 0 us -> 60 us
  other arithmetic: 41.2 us -> 1.24 us
  starting transfers between devices: 0.51 us -> 19 us
    reduce_scatter x2 -> x0, waiting for transfers between devices: 397 us -> none  [the longest x1 255 us: shards(): lax.psum_scatter(qkv_part.astype(jnp.bfloat16), 'ctx', scatter_dimension=...]
    all_gather x3 -> x1, waiting for transfers between devices: 239 us -> 0.01 us  [shards(): both = lax.all_gather(jnp.concatenate([normed, cot], axis=1), 'grp', axis=0)]
    dot_general x42 -> x0, matrix products: 222 us -> none  [the longest x17 62.4 us: scores_of(): jnp.einsum('qhd,khd->hqk', query_rows, key_rows_block, preferred_element_...]
    all_gather x2 -> x1, blocking collectives: 161 us -> 8.78 us  [shards(): full = lax.all_gather(share, 'grp', axis=0).astype(F32)]
    pallas_call x0 -> x4, Pallas kernels: none -> 60 us  [the longest x1 39.9 us: attend(): pl.pallas_call(attend_kernel, in_specs=[vmem], out_specs=vmem, out_shape=...]
    all_to_all x0 -> x2, blocking collectives: none -> 57.5 us  [the longest x1 31.3 us: shards(): parts = lax.all_to_all(weights(both, cols), 'ctx', 0, 0, tiled=True)]
    squeeze x24 -> x0, local copies, waits for them, and re-layouts: 54.6 us -> none  [shards(): lax.scan(stat_step, start_stats, (kv_blocks, id_blocks))]
    reshape x2, local copies, waits for them, and re-layouts: 47.8 us -> 1.16 us  [shards(): full[:, :, :768].reshape(N_GRP, 32, 3, 256).transpose(1, 2, 0, 3)]
  transfers between devices with their start and end apart: 6 -> 3, of which waited for: 6 -> 2; matrix products, arithmetic and copies ran while one was open for 6% -> 0% of each run, Pallas kernels for 0% -> 24%
where the time goes in v1:
time: 202 us; the launch traced here: 201 us
  blocking collectives  66.3 us (33%)
  Pallas kernels  60 us (30%)
  waiting for transfers between devices  36.1 us (18%)
  starting transfers between devices  19 us (9%)
  between operations  14.1 us (7%)
  local copies, waits for them, and re-layouts  4.26 us (2%)
    pallas_call x1, Pallas kernels, attend(): pl.pallas_call(attend_kernel, in_specs=[vmem], out_specs=vmem, out_shape=...  39.9 us
    all_to_all x1, blocking collectives, shards(): parts = lax.all_to_all(weights(both, cols), 'ctx', 0, 0, tiled=True)  31.3 us
    all_to_all x1, blocking collectives, shards(): back = lax.all_to_all(attend(recv), 'ctx', 0, 0, tiled=True)  26.2 us
    all_to_all x1, waiting for transfers between devices, shards(): recv = lax.all_to_all(send, 'ctx', 0, 0, tiled=True)  22.8 us
    all_to_all x1, waiting for transfers between devices, shards(): cols = lax.all_to_all(cols, 'grp', 0, 0, tiled=True)  13.4 us
    all_to_all x1, starting transfers between devices, shards(): recv = lax.all_to_all(send, 'ctx', 0, 0, tiled=True)  11.3 us
    pallas_call x1, Pallas kernels, unproject(): pl.pallas_call(unproject_kernel, grid=(4,), in_specs=[pl.BlockSpec((8, OU...  8.89 us
    all_gather x1, blocking collectives, shards(): full = lax.all_gather(share, 'grp', axis=0).astype(F32)  8.78 us
  transfers between devices with their start and end apart: 3, of which 2 were waited for; matrix products, arithmetic and copies ran while one was open for 0% of the time, Pallas kernels for 24%

profile of v1, /device:TPU:1, one launch (start us, length us, event | category | flops | bytes accessed | tf_op | source)
XLA Modules:
  0.0 201.0 jit_solution(11514378398629611979)
XLA Ops:
  7.2 6.8 %project.1 = (bf16[32,208,128]{2,1,0:T(8,128)(2,1)}, bf16[128,1024]{1,0:T(8,128)(2,1)}) custom-call(bf16[128,1024]{1,0:T(8,128)(2,1)} %bitcast.18, bf16[128,1024]{1,0:T(8,128)(2,1)} %bitcast.20, f32[1,1024]{1,0:T(1,128)} %bitcast.23, s32[1,128]{1,0:T(1,128)} %ids_ref.1, bf16[1024,3072]{1,0:T(8,128)(2,1)} %wv_ref.3, bf16[1024,3072]{1,0:T(8,128)(2,1)} %wv_ref.3, ...), custom_call_target="tpu_custom_call" | custom-call | tf_op jit(solution)/shard_map/project/pallas_call | solution.py:80
  13.9 0.0 copy-start.2
  13.9 0.0 copy-start.3
  13.9 11.3 %all-to-all-start = ((bf16[32,208,128]{2,1,0:T(8,128)(2,1)}), bf16[32,208,128]{2,1,0:T(8,128)(2,1)S(1)}, u32[]{:S(2)}, u32[]{:S(2)}) async-start(bf16[32,208,128]{2,1,0:T(8,128)(2,1)} %get-tuple-element.9), calls=%async_computation | async-start | bytes 3407872 | tf_op jit(solution)/shard_map/all_to_all | solution.py:330
  25.3 0.0 all-gather.4.cloned.1.call-start
  25.3 0.0 copy-done.2
  25.3 0.0 copy-done.3
  25.3 0.9 pad_maximum_fusion
  26.2 0.0 all-gather.4.cloned.1.call-update
  26.2 22.8 %all-to-all-done.recv_ref = bf16[32,208,128]{2,1,0:T(8,128)(2,1)S(1)} async-done(((bf16[32,208,128]{2,1,0:T(8,128)(2,1)}), bf16[32,208,128]{2,1,0:T(8,128)(2,1)S(1)}, u32[]{:S(2)}, u32[]{:S(2)}) %all-to-all-start) | async-done | bytes 1703968 | tf_op jit(solution)/shard_map/all_to_all | solution.py:330
  49.0 0.0 copy-start
  49.0 1.2 copy-done
  50.2 39.9 %attend.1 = bf16[32,192,128]{2,1,0:T(8,128)(2,1)} custom-call(bf16[32,208,128]{2,1,0:T(8,128)(2,1)} %copy-done), custom_call_target="tpu_custom_call" | custom-call | tf_op jit(solution)/shard_map/attend/pallas_call | solution.py:211
  90.1 26.2 %all_to_all.20.recv_ref = bf16[32,192,128]{2,1,0:T(8,128)(2,1)} all-to-all(bf16[32,192,128]{2,1,0:T(8,128)(2,1)} %attend.1), channel_id=1, replica_groups=mesh['grp'=4,'ctx'=32] {'ctx'}, dimensions={0} | all-to-all | bytes 3145728 | tf_op jit(solution)/shard_map/all_to_all | solution.py:332
  116.3 8.9 %unproject.1 = (bf16[128,1024]{1,0:T(8,128)(2,1)}, bf16[128,1024]{1,0:T(8,128)(2,1)}, bf16[4,128,1024]{2,1,0:T(8,128)(2,1)}) custom-call(bf16[32,192,128]{2,1,0:T(8,128)(2,1)} %all_to_all.20.recv_ref, bf16[128,1024]{1,0:T(8,128)(2,1)} %bitcast.19, f32[1,1024]{1,0:T(1,128)} %bitcast.24, bf16[1024,3072]{1,0:T(8,128)(2,1)} %wv_ref.3, ...), custom_call_target="tpu_custom_call" | custom-call | tf_op jit(solution)/shard_map/unproject/pallas_call | solution.py:276
  125.2 7.6 %all-to-all-start.2 = ((bf16[4,128,1024]{2,1,0:T(8,128)(2,1)}), bf16[4,128,1024]{2,1,0:T(8,128)(2,1)S(1)}, u32[]{:S(2)}, u32[]{:S(2)}) async-start(bf16[4,128,1024]{2,1,0:T(8,128)(2,1)} %get-tuple-element.13), calls=%async_computation.2 | async-start | bytes 2097152 | tf_op jit(solution)/shard_map/all_to_all | solution.py:334
  132.8 0.0 all-gather.4.cloned.1.call-done
  132.8 13.4 %all-to-all-done.2.cols_ref = bf16[4,128,1024]{2,1,0:T(8,128)(2,1)S(1)} async-done(((bf16[4,128,1024]{2,1,0:T(8,128)(2,1)}), bf16[4,128,1024]{2,1,0:T(8,128)(2,1)S(1)}, u32[]{:S(2)}, u32[]{:S(2)}) %all-to-all-start.2) | async-done | bytes 1048608 | tf_op jit(solution)/shard_map/all_to_all | solution.py:334
  146.2 0.0 copy-start.1
  146.2 1.0 copy-done.1
  147.1 4.5 %weights.1 = bf16[32,32,1024]{2,1,0:T(8,128)(2,1)} custom-call(bf16[4,128,2048]{2,1,0:T(8,128)(2,1)} %bitcast.17, bf16[4,128,1024]{2,1,0:T(8,128)(2,1)} %copy-done.1), custom_call_target="tpu_custom_call" | custom-call | tf_op jit(solution)/shard_map/weights/pallas_call | solution.py:316
  151.6 31.3 %all_to_all.21 = bf16[32,32,1024]{2,1,0:T(8,128)(2,1)S(1)} all-to-all(bf16[32,32,1024]{2,1,0:T(8,128)(2,1)} %weights.1), channel_id=1, replica_groups=mesh['grp'=4,'ctx'=32] {'ctx'}, dimensions={0} | all-to-all | bytes 4194304 | tf_op jit(solution)/shard_map/all_to_all | solution.py:335
  182.9 0.4 convert_reduce_fusion
  183.3 8.8 %all-gather.1 = bf16[128,1024]{1,0:T(8,128)(2,1)S(1)} all-gather(bf16[32,1024]{1,0:T(8,128)(2,1)S(1)} %multiply_convert_fusion), channel_id=3, replica_groups=mesh['grp'=4,'ctx'=32] {'grp'}, dimensions={0}, use_global_device_ids=true | all-gather | bytes 327680 | tf_op jit(solution)/shard_map/all_gather | solution.py:338
  192.1 0.7 slice.9
  192.8 0.2 reshape.33
  193.0 0.3 copy.10
  193.3 0.9 reshape.34
  (2 shorter events, 0.0 us)
Async XLA Ops:
  13.9 11.4 %copy-start.2 = (bf16[1,128,1024]{2,1,0:T(8,128)(2,1)S(1)}, bf16[1,128,1024]{2,1,0:T(8,128)(2,1)}, u32[]{:S(2)}) copy-start(bf16[1,128,1024]{2,1,0:T(8,128)(2,1)} %param.11) | copy-start | bytes 786436
  13.9 11.4 %copy-start.3 = (bf16[128,1024]{1,0:T(8,128)(2,1)S(1)}, bf16[128,1024]{1,0:T(8,128)(2,1)}, u32[]{:S(2)}) copy-start(bf16[128,1024]{1,0:T(8,128)(2,1)} %get-tuple-element.12) | copy-start | bytes 786436
  13.9 35.1 %all-to-all-start = ((bf16[32,208,128]{2,1,0:T(8,128)(2,1)}), bf16[32,208,128]{2,1,0:T(8,128)(2,1)S(1)}, u32[]{:S(2)}, u32[]{:S(2)}) async-start(bf16[32,208,128]{2,1,0:T(8,128)(2,1)} %get-tuple-element.9), calls=%async_computation | async-start | bytes 3407872 | tf_op jit(solution)/shard_map/all_to_all | solution.py:330
  25.3 107.5 %all-gather.4.cloned.1.call-start = ((), (), s32[]{:S(2)}) async-start(), calls=%async_computation.4 | async-start | bytes 2621440 | tf_op jit(solution)/shard_map/all_gather | solution.py:331
  49.0 1.2 copy-start
  125.2 21.0 %all-to-all-start.2 = ((bf16[4,128,1024]{2,1,0:T(8,128)(2,1)}), bf16[4,128,1024]{2,1,0:T(8,128)(2,1)S(1)}, u32[]{:S(2)}, u32[]{:S(2)}) async-start(bf16[4,128,1024]{2,1,0:T(8,128)(2,1)} %get-tuple-element.13), calls=%async_computation.2 | async-start | bytes 2097152 | tf_op jit(solution)/shard_map/all_to_all | solution.py:334
  146.2 1.0 copy-start.1
Sparse Core Ops, SparseCore 0:
  27.8 36.6 all-gather.3

commit v2 on v1

v2 whole, which is shorter than its diff:
```python
import functools
import math

import jax
import jax.numpy as jnp
from jax import lax
from jax.experimental import pallas as pl
from jax.experimental.pallas import tpu as pltpu
from jax.sharding import Mesh, PartitionSpec as P

HEADS = 16
HEAD_DIM = 64
D = HEADS * HEAD_DIM
TOK = 128
HALF = TOK // 2
N_CTX = 32
N_GRP = 4
N_X = 4
N_R = 8
SEQ = TOK * N_CTX
ID_ROWS = 16
IN_ROWS = TOK + HALF + ID_ROWS
OUT_ROWS = TOK + HALF
TQ = 256
TK = 1152
SUB = 128
Q_SRC = TQ // HALF
N_QB = N_CTX // Q_SRC
EPSILON = 1e-06
MASK = -1e30
VMEM = 56 * 1024 * 1024
F32 = jnp.float32
BF16 = jnp.bfloat16


def dot_nn(a, b):
    return jnp.dot(a, b, preferred_element_type=F32)


def dot_nt(a, b):
    return lax.dot_general(a, b, (((1,), (1,)), ((), ())), preferred_element_type=F32)


def dot_tn(a, b):
    return lax.dot_general(a, b, (((0,), (0,)), ((), ())), preferred_element_type=F32)


def lanes(shape):
    return lax.broadcasted_iota(jnp.int32, shape, 1)


def project_kernel(x_ref, cot_ref, gain_ref, ids_ref, wq_ref, wk_ref, wv_ref, wo_ref, send_ref, both_ref):
    @pl.when(pl.program_id(0) == 0)
    def _():
        x = x_ref[...].astype(F32)
        cen = x - jnp.mean(x, axis=1, keepdims=True)
        inv = lax.rsqrt(jnp.mean(cen * cen, axis=1, keepdims=True) + EPSILON)
        both_ref[:, :D] = (cen * inv * gain_ref[...]).astype(BF16)
        both_ref[:, D:] = cot_ref[...]

    n = both_ref[:, :D]
    q = dot_nn(n, wq_ref[...])
    k = dot_nn(n, wk_ref[...])
    v = dot_nn(n, wv_ref[...])
    g = dot_nt(cot_ref[...], wo_ref[...])
    ids = ids_ref[...].astype(F32)
    rolled = jnp.concatenate([ids[:, HALF:], ids[:, :HALF]], axis=1)
    for h in range(4):
        cols = slice(h * HEAD_DIM, (h + 1) * HEAD_DIM)
        kv = jnp.concatenate([k[:, cols], v[:, cols]], axis=1).astype(BF16)
        qg = jnp.concatenate([q[:, cols], g[:, cols]], axis=1).astype(BF16)
        for p in range(2):
            own = ids if p == 0 else rolled
            rows = jnp.concatenate(
                [jnp.broadcast_to(ids, (8, TOK)), jnp.broadcast_to(own, (8, TOK))], axis=0
            )
            send_ref[2 * h + p, :TOK, :] = kv
            send_ref[2 * h + p, TOK:OUT_ROWS, :] = qg[p * HALF:(p + 1) * HALF, :]
            send_ref[2 * h + p, OUT_ROWS:, :] = rows.astype(BF16)


def project(x, cot, gain, ids, w_qkv, w_out):
    whole = lambda shape: pl.BlockSpec(shape, lambda j: (0, 0))
    return pl.pallas_call(
        project_kernel,
        grid=(4,),
        in_specs=[
            whole((TOK, D)),
            whole((TOK, D)),
            whole((1, D)),
            whole((1, TOK)),
            pl.BlockSpec((D, 256), lambda j: (0, j)),
            pl.BlockSpec((D, 256), lambda j: (0, 4 + j)),
            pl.BlockSpec((D, 256), lambda j: (0, 8 + j)),
            pl.BlockSpec((256, D), lambda j: (j, 0)),
        ],
        out_specs=[pl.BlockSpec((8, IN_ROWS, TOK), lambda j: (j, 0, 0)), whole((TOK, 2 * D))],
        out_shape=[
            jax.ShapeDtypeStruct((N_CTX, IN_ROWS, TOK), BF16),
            jax.ShapeDtypeStruct((TOK, 2 * D), BF16),
        ],
        compiler_params=pltpu.CompilerParams(vmem_limit_bytes=VMEM),
        name="project",
    )(x, cot, gain, ids, w_qkv, w_qkv, w_qkv, w_out)


def attend_kernel(recv_ref, send_ref, kx, vx, kvt, idm, sc, acc):
    lane = lanes((TOK, TOK))
    feature = lane.astype(F32) - HEAD_DIM

    def prepare(c, largest):
        kv = recv_ref[c, :TOK, :].astype(F32)
        idrow = recv_ref[c, OUT_ROWS:, :].astype(F32)[:1]
        idm[pl.ds(c, 1), :] = idrow
        idcol = jnp.broadcast_to(idrow, (TOK, TOK)).T
        extra = jnp.where((feature == idcol) | ((feature > HEADS) & (feature < HEADS + 4)), 1.0, 0.0)
        rows = pl.ds(pl.multiple_of(c * TOK, TOK), TOK)
        kx[rows, :] = jnp.where(lane < HEAD_DIM, kv, extra).astype(BF16)
        vx[rows, :] = jnp.where(lane < HEAD_DIM, jnp.where(lane < 3, 1.0, 0.0), kv).astype(BF16)
        flipped = kv.T
        kvt[:TOK, rows] = flipped.astype(BF16)
        kvt[TOK:, rows] = jnp.ones((16, TOK), BF16)
        acc[rows, :] = jnp.zeros((TOK, TOK), F32)
        norm = jnp.sum(flipped[:HEAD_DIM] * flipped[:HEAD_DIM], axis=0, keepdims=True)
        return jnp.maximum(largest, norm)

    largest = lax.fori_loop(0, N_CTX, prepare, jnp.zeros((1, TOK), F32), unroll=4)
    key_norm = jnp.max(largest)
    for c in range(N_CTX, (SEQ + TK) // TOK):
        rows = slice(c * TOK, (c + 1) * TOK)
        kx[rows, :] = jnp.where(feature == HEADS, 1.0, 0.0).astype(BF16)
        vx[rows, :] = jnp.zeros((TOK, TOK), BF16)
        kvt[:, rows] = jnp.zeros((TOK + 16, TOK), BF16)

    lane_q = lanes((TQ, TOK))
    feature_q = lane_q.astype(F32) - HEAD_DIM
    row_t = lax.broadcasted_iota(jnp.int32, (TOK, TQ), 0)

    def three(row, start, rest):
        hi = row.astype(BF16).astype(F32)
        mid = (row - hi).astype(BF16).astype(F32)
        low = row - hi - mid
        for n, part in enumerate((hi, mid, low)):
            rest = jnp.where(row_t == start + n, part, rest)
        return rest.astype(BF16)

    def query_block(i, carry):
        c0 = i * Q_SRC
        qd = recv_ref[pl.ds(c0, Q_SRC), TOK:OUT_ROWS, :].reshape(TQ, TOK).astype(F32)
        idcols = []
        lowest, highest = None, None
        for a in range(Q_SRC):
            both = recv_ref[c0 + a, OUT_ROWS:, :].astype(F32)
            idcols.append(jnp.broadcast_to(both[8:9], (TOK, TOK)).T[:HALF])
            lowest = both if lowest is None else jnp.minimum(lowest, both)
            highest = both if highest is None else jnp.maximum(highest, both)
        idcol = jnp.concatenate(idcols, axis=0)
        every = idm[...]
        below = jnp.sum(jnp.where(every < jnp.min(lowest), 1.0, 0.0)).astype(jnp.int32)
        upto = jnp.sum(jnp.where(every <= jnp.max(highest), 1.0, 0.0)).astype(jnp.int32)
        start = below // TOK
        steps = (upto - start * TOK + (TK - 1)) // TK

        qdt = qd.T
        other = jnp.where((feature_q != idcol) & (feature_q < HEADS + 1), MASK, 0.0)
        qxt_f = jnp.where(lane_q < HEAD_DIM, qd * 0.125, other).T
        norms = jnp.sum(qxt_f[:HEAD_DIM] * qxt_f[:HEAD_DIM], axis=0, keepdims=True)
        small = jnp.max(norms) * key_norm < 1600.0

        def at(kb, t, size):
            return pl.ds(pl.multiple_of(start * TOK + kb * TK + t * size, TOK), size)

        def largest_step(kb, top):
            for t in range(TK // SUB):
                s = dot_nn(kx[at(kb, t, SUB), :], qxt_f.astype(BF16))
                for r in range(0, SUB, 8):
                    top = jnp.maximum(top, s[r:r + 8])
            return top

        top = lax.fori_loop(0, jnp.where(small, 0, steps), largest_step, jnp.full((8, TQ), MASK, F32))
        top = jnp.where(small, 0.0, jnp.max(top, axis=0, keepdims=True))
        qxt = three(-top, HEAD_DIM + HEADS + 1, qxt_f)

        def value_step(kb, ot):
            tiles = [at(kb, t, SUB) for t in range(TK // SUB)]
            e = [jnp.exp(dot_nn(kx[rows, :], qxt)).astype(BF16) for rows in tiles]
            for rows, part in zip(tiles, e):
                ot = ot + dot_nn(kvt[HEAD_DIM:, rows], part)
            for rows, part in zip(tiles, e):
                sc[rows, :] = part
            return ot

        ot = lax.fori_loop(0, steps, value_step, jnp.zeros((HEAD_DIM + 16, TQ), F32))
        inv = 1.0 / ot[HEAD_DIM:HEAD_DIM + 1]
        ot = (ot[:HEAD_DIM] * inv).astype(BF16).astype(F32)
        delta = jnp.sum(ot * qdt[HEAD_DIM:], axis=0, keepdims=True)
        gxt = three(-delta, 0, jnp.where(row_t < HEAD_DIM, 0.0, qdt))

        scaled = (qdt * inv).T
        right = jnp.concatenate(
            [
                jnp.where(lane_q < HEAD_DIM, scaled * 0.125, 0.0).astype(BF16),
                jnp.where(lane_q >= HEAD_DIM, scaled, 0.0).astype(BF16),
            ],
            axis=0,
        )

        def grad_step(kb, dqt):
            tiles = [at(kb, t, SUB) for t in range(TK // SUB)]
            e = [sc[rows, :] for rows in tiles]
            ds = [part * dot_nn(vx[rows, :], gxt).astype(BF16) for rows, part in zip(tiles, e)]
            for rows, part in zip(tiles, ds):
                dqt = dqt + dot_nn(kvt[:HEAD_DIM, rows], part)
            added = [
                acc[rows, :] + dot_nn(jnp.concatenate([a, b], axis=1), right)
                for rows, a, b in zip(tiles, ds, e)
            ]
            for rows, part in zip(tiles, added):
                acc[rows, :] = part
            return dqt

        dqt = lax.fori_loop(0, steps, grad_step, jnp.zeros((HEAD_DIM, TQ), F32))
        both = jnp.concatenate([ot, dqt * (inv * 0.125)], axis=0).T.astype(BF16)
        for a in range(Q_SRC):
            send_ref[(c0 + a) % N_R, (c0 + a) // N_R, TOK:, :] = both[a * HALF:(a + 1) * HALF]
        return carry

    lax.fori_loop(0, N_QB, query_block, 0)

    def finish(c, carry):
        rows = pl.ds(pl.multiple_of(c * TOK, TOK), TOK)
        send_ref[c % N_R, c // N_R, :TOK, :] = acc[rows, :].astype(BF16)
        return carry

    lax.fori_loop(0, N_CTX, finish, 0, unroll=4)


def attend(recv):
    vmem = pl.BlockSpec(memory_space=pltpu.VMEM)
    padded = SEQ + TK
    return pl.pallas_call(
        attend_kernel,
        in_specs=[vmem],
        out_specs=vmem,
        out_shape=jax.ShapeDtypeStruct((N_R, N_X, OUT_ROWS, TOK), BF16),
        scratch_shapes=[
            pltpu.VMEM((padded, TOK), BF16),
            pltpu.VMEM((padded, TOK), BF16),
            pltpu.VMEM((TOK + 16, padded), BF16),
            pltpu.VMEM((N_CTX, TOK), F32),
            pltpu.VMEM((padded, TQ), BF16),
            pltpu.VMEM((padded, TOK), F32),
        ],
        compiler_params=pltpu.CompilerParams(vmem_limit_bytes=VMEM),
        cost_estimate=pl.CostEstimate(flops=25 * 10**9, bytes_accessed=4 * 10**6, transcendentals=0),
        name="attend",
    )(recv)


def unproject_kernel(me_ref, a_ref, b_ref, c_ref, d_ref, x_ref, gain_ref, wqkv_ref, wo_ref, out_ref, gx_ref):
    result = jnp.zeros((TOK, D), F32)
    g = jnp.zeros((TOK, D), F32)
    for d, ref in enumerate((a_ref, b_ref, c_ref, d_ref)):
        start = (me_ref[0] ^ d) * 256
        result = result + dot_nn(ref[:, 768:], wo_ref[pl.ds(pl.multiple_of(start, 256), 256), :])
        for n in range(3):
            cols = pl.ds(pl.multiple_of(start + n * D, 256), 256)
            g = g + dot_nt(ref[:, n * 256:(n + 1) * 256], wqkv_ref[:, cols])
    out_ref[...] = result.astype(BF16)
    x = x_ref[...].astype(F32)
    cen = x - jnp.mean(x, axis=1, keepdims=True)
    inv = lax.rsqrt(jnp.mean(cen * cen, axis=1, keepdims=True) + EPSILON)
    x_hat = cen * inv
    g = g * gain_ref[...]
    gx = inv * (
        g - jnp.mean(g, axis=1, keepdims=True) - x_hat * jnp.mean(g * x_hat, axis=1, keepdims=True)
    )
    gx_ref[...] = gx.astype(BF16)


def unproject(me, pieces, x, gain, w_qkv, w_out):
    vmem = pl.BlockSpec(memory_space=pltpu.VMEM)
    return pl.pallas_call(
        unproject_kernel,
        in_specs=[pl.BlockSpec(memory_space=pltpu.SMEM)] + [vmem] * 8,
        out_specs=[vmem] * 2,
        out_shape=[jax.ShapeDtypeStruct((TOK, D), BF16)] * 2,
        compiler_params=pltpu.CompilerParams(vmem_limit_bytes=VMEM),
        cost_estimate=pl.CostEstimate(flops=7 * 10**9, bytes_accessed=10**7, transcendentals=0),
        name="unproject",
    )(me, *pieces, x, gain, w_qkv, w_out)


def weights_kernel(me_ref, recv_ref, b0, b1, b2, b3, cols_ref, send_ref):
    for i in range(N_X):
        at = me_ref[0] ^ i
        parts = [[], [], [], []]
        for h in range(4):
            lo, hi = recv_ref[2 * h, at].astype(F32), recv_ref[2 * h + 1, at].astype(F32)
            kv = lo[:TOK] + hi[:TOK]
            aq = jnp.concatenate([lo[TOK:], hi[TOK:]], axis=0)
            parts[0].append(aq[:, HEAD_DIM:])
            parts[1].append(kv[:, :HEAD_DIM])
            parts[2].append(kv[:, HEAD_DIM:])
            parts[3].append(aq[:, :HEAD_DIM])
        for n, part in enumerate(parts):
            cols_ref[i, :, n * 256:(n + 1) * 256] = jnp.concatenate(part, axis=1).astype(BF16)
    cols = cols_ref[...].reshape(N_X * TOK, D)
    both = jnp.concatenate([b0[...], b1[...], b2[...], b3[...]], axis=0)
    for m in range(4):
        part = dot_tn(both[:, m * 256:(m + 1) * 256], cols[:, :768])
        for r in range(N_R):
            send_ref[8 * m + r, :, :768] = part[32 * r:32 * r + 32].astype(BF16)
    for m in range(N_GRP):
        part = dot_tn(cols[:, 768:], both[:, D + m * 256:D + (m + 1) * 256])
        for r in range(N_R):
            send_ref[8 * m + r, :, 768:] = part[32 * r:32 * r + 32].astype(BF16)


def weights(me, recv, both):
    vmem = pl.BlockSpec(memory_space=pltpu.VMEM)
    return pl.pallas_call(
        weights_kernel,
        in_specs=[pl.BlockSpec(memory_space=pltpu.SMEM)] + [vmem] * 5,
        out_specs=[vmem] * 2,
        out_shape=[
            jax.ShapeDtypeStruct((N_X, TOK, D), BF16),
            jax.ShapeDtypeStruct((N_CTX, 32, D), BF16),
        ],
        compiler_params=pltpu.CompilerParams(vmem_limit_bytes=VMEM),
        name="weights",
    )(me, recv, *both)


def assemble_kernel(me_ref, a_ref, b_ref, c_ref, d_ref, qkv_ref, out_ref):
    for d, ref in enumerate((a_ref, b_ref, c_ref, d_ref)):
        start = (me_ref[0] ^ d) * 256
        part = ref[...].astype(F32)
        for n in range(3):
            cols = pl.ds(pl.multiple_of(start + n * D, 256), 256)
            qkv_ref[:, cols] = part[:, n * 256:(n + 1) * 256]
        out_ref[:, pl.ds(pl.multiple_of(start, 256), 256)] = part[:, 768:]


def assemble(me, parts):
    vmem = pl.BlockSpec(memory_space=pltpu.VMEM)
    return pl.pallas_call(
        assemble_kernel,
        in_specs=[pl.BlockSpec(memory_space=pltpu.SMEM)] + [vmem] * 4,
        out_specs=[vmem] * 2,
        out_shape=[jax.ShapeDtypeStruct((32, 3 * D), F32), jax.ShapeDtypeStruct((32, D), F32)],
        name="assemble",
    )(me, *parts)


def swap(piece, axis, d):
    return piece if d == 0 else lax.ppermute(piece, axis, [(i, i ^ d) for i in range(4)])


def shards(patches, gain, w_qkv, w_out, image_ids, grad_out):
    x, cot = patches[0], grad_out[0]
    gain_row = gain[None]
    me = lax.axis_index("x").astype(jnp.int32)[None]
    send, both = project(x, cot, gain_row, image_ids, w_qkv, w_out)
    recv = lax.all_to_all(send, ("x", "r"), 0, 0, tiled=True)
    recv, both = lax.optimization_barrier((recv, both))
    both = [swap(both, "x", d) for d in range(N_X)]
    done, both = lax.optimization_barrier((attend(recv), both))
    back = lax.all_to_all(done, "r", 0, 0, tiled=True)
    cols, terms = weights(me, back, both)
    cols = [swap(cols[d], "x", d) for d in range(N_X)]
    parts = lax.all_to_all(terms, ("grp", "r"), 0, 0, tiled=True)
    out, grad_x = unproject(me, cols, x, gain_row, w_qkv, w_out)
    parts, out, grad_x = lax.optimization_barrier((parts, out, grad_x))
    factor = 1.0 / math.sqrt(N_GRP * SEQ)
    share = (jnp.sum(parts.astype(F32), axis=0) * factor).astype(BF16)
    flip = [(s * N_X + j, j * N_X + s) for s in range(N_GRP) for j in range(N_X)]
    share_qkv = lax.ppermute(share[:, :768], ("grp", "x"), flip)
    share = jnp.concatenate([share_qkv, share[:, 768:]], axis=1)
    shares = [swap(share, "grp", d) for d in range(N_GRP)]
    grad_qkv, grad_w_out = assemble(lax.axis_index("grp").astype(jnp.int32)[None], shares)
    return out[None], grad_x[None], grad_qkv, grad_w_out


def solution(mesh):
    fine = Mesh(mesh.devices.reshape(N_GRP, N_X, N_R), ("grp", "x", "r"))
    ctx = ("x", "r")
    in_specs = (P("grp", ctx, None), P(), P(), P(), P("grp", ctx), P("grp", ctx, None))
    out_specs = (P("grp", ctx, None), P("grp", ctx, None), P(ctx, None), P(ctx, None))
    return jax.shard_map(shards, mesh=fine, in_specs=in_specs, out_specs=out_specs, check_vma=False)
```

time: 202 us -> 160 us (0.79)
  blocking collectives: 66.3 us -> 35.3 us
  between operations: 14.1 us -> 0.75 us
  waiting for transfers between devices: 36.1 us -> 44.1 us
  Pallas kernels: 60 us -> 52.7 us
  starting transfers between devices: 19 us -> 22.7 us
    all_to_all x2 -> x1, blocking collectives: 57.5 us -> 35.3 us  [shards(): recv = lax.all_to_all(send, ('x', 'r'), 0, 0, tiled=True)]
    ppermute x0 -> x10, waiting for transfers between devices: none -> 16.7 us  [the longest x9 14.4 us: swap(): lax.ppermute(piece, axis, [(i, i ^ d) for i in range(4)])]
    ppermute x0 -> x10, starting transfers between devices: none -> 14.4 us  [the longest x9 11.4 us: swap(): lax.ppermute(piece, axis, [(i, i ^ d) for i in range(4)])]
    all_to_all x2, starting transfers between devices: 19 us -> 8.28 us  [the longest x1 4.69 us: shards(): parts = lax.all_to_all(terms, ('grp', 'r'), 0, 0, tiled=True)]
    all_gather x1 -> x0, blocking collectives: 8.78 us -> none  [shards(): full = lax.all_gather(share, 'grp', axis=0).astype(F32)]
    all_to_all x2, waiting for transfers between devices: 36.1 us -> 27.4 us  [the longest x1 22.9 us: shards(): back = lax.all_to_all(done, 'r', 0, 0, tiled=True)]
    pallas_call x1, Pallas kernels: 39.9 us -> 32.1 us  [attend(): pl.pallas_call(attend_kernel, in_specs=[vmem], out_specs=vmem, out_shape=...]
    pallas_call x2 -> x3, Pallas kernels: 13.4 us -> 13.8 us  [the longest x1 7.2 us: unproject(): pl.pallas_call(unproject_kernel, in_specs=[pl.BlockSpec(memory_space=pltp...]
  transfers between devices with their start and end apart: 3 -> 12, of which waited for: 2 -> 7; matrix products, arithmetic and copies ran while one was open for 0% -> 0% of each run, Pallas kernels for 24% -> 25%
where the time goes in v2:
time: 160 us; the launch traced here: 159 us
  Pallas kernels  52.7 us (33%)
  waiting for transfers between devices  44.1 us (28%)
  blocking collectives  35.3 us (22%)
  starting transfers between devices  22.7 us (14%)
  local copies, waits for them, and re-layouts  3.27 us (2%)
    all_to_all x1, blocking collectives, shards(): recv = lax.all_to_all(send, ('x', 'r'), 0, 0, tiled=True)  35.3 us
    pallas_call x1, Pallas kernels, attend(): pl.pallas_call(attend_kernel, in_specs=[vmem], out_specs=vmem, out_shape=...  32.1 us
    all_to_all x1, waiting for transfers between devices, shards(): back = lax.all_to_all(done, 'r', 0, 0, tiled=True)  22.9 us
    ppermute x9, waiting for transfers between devices, swap(): lax.ppermute(piece, axis, [(i, i ^ d) for i in range(4)])  14.4 us
    ppermute x9, starting transfers between devices, swap(): lax.ppermute(piece, axis, [(i, i ^ d) for i in range(4)])  11.4 us
    pallas_call x1, Pallas kernels, unproject(): pl.pallas_call(unproject_kernel, in_specs=[pl.BlockSpec(memory_space=pltp...  7.2 us
    pallas_call x1, Pallas kernels, project(): pl.pallas_call(project_kernel, grid=(4,), in_specs=[whole((TOK, D)), whol...  6.8 us
    pallas_call x1, Pallas kernels, weights(): pl.pallas_call(weights_kernel, in_specs=[pl.BlockSpec(memory_space=pltpu....  4.89 us
  transfers between devices with their start and end apart: 12, of which 7 were waited for; matrix products, arithmetic and copies ran while one was open for 0% of the time, Pallas kernels for 25%

profile of v2, /device:TPU:1, one launch (start us, length us, event | category | flops | bytes accessed | tf_op | source)
XLA Modules:
  0.0 159.2 jit_solution(13794108905050531940)
XLA Ops:
  0.6 6.8 %project.1 = (bf16[32,208,128]{2,1,0:T(8,128)(2,1)}, bf16[128,2048]{1,0:T(8,128)(2,1)}) custom-call(bf16[128,1024]{1,0:T(8,128)(2,1)} %bitcast.16, bf16[128,1024]{1,0:T(8,128)(2,1)} %bitcast.15, f32[1,1024]{1,0:T(1,128)} %bitcast.18, s32[1,128]{1,0:T(1,128)} %ids_ref.1, bf16[1024,3072]{1,0:T(8,128)(2,1)} %wqkv_ref.1, bf16[1024,3072]{1,0:T(8,128)(2,1)} %wqkv_ref.1, ...), custom_call_target="tpu_custom_call" | custom-call | tf_op jit(solution)/shard_map/project/pallas_call | solution.py:84
  7.4 35.3 %all_to_all.15.recv_ref = bf16[32,208,128]{2,1,0:T(8,128)(2,1)} all-to-all(bf16[32,208,128]{2,1,0:T(8,128)(2,1)} %get-tuple-element.22), channel_id=1, replica_groups=mesh['grp'=4,'x'=4,'r'=8] {'x','r'}, dimensions={0} | all-to-all | bytes 3407872 | tf_op jit(solution)/shard_map/all_to_all | solution.py:365
  42.8 0.7 collective-permute-start.2
  43.5 1.1 collective-permute-start.1
  44.5 1.5 collective-permute-start
  46.0 32.1 %attend.1 = bf16[8,4,192,128]{3,2,1,0:T(8,128)(2,1)} custom-call(bf16[32,208,128]{2,1,0:T(8,128)(2,1)} %all_to_all.15.recv_ref), custom_call_target="tpu_custom_call" | custom-call | flops 24999999488 | bytes 4000000 | tf_op jit(solution)/shard_map/attend/pallas_call | solution.py:241
  78.1 3.6 %all-to-all-start.1 = ((bf16[8,4,192,128]{3,2,1,0:T(8,128)(2,1)}), bf16[8,4,192,128]{3,2,1,0:T(8,128)(2,1)S(1)}, u32[]{:S(2)}, u32[]{:S(2)}) async-start(bf16[8,4,192,128]{3,2,1,0:T(8,128)(2,1)} %attend.1), calls=%async_computation.1 | async-start | bytes 3145728 | tf_op jit(solution)/shard_map/all_to_all | solution.py:369
  81.7 22.9 %all-to-all-done.1.recv_ref = bf16[8,4,192,128]{3,2,1,0:T(8,128)(2,1)S(1)} async-done(((bf16[8,4,192,128]{3,2,1,0:T(8,128)(2,1)}), bf16[8,4,192,128]{3,2,1,0:T(8,128)(2,1)S(1)}, u32[]{:S(2)}, u32[]{:S(2)}) %all-to-all-start.1) | async-done | bytes 1572896 | tf_op jit(solution)/shard_map/all_to_all | solution.py:369
  104.6 1.1 copy-done
  105.7 4.9 %weights.1 = (bf16[4,128,1024]{2,1,0:T(8,128)(2,1)}, bf16[32,32,1024]{2,1,0:T(8,128)(2,1)}) custom-call(s32[1]{0:T(128)} %bitcast.me_ref, bf16[8,4,192,128]{3,2,1,0:T(8,128)(2,1)} %copy-done, bf16[128,2048]{1,0:T(8,128)(2,1)} %get-tuple-element.27.b0, bf16[128,2048]{1,0:T(8,128)(2,1)} %collective-permute-done.b1, bf16[128,2048]{1,0:T(8,128)(2,1)} %copy-done.4, ...), custom_call_target="tpu_custom_call" | custom-call | tf_op jit(solution)/shard_map/weights/pallas_call | solution.py:322
  110.6 4.7 %all-to-all-start.2 = ((bf16[32,32,1024]{2,1,0:T(8,128)(2,1)}), bf16[32,32,1024]{2,1,0:T(8,128)(2,1)S(1)}, u32[]{:S(2)}, u32[]{:S(2)}) async-start(bf16[32,32,1024]{2,1,0:T(8,128)(2,1)} %get-tuple-element.31), calls=%async_computation.2 | async-start | bytes 4194304 | tf_op jit(solution)/shard_map/all_to_all | solution.py:372
  115.3 0.8 slice_bitcast_fusion
  116.1 1.4 collective-permute-start.5
  117.5 0.6 collective-permute-start.4
  118.1 1.3 collective-permute-start.3
  119.3 11.2 %collective-permute-done.5.d_ref = bf16[128,1024]{1,0:T(8,128)(2,1)S(1)} collective-permute-done((bf16[128,1024]{1,0:T(8,128)(2,1)S(1)}, bf16[128,1024]{1,0:T(8,128)(2,1)S(1)}, u32[]{:S(2)}, u32[]{:S(2)}) %collective-permute-start.5) | collective-permute-done | bytes 262176 | tf_op jit(solution)/shard_map/ppermute | solution.py:357
  130.5 0.3 collective-permute-done.3.b_ref
  130.8 0.4 copy-done.9
  131.2 0.1 copy-done.10
  131.3 0.2 copy-done.11
  131.5 7.2 %unproject.1 = (bf16[128,1024]{1,0:T(8,128)(2,1)}, bf16[128,1024]{1,0:T(8,128)(2,1)}) custom-call(s32[1]{0:T(128)} %bitcast.me_ref, bf16[128,1024]{1,0:T(8,128)(2,1)} %get-tuple-element.43.a_ref, bf16[128,1024]{1,0:T(8,128)(2,1)} %copy-done.11, bf16[128,1024]{1,0:T(8,128)(2,1)} %copy-done.10, bf16[128,1024]{1,0:T(8,128)(2,1)} %copy-done.9, ...), custom_call_target="tpu_custom_call" | custom-call | flops 7000000000 | bytes 10000000 | tf_op jit(solution)/shard_map/unproject/pallas_call | solution.py:283
  138.8 4.5 %all-to-all-done.2 = bf16[32,32,1024]{2,1,0:T(8,128)(2,1)S(1)} async-done(((bf16[32,32,1024]{2,1,0:T(8,128)(2,1)}), bf16[32,32,1024]{2,1,0:T(8,128)(2,1)S(1)}, u32[]{:S(2)}, u32[]{:S(2)}) %all-to-all-start.2) | async-done | bytes 2097184 | tf_op jit(solution)/shard_map/all_to_all | solution.py:372
  143.3 0.4 convert_reduce_fusion
  143.6 3.1 %collective-permute-start.6 = (bf16[32,768]{1,0:T(8,128)(2,1)S(1)}, bf16[32,768]{1,0:T(8,128)(2,1)S(1)}, u32[]{:S(2)}, u32[]{:S(2)}) collective-permute-start(bf16[32,768]{1,0:T(8,128)(2,1)S(1)} %slice.24), channel_id=1, source_target_pairs={{0,0},{8,32},{16,64},{24,96},{32,8},{40,40},{48,72},{56,104},{64,1... | collective-permute-start | bytes 147464 | tf_op jit(solution)/shard_map/ppermute | solution.py:378
  146.7 2.3 %collective-permute-done.6 = bf16[32,768]{1,0:T(8,128)(2,1)S(1)} collective-permute-done((bf16[32,768]{1,0:T(8,128)(2,1)S(1)}, bf16[32,768]{1,0:T(8,128)(2,1)S(1)}, u32[]{:S(2)}, u32[]{:S(2)}) %collective-permute-start.6) | collective-permute-done | bytes 49184 | tf_op jit(solution)/shard_map/ppermute | solution.py:378
  149.1 4.4 %collective-permute-start.9 = (bf16[32,1024]{1,0:T(8,128)(2,1)S(1)}, bf16[32,1024]{1,0:T(8,128)(2,1)S(1)}, u32[]{:S(2)}, u32[]{:S(2)}) collective-permute-start(bf16[32,1024]{1,0:T(8,128)(2,1)S(1)} %pad_maximum_fusion.a_ref), channel_id=1, source_target_pairs={{0,96},{32,64},{64,32},{96,0},{1,97},{33,65},{65,33},{97,1},{2,98}... | collective-permute-start | bytes 196616 | tf_op jit(solution)/shard_map/ppermute | solution.py:357
  153.5 0.5 collective-permute-start.7
  153.9 1.5 collective-permute-done.9.d_ref
  155.4 1.4 collective-permute-done.8.c_ref
  156.8 0.6 copy-done.7
  157.4 0.0 copy-done.8
  157.5 1.8 %assemble.1 = (f32[32,3072]{1,0:T(8,128)}, f32[32,1024]{1,0:T(8,128)}) custom-call(s32[1]{0:T(128)} %bitcast.10.me_ref, bf16[32,1024]{1,0:T(8,128)(2,1)} %copy-done.5, bf16[32,1024]{1,0:T(8,128)(2,1)} %copy-done.8, bf16[32,1024]{1,0:T(8,128)(2,1)} %copy-done.7, bf16[32,1024]{1,0:T(8,128)(2,1)} %copy-done.6), custom_call_target="tpu_custom_call" | custom-call | tf_op jit(solution)/shard_map/assemble/pallas_call | solution.py:347
  (28 shorter events, 0.1 us)
Async XLA Ops:
  7.4 35.3 %copy-start.2 = (bf16[128,2048]{1,0:T(8,128)(2,1)S(1)}, bf16[128,2048]{1,0:T(8,128)(2,1)}, u32[]{:S(2)}) copy-start(bf16[128,2048]{1,0:T(8,128)(2,1)} %get-tuple-element.27.b0) | copy-start | bytes 1572868
  42.8 35.3 %collective-permute-start.2 = (bf16[128,2048]{1,0:T(8,128)(2,1)S(1)}, bf16[128,2048]{1,0:T(8,128)(2,1)S(1)}, u32[]{:S(2)}, u32[]{:S(2)}) collective-permute-start(bf16[128,2048]{1,0:T(8,128)(2,1)S(1)} %copy-done.2), channel_id=1, source_target_pairs={{0,24},{8,16},{16,8},{24,0},{1,25},{9,17},{17,9},{25,1},{2,26},{10... | collective-permute-start | bytes 1572872 | tf_op jit(solution)/shard_map/ppermute | solution.py:357
  43.5 34.6 %collective-permute-start.1 = (bf16[128,2048]{1,0:T(8,128)(2,1)S(1)}, bf16[128,2048]{1,0:T(8,128)(2,1)S(1)}, u32[]{:S(2)}, u32[]{:S(2)}) collective-permute-start(bf16[128,2048]{1,0:T(8,128)(2,1)S(1)} %copy-done.2), channel_id=1, source_target_pairs={{0,16},{8,24},{16,0},{24,8},{1,17},{9,25},{17,1},{25,9},{2,18},{10... | collective-permute-start | bytes 1572872 | tf_op jit(solution)/shard_map/ppermute | solution.py:357
  44.5 33.6 %collective-permute-start = (bf16[128,2048]{1,0:T(8,128)(2,1)S(1)}, bf16[128,2048]{1,0:T(8,128)(2,1)}, u32[]{:S(2)}, u32[]{:S(2)}) collective-permute-start(bf16[128,2048]{1,0:T(8,128)(2,1)S(1)} %copy-done.2), channel_id=1, source_target_pairs={{0,8},{8,0},{16,24},{24,16},{1,9},{9,1},{17,25},{25,17},{2,10},{10... | collective-permute-start | bytes 1572872 | tf_op jit(solution)/shard_map/ppermute | solution.py:357
  78.1 26.5 %copy-start.3 = (bf16[128,2048]{1,0:T(8,128)(2,1)}, bf16[128,2048]{1,0:T(8,128)(2,1)S(1)}, u32[]{:S(2)}) copy-start(bf16[128,2048]{1,0:T(8,128)(2,1)S(1)} %collective-permute-done.2.b3) | copy-start | bytes 1572868
  78.1 26.5 %copy-start.4 = (bf16[128,2048]{1,0:T(8,128)(2,1)}, bf16[128,2048]{1,0:T(8,128)(2,1)S(1)}, u32[]{:S(2)}) copy-start(bf16[128,2048]{1,0:T(8,128)(2,1)S(1)} %collective-permute-done.1.b2) | copy-start | bytes 1572868
  78.1 26.5 %all-to-all-start.1 = ((bf16[8,4,192,128]{3,2,1,0:T(8,128)(2,1)}), bf16[8,4,192,128]{3,2,1,0:T(8,128)(2,1)S(1)}, u32[]{:S(2)}, u32[]{:S(2)}) async-start(bf16[8,4,192,128]{3,2,1,0:T(8,128)(2,1)} %attend.1), calls=%async_computation.1 | async-start | bytes 3145728 | tf_op jit(solution)/shard_map/all_to_all | solution.py:369
  104.6 1.1 copy-start
  110.6 4.7 %copy-start.1 = (bf16[4,128,1024]{2,1,0:T(8,128)(2,1)S(1)}, bf16[4,128,1024]{2,1,0:T(8,128)(2,1)}, u32[]{:S(2)}) copy-start(bf16[4,128,1024]{2,1,0:T(8,128)(2,1)} %get-tuple-element.32) | copy-start | bytes 3145732
  110.6 32.7 %all-to-all-start.2 = ((bf16[32,32,1024]{2,1,0:T(8,128)(2,1)}), bf16[32,32,1024]{2,1,0:T(8,128)(2,1)S(1)}, u32[]{:S(2)}, u32[]{:S(2)}) async-start(bf16[32,32,1024]{2,1,0:T(8,128)(2,1)} %get-tuple-element.31), calls=%async_computation.2 | async-start | bytes 4194304 | tf_op jit(solution)/shard_map/all_to_all | solution.py:372
  116.1 14.4 %collective-permute-start.5 = (bf16[128,1024]{1,0:T(8,128)(2,1)S(1)}, bf16[128,1024]{1,0:T(8,128)(2,1)S(1)}, u32[]{:S(2)}, u32[]{:S(2)}) collective-permute-start(bf16[128,1024]{1,0:T(8,128)(2,1)S(1)} %get-tuple-element.40), channel_id=1, source_target_pairs={{0,24},{8,16},{16,8},{24,0},{1,25},{9,17},{17,9},{25,1},{2,26},{10... | collective-permute-start | bytes 786440 | tf_op jit(solution)/shard_map/ppermute | solution.py:357
  117.5 13.0 %collective-permute-start.4 = (bf16[128,1024]{1,0:T(8,128)(2,1)S(1)}, bf16[128,1024]{1,0:T(8,128)(2,1)S(1)}, u32[]{:S(2)}, u32[]{:S(2)}) collective-permute-start(bf16[128,1024]{1,0:T(8,128)(2,1)S(1)} %get-tuple-element.41), channel_id=1, source_target_pairs={{0,16},{8,24},{16,0},{24,8},{1,17},{9,25},{17,1},{25,9},{2,18},{10... | collective-permute-start | bytes 786440 | tf_op jit(solution)/shard_map/ppermute | solution.py:357
  118.1 12.8 %collective-permute-start.3 = (bf16[128,1024]{1,0:T(8,128)(2,1)S(1)}, bf16[128,1024]{1,0:T(8,128)(2,1)S(1)}, u32[]{:S(2)}, u32[]{:S(2)}) collective-permute-start(bf16[128,1024]{1,0:T(8,128)(2,1)S(1)} %get-tuple-element.42), channel_id=1, source_target_pairs={{0,8},{8,0},{16,24},{24,16},{1,9},{9,1},{17,25},{25,17},{2,10},{10... | collective-permute-start | bytes 786440 | tf_op jit(solution)/shard_map/ppermute | solution.py:357
  130.5 0.7 copy-start.9
  130.5 0.8 copy-start.10
  130.8 0.7 copy-start.11
  143.6 5.4 %collective-permute-start.6 = (bf16[32,768]{1,0:T(8,128)(2,1)S(1)}, bf16[32,768]{1,0:T(8,128)(2,1)S(1)}, u32[]{:S(2)}, u32[]{:S(2)}) collective-permute-start(bf16[32,768]{1,0:T(8,128)(2,1)S(1)} %slice.24), channel_id=1, source_target_pairs={{0,0},{8,32},{16,64},{24,96},{32,8},{40,40},{48,72},{56,104},{64,1... | collective-permute-start | bytes 147464 | tf_op jit(solution)/shard_map/ppermute | solution.py:378
  149.1 7.8 %copy-start.5 = (bf16[32,1024]{1,0:T(8,128)(2,1)}, bf16[32,1024]{1,0:T(8,128)(2,1)S(1)}, u32[]{:S(2)}) copy-start(bf16[32,1024]{1,0:T(8,128)(2,1)S(1)} %pad_maximum_fusion.a_ref) | copy-start | bytes 196612
  149.1 6.3 %collective-permute-start.9 = (bf16[32,1024]{1,0:T(8,128)(2,1)S(1)}, bf16[32,1024]{1,0:T(8,128)(2,1)S(1)}, u32[]{:S(2)}, u32[]{:S(2)}) collective-permute-start(bf16[32,1024]{1,0:T(8,128)(2,1)S(1)} %pad_maximum_fusion.a_ref), channel_id=1, source_target_pairs={{0,96},{32,64},{64,32},{96,0},{1,97},{33,65},{65,33},{97,1},{2,98}... | collective-permute-start | bytes 196616 | tf_op jit(solution)/shard_map/ppermute | solution.py:357
  153.4 3.4 %collective-permute-start.8 = (bf16[32,1024]{1,0:T(8,128)(2,1)S(1)}, bf16[32,1024]{1,0:T(8,128)(2,1)S(1)}, u32[]{:S(2)}, u32[]{:S(2)}) collective-permute-start(bf16[32,1024]{1,0:T(8,128)(2,1)S(1)} %pad_maximum_fusion.a_ref), channel_id=1, source_target_pairs={{0,64},{32,96},{64,0},{96,32},{1,65},{33,97},{65,1},{97,33},{2,66}... | collective-permute-start | bytes 196616 | tf_op jit(solution)/shard_map/ppermute | solution.py:357
  153.5 3.4 %collective-permute-start.7 = (bf16[32,1024]{1,0:T(8,128)(2,1)S(1)}, bf16[32,1024]{1,0:T(8,128)(2,1)S(1)}, u32[]{:S(2)}, u32[]{:S(2)}) collective-permute-start(bf16[32,1024]{1,0:T(8,128)(2,1)S(1)} %pad_maximum_fusion.a_ref), channel_id=1, source_target_pairs={{0,32},{32,0},{64,96},{96,64},{1,33},{33,1},{65,97},{97,65},{2,34}... | collective-permute-start | bytes 196616 | tf_op jit(solution)/shard_map/ppermute | solution.py:357
  155.4 1.4 copy-start.6
  156.8 0.6 copy-start.7
  156.8 0.6 copy-start.8

commit v3 on v2

v3 whole, which is shorter than its diff:
```python
import functools
import math

import jax
import jax.numpy as jnp
from jax import lax
from jax.experimental import pallas as pl
from jax.experimental.pallas import tpu as pltpu
from jax.sharding import Mesh, PartitionSpec as P

HEADS = 16
HEAD_DIM = 64
D = HEADS * HEAD_DIM
TOK = 128
HALF = TOK // 2
N_CTX = 32
N_GRP = 4
N_X = 4
N_R = 8
SEQ = TOK * N_CTX
ID_ROWS = 16
IN_ROWS = TOK + HALF + ID_ROWS
OUT_ROWS = TOK + HALF
TQ = 256
LARGE, MIDDLE, SMALL = 2176, 896, 384
SUB = 128
Q_SRC = TQ // HALF
N_QB = N_CTX // Q_SRC
EPSILON = 1e-06
MASK = -1e30
MIB = 1024 * 1024
F32 = jnp.float32
BF16 = jnp.bfloat16


def dot_nn(a, b):
    return jnp.dot(a, b, preferred_element_type=F32)


def dot_nt(a, b):
    return lax.dot_general(a, b, (((1,), (1,)), ((), ())), preferred_element_type=F32)


def dot_tn(a, b):
    return lax.dot_general(a, b, (((0,), (0,)), ((), ())), preferred_element_type=F32)


def lanes(shape):
    return lax.broadcasted_iota(jnp.int32, shape, 1)


def fetch(wqkv_hbm, wo_hbm, wqkv, wo, sems, n, start):
    start = start if isinstance(start, int) else pl.multiple_of(start, 256)
    copies = [pltpu.make_async_copy(wo_hbm.at[pl.ds(start, 256), :], wo.at[n], sems.at[n, 3])]
    for m in range(3):
        cols = pl.ds(start + m * D, 256)
        copies.append(pltpu.make_async_copy(wqkv_hbm.at[:, cols], wqkv.at[n, m], sems.at[n, m]))
    return copies


FETCHED = [
    pltpu.VMEM((4, 3, D, 256), BF16),
    pltpu.VMEM((4, 256, D), BF16),
    pltpu.SemaphoreType.DMA((4, 4)),
]


def project_kernel(x_hbm, cot_hbm, gain_hbm, ids_hbm, wqkv_hbm, wo_hbm, send_ref, both_ref, x_ref, gain_ref, ids_ref, wqkv, wo, sems, in_sems):
    cot_ref = both_ref.at[:, D:]
    arrays = ((x_hbm, x_ref), (gain_hbm, gain_ref), (ids_hbm, ids_ref), (cot_hbm, cot_ref))
    inputs = [pltpu.make_async_copy(*pair, in_sems.at[n]) for n, pair in enumerate(arrays)]
    copies = [fetch(wqkv_hbm, wo_hbm, wqkv, wo, sems, n, n * 256) for n in range(4)]
    for copy in inputs + copies[0]:
        copy.start()
    for copy in inputs[:3]:
        copy.wait()
    for group in copies[1:]:
        for copy in group:
            copy.start()
    x = x_ref[...].astype(F32)
    cen = x - jnp.mean(x, axis=1, keepdims=True)
    inv = lax.rsqrt(jnp.mean(cen * cen, axis=1, keepdims=True) + EPSILON)
    n = (cen * inv * gain_ref[...]).astype(BF16)
    both_ref[:, :D] = n
    ids = ids_ref[...].astype(F32)
    rolled = jnp.concatenate([ids[:, HALF:], ids[:, :HALF]], axis=1)
    inputs[3].wait()
    for j in range(4):
        for copy in copies[j]:
            copy.wait()
        g = dot_nt(cot_ref[...], wo[j])
        q, k, v = (dot_nn(n, wqkv[j, m]) for m in range(3))
        for h in range(4):
            cols = slice(h * HEAD_DIM, (h + 1) * HEAD_DIM)
            kv = jnp.concatenate([k[:, cols], v[:, cols]], axis=1).astype(BF16)
            qg = jnp.concatenate([q[:, cols], g[:, cols]], axis=1).astype(BF16)
            for p in range(2):
                own = ids if p == 0 else rolled
                rows = jnp.concatenate(
                    [jnp.broadcast_to(ids, (8, TOK)), jnp.broadcast_to(own, (8, TOK))], axis=0
                )
                to = 8 * j + 2 * h + p
                send_ref[to, :TOK, :] = kv
                send_ref[to, TOK:OUT_ROWS, :] = qg[p * HALF:(p + 1) * HALF, :]
                send_ref[to, OUT_ROWS:, :] = rows.astype(BF16)


def project(x, cot, gain, ids, w_qkv, w_out):
    vmem = pl.BlockSpec(memory_space=pltpu.VMEM)
    hbm = pl.BlockSpec(memory_space=pltpu.HBM)
    return pl.pallas_call(
        project_kernel,
        in_specs=[hbm] * 6,
        out_specs=[vmem] * 2,
        out_shape=[
            jax.ShapeDtypeStruct((N_CTX, IN_ROWS, TOK), BF16),
            jax.ShapeDtypeStruct((TOK, 2 * D), BF16),
        ],
        scratch_shapes=[
            pltpu.VMEM((TOK, D), BF16),
            pltpu.VMEM((1, D), F32),
            pltpu.VMEM((1, TOK), jnp.int32),
            *FETCHED,
            pltpu.SemaphoreType.DMA((4,)),
        ],
        compiler_params=pltpu.CompilerParams(vmem_limit_bytes=56 * MIB),
        name="project",
    )(x, cot, gain, ids, w_qkv, w_out)


def attend_kernel(recv_ref, send_ref, kx, vx, kvt, idm, sc, acc):
    lane = lanes((TOK, TOK))
    feature = lane.astype(F32) - HEAD_DIM

    def prepare(c, largest):
        kv = recv_ref[c, :TOK, :].astype(F32)
        idrow = recv_ref[c, OUT_ROWS:, :].astype(F32)[:1]
        idm[pl.ds(c, 1), :] = idrow
        idcol = jnp.broadcast_to(idrow, (TOK, TOK)).T
        extra = jnp.where((feature == idcol) | ((feature > HEADS) & (feature < HEADS + 4)), 1.0, 0.0)
        rows = pl.ds(pl.multiple_of(c * TOK, TOK), TOK)
        kx[rows, :] = jnp.where(lane < HEAD_DIM, kv, extra).astype(BF16)
        vx[rows, :] = jnp.where(lane < HEAD_DIM, jnp.where(lane < 3, 1.0, 0.0), kv).astype(BF16)
        flipped = kv.T
        kvt[:TOK, rows] = flipped.astype(BF16)
        kvt[TOK:, rows] = jnp.ones((16, TOK), BF16)
        acc[rows, :] = jnp.zeros((TOK, TOK), F32)
        norm = jnp.sum(flipped[:HEAD_DIM] * flipped[:HEAD_DIM], axis=0, keepdims=True)
        return jnp.maximum(largest, norm)

    largest = lax.fori_loop(0, N_CTX, prepare, jnp.zeros((1, TOK), F32), unroll=4)
    key_norm = jnp.max(largest)
    for c in range(N_CTX, (SEQ + LARGE) // TOK):
        rows = slice(c * TOK, (c + 1) * TOK)
        kx[rows, :] = jnp.where(feature == HEADS, 1.0, 0.0).astype(BF16)
        vx[rows, :] = jnp.zeros((TOK, TOK), BF16)
        kvt[:, rows] = jnp.zeros((TOK + 16, TOK), BF16)

    lane_q = lanes((TQ, TOK))
    feature_q = lane_q.astype(F32) - HEAD_DIM
    row_t = lax.broadcasted_iota(jnp.int32, (TOK, TQ), 0)

    def three(row, start, rest):
        hi = row.astype(BF16).astype(F32)
        mid = (row - hi).astype(BF16).astype(F32)
        low = row - hi - mid
        for n, part in enumerate((hi, mid, low)):
            rest = jnp.where(row_t == start + n, part, rest)
        return rest.astype(BF16)

    def query_block(i, carry):
        c0 = i * Q_SRC
        qd = recv_ref[pl.ds(c0, Q_SRC), TOK:OUT_ROWS, :].reshape(TQ, TOK).astype(F32)
        idcols = []
        lowest, highest = None, None
        for a in range(Q_SRC):
            both = recv_ref[c0 + a, OUT_ROWS:, :].astype(F32)
            idcols.append(jnp.broadcast_to(both[8:9], (TOK, TOK)).T[:HALF])
            lowest = both if lowest is None else jnp.minimum(lowest, both)
            highest = both if highest is None else jnp.maximum(highest, both)
        idcol = jnp.concatenate(idcols, axis=0)
        every = idm[...]
        below = jnp.sum(jnp.where(every < jnp.min(lowest), 1.0, 0.0)).astype(jnp.int32)
        upto = jnp.sum(jnp.where(every <= jnp.max(highest), 1.0, 0.0)).astype(jnp.int32)
        start = below // TOK
        extent = upto - start * TOK
        n_large = (extent + (LARGE - 1 - MIDDLE - SMALL)) // LARGE
        extent = jnp.maximum(extent - n_large * LARGE, 0)
        n_middle = (extent + (MIDDLE - 1 - SMALL)) // MIDDLE
        n_small = (jnp.maximum(extent - n_middle * MIDDLE, 0) + (SMALL - 1)) // SMALL

        qdt = qd.T
        other = jnp.where((feature_q != idcol) & (feature_q < HEADS + 1), MASK, 0.0)
        qxt_f = jnp.where(lane_q < HEAD_DIM, qd * 0.125, other).T
        norms = jnp.sum(qxt_f[:HEAD_DIM] * qxt_f[:HEAD_DIM], axis=0, keepdims=True)
        small = jnp.max(norms) * key_norm < 1600.0

        def steps(step, state, wanted=True):
            def run(first, size):
                def body(n, state):
                    base = first + n * size
                    return step(
                        [
                            pl.ds(pl.multiple_of(base + t * SUB, TOK), SUB)
                            for t in range(size // SUB)
                        ],
                        state,
                    )

                return body

            first = start * TOK
            for size, count in ((LARGE, n_large), (MIDDLE, n_middle), (SMALL, n_small)):
                state = lax.fori_loop(0, jnp.where(wanted, count, 0), run(first, size), state)
                first = first + count * size
            return state

        def largest_step(tiles, top):
            for rows in tiles:
                s = dot_nn(kx[rows, :], qxt_f.astype(BF16))
                for r in range(0, SUB, 8):
                    top = jnp.maximum(top, s[r:r + 8])
            return top

        top = steps(largest_step, jnp.full((8, TQ), MASK, F32), ~small)
        top = jnp.where(small, 0.0, jnp.max(top, axis=0, keepdims=True))
        qxt = three(-top, HEAD_DIM + HEADS + 1, qxt_f)

        def value_step(tiles, ot):
            e = [jnp.exp(dot_nn(kx[rows, :], qxt)).astype(BF16) for rows in tiles]
            for n in range(0, len(tiles), 2):
                k = min(2, len(tiles) - n)
                rows = pl.ds(pl.multiple_of(tiles[n].start, TOK), k * SUB)
                ot = ot + dot_nn(kvt[HEAD_DIM:, rows], jnp.concatenate(e[n:n + k], axis=0))
            for rows, part in zip(tiles, e):
                sc[rows, :] = part
            return ot

        ot = steps(value_step, jnp.zeros((HEAD_DIM + 16, TQ), F32))
        inv = 1.0 / ot[HEAD_DIM:HEAD_DIM + 1]
        ot = (ot[:HEAD_DIM] * inv).astype(BF16).astype(F32)
        delta = jnp.sum(ot * qdt[HEAD_DIM:], axis=0, keepdims=True)
        gxt = three(-delta, 0, jnp.where(row_t < HEAD_DIM, 0.0, qdt))

        scaled = (qdt * inv).T
        right = jnp.concatenate(
            [
                jnp.where(lane_q < HEAD_DIM, scaled * 0.125, 0.0).astype(BF16),
                jnp.where(lane_q >= HEAD_DIM, scaled, 0.0).astype(BF16),
            ],
            axis=0,
        )

        def grad_step(tiles, dqt):
            e = [sc[rows, :] for rows in tiles]
            ds = [part * dot_nn(vx[rows, :], gxt).astype(BF16) for rows, part in zip(tiles, e)]
            for n in range(0, len(tiles), 2):
                k = min(2, len(tiles) - n)
                rows = pl.ds(pl.multiple_of(tiles[n].start, TOK), k * SUB)
                dqt = dqt + dot_nn(kvt[:HEAD_DIM, rows], jnp.concatenate(ds[n:n + k], axis=0))
            added = [
                acc[rows, :] + dot_nn(jnp.concatenate([a, b], axis=1), right)
                for rows, a, b in zip(tiles, ds, e)
            ]
            for rows, part in zip(tiles, added):
                acc[rows, :] = part
            return dqt

        dqt = steps(grad_step, jnp.zeros((HEAD_DIM, TQ), F32))
        both = jnp.concatenate([ot, dqt * (inv * 0.125)], axis=0).T.astype(BF16)
        for a in range(Q_SRC):
            send_ref[(c0 + a) % N_R, (c0 + a) // N_R, TOK:, :] = both[a * HALF:(a + 1) * HALF]
        return carry

    lax.fori_loop(0, N_QB, query_block, 0)

    def finish(c, carry):
        rows = pl.ds(pl.multiple_of(c * TOK, TOK), TOK)
        send_ref[c % N_R, c // N_R, :TOK, :] = acc[rows, :].astype(BF16)
        return carry

    lax.fori_loop(0, N_CTX, finish, 0, unroll=4)


def attend(recv):
    vmem = pl.BlockSpec(memory_space=pltpu.VMEM)
    padded = SEQ + LARGE
    return pl.pallas_call(
        attend_kernel,
        in_specs=[vmem],
        out_specs=vmem,
        out_shape=jax.ShapeDtypeStruct((N_R, N_X, OUT_ROWS, TOK), BF16),
        scratch_shapes=[
            pltpu.VMEM((padded, TOK), BF16),
            pltpu.VMEM((padded, TOK), BF16),
            pltpu.VMEM((TOK + 16, padded), BF16),
            pltpu.VMEM((N_CTX, TOK), F32),
            pltpu.VMEM((padded, TQ), BF16),
            pltpu.VMEM((padded, TOK), F32),
        ],
        compiler_params=pltpu.CompilerParams(vmem_limit_bytes=28 * MIB),
        cost_estimate=pl.CostEstimate(flops=25 * 10**9, bytes_accessed=4 * 10**6, transcendentals=0),
        name="attend",
    )(recv)


def unproject_kernel(me_ref, c0, c1, c2, c3, x_hbm, gain_hbm, wqkv_hbm, wo_hbm, out_ref, gx_ref, x_ref, gain_ref, wqkv, wo, sems, in_sems):
    copies = [
        fetch(wqkv_hbm, wo_hbm, wqkv, wo, sems, d, (me_ref[0] ^ d) * 256) for d in range(N_X)
    ]
    for group in copies:
        for copy in group:
            copy.start()
    inputs = [
        pltpu.make_async_copy(x_hbm, x_ref, in_sems.at[0]),
        pltpu.make_async_copy(gain_hbm, gain_ref, in_sems.at[1]),
    ]
    for copy in inputs:
        copy.start()
    result = jnp.zeros((TOK, D), F32)
    g = jnp.zeros((TOK, D), F32)
    for d, ref in enumerate((c0, c1, c2, c3)):
        for copy in copies[d]:
            copy.wait()
        result = result + dot_nn(ref[:, 768:], wo[d])
        for m in range(3):
            g = g + dot_nt(ref[:, m * 256:(m + 1) * 256], wqkv[d, m])
    out_ref[...] = result.astype(BF16)
    for copy in inputs:
        copy.wait()
    x = x_ref[...].astype(F32)
    cen = x - jnp.mean(x, axis=1, keepdims=True)
    inv = lax.rsqrt(jnp.mean(cen * cen, axis=1, keepdims=True) + EPSILON)
    x_hat = cen * inv
    g = g * gain_ref[...]
    gx = inv * (
        g - jnp.mean(g, axis=1, keepdims=True) - x_hat * jnp.mean(g * x_hat, axis=1, keepdims=True)
    )
    gx_ref[...] = gx.astype(BF16)


def unproject(me, pieces, x, gain, w_qkv, w_out):
    vmem = pl.BlockSpec(memory_space=pltpu.VMEM)
    hbm = pl.BlockSpec(memory_space=pltpu.HBM)
    return pl.pallas_call(
        unproject_kernel,
        in_specs=[pl.BlockSpec(memory_space=pltpu.SMEM)] + [vmem] * 4 + [hbm] * 4,
        out_specs=[vmem] * 2,
        out_shape=[jax.ShapeDtypeStruct((TOK, D), BF16)] * 2,
        scratch_shapes=[
            pltpu.VMEM((TOK, D), BF16),
            pltpu.VMEM((1, D), F32),
            *FETCHED,
            pltpu.SemaphoreType.DMA((2,)),
        ],
        compiler_params=pltpu.CompilerParams(vmem_limit_bytes=56 * MIB),
        cost_estimate=pl.CostEstimate(flops=7 * 10**9, bytes_accessed=10**7, transcendentals=0),
        name="unproject",
    )(me, *pieces, x, gain, w_qkv, w_out)


def repack_kernel(me_ref, recv_ref, *cols_refs):
    for d, cols_ref in enumerate(cols_refs):
        at = me_ref[0] ^ d
        parts = [[], [], [], []]
        for h in range(4):
            lo, hi = recv_ref[2 * h, at].astype(F32), recv_ref[2 * h + 1, at].astype(F32)
            kv = lo[:TOK] + hi[:TOK]
            aq = jnp.concatenate([lo[TOK:], hi[TOK:]], axis=0)
            parts[0].append(aq[:, HEAD_DIM:])
            parts[1].append(kv[:, :HEAD_DIM])
            parts[2].append(kv[:, HEAD_DIM:])
            parts[3].append(aq[:, :HEAD_DIM])
        for n, part in enumerate(parts):
            cols_ref[:, n * 256:(n + 1) * 256] = jnp.concatenate(part, axis=1).astype(BF16)


def repack(me, recv):
    vmem = pl.BlockSpec(memory_space=pltpu.VMEM)
    return pl.pallas_call(
        repack_kernel,
        in_specs=[pl.BlockSpec(memory_space=pltpu.SMEM), vmem],
        out_specs=[vmem] * N_X,
        out_shape=[jax.ShapeDtypeStruct((TOK, D), BF16)] * N_X,
        compiler_params=pltpu.CompilerParams(vmem_limit_bytes=16 * MIB),
        name="repack",
    )(me, recv)


def weights_kernel(me_ref, c0, c1, c2, c3, b0, b1, b2, b3, own_ref, other_ref):
    cols_refs = (c0, c1, c2, c3)
    cols = jnp.concatenate([ref[...] for ref in cols_refs], axis=0)
    both = jnp.concatenate([b0[...], b1[...], b2[...], b3[...]], axis=0)
    first_core = me_ref[1] == 0
    for zl in range(2):
        parts = []
        for m in (2 * zl, 2 * zl + 1):
            left = dot_tn(both[:, m * 256:(m + 1) * 256], cols[:, :768])
            right = dot_tn(cols[:, 768:], both[:, D + m * 256:D + (m + 1) * 256])
            parts.append((left, right))
        for n in range(2):
            cols_of = slice(0, 768) if n == 0 else slice(768, D)
            own = jnp.where(first_core, parts[0][n], parts[1][n]).astype(BF16)
            other = jnp.where(first_core, parts[1][n], parts[0][n]).astype(BF16)
            for r in range(N_R):
                own_ref[8 * zl + r, :, cols_of] = own[32 * r:32 * r + 32]
                other_ref[8 * zl + r, :, cols_of] = other[32 * r:32 * r + 32]


def weights(me, cols, both):
    vmem = pl.BlockSpec(memory_space=pltpu.VMEM)
    return pl.pallas_call(
        weights_kernel,
        in_specs=[pl.BlockSpec(memory_space=pltpu.SMEM)] + [vmem] * 8,
        out_specs=[vmem] * 2,
        out_shape=[jax.ShapeDtypeStruct((N_CTX // 2, 32, D), BF16)] * 2,
        cost_estimate=pl.CostEstimate(flops=2 * 10**9, bytes_accessed=4 * 10**6, transcendentals=0),
        compiler_params=pltpu.CompilerParams(vmem_limit_bytes=24 * MIB),
        name="weights",
    )(me, *cols, *both)


def assemble_kernel(me_ref, a_ref, b_ref, c_ref, d_ref, qkv_ref, out_ref):
    for d, ref in enumerate((a_ref, b_ref, c_ref, d_ref)):
        start = (me_ref[0] ^ d) * 256
        part = ref[...].astype(F32)
        for n in range(3):
            cols = pl.ds(pl.multiple_of(start + n * D, 256), 256)
            qkv_ref[:, cols] = part[:, n * 256:(n + 1) * 256]
        out_ref[:, pl.ds(pl.multiple_of(start, 256), 256)] = part[:, 768:]


def assemble(me, parts):
    vmem = pl.BlockSpec(memory_space=pltpu.VMEM)
    return pl.pallas_call(
        assemble_kernel,
        in_specs=[pl.BlockSpec(memory_space=pltpu.SMEM)] + [vmem] * 4,
        out_specs=[vmem] * 2,
        out_shape=[jax.ShapeDtypeStruct((32, 3 * D), F32), jax.ShapeDtypeStruct((32, D), F32)],
        compiler_params=pltpu.CompilerParams(vmem_limit_bytes=8 * MIB),
        name="assemble",
    )(me, *parts)


def swap(piece, axis, d):
    return piece if d == 0 else lax.ppermute(piece, axis, [(i, i ^ d) for i in range(4)])


def shards(patches, gain, w_qkv, w_out, image_ids, grad_out):
    x, cot = patches[0], grad_out[0]
    gain_row = gain[None]
    me = jnp.stack([lax.axis_index("x"), lax.axis_index("core")]).astype(jnp.int32)
    send, both = project(x, cot, gain_row, image_ids, w_qkv, w_out)
    recv = lax.all_to_all(send, ("x", "r"), 0, 0, tiled=True)
    recv, both = lax.optimization_barrier((recv, both))
    both = [swap(both, "x", d) for d in range(N_X)]
    done, both = lax.optimization_barrier((attend(recv), both))
    back = lax.all_to_all(done, "r", 0, 0, tiled=True)
    cols = repack(me, back)
    own, other = weights(me, cols, both)
    got = lax.ppermute(other, "core", [(0, 1), (1, 0)])
    cols = [swap(cols[d], "x", d) for d in range(N_X)]
    terms = (own.astype(F32) + got.astype(F32)).astype(BF16)
    parts = lax.all_to_all(terms, ("zl", "r"), 0, 0, tiled=True)
    out, grad_x = unproject(me, cols, x, gain_row, w_qkv, w_out)
    factor = 1.0 / math.sqrt(N_GRP * SEQ)
    share = (jnp.sum(parts.astype(F32), axis=0) * factor).astype(BF16)
    flip = [(s * N_X + j, j * N_X + s) for s in range(N_GRP) for j in range(N_X)]
    share_qkv = lax.ppermute(share[:, :768], ("zl", "core", "x"), flip)
    share = jnp.concatenate([share_qkv, share[:, 768:]], axis=1)
    shares = [swap(share, ("zl", "core"), d) for d in range(N_GRP)]
    grad_qkv, grad_w_out = assemble(lax.axis_index(("zl", "core")).astype(jnp.int32)[None], shares)
    return out[None], grad_x[None], grad_qkv, grad_w_out


def solution(mesh):
    fine = Mesh(mesh.devices.reshape(2, 2, N_X, N_R), ("zl", "core", "x", "r"))
    grp, ctx = ("zl", "core"), ("x", "r")
    in_specs = (P(grp, ctx, None), P(), P(), P(), P(grp, ctx), P(grp, ctx, None))
    out_specs = (P(grp, ctx, None), P(grp, ctx, None), P(ctx, None), P(ctx, None))
    return jax.shard_map(shards, mesh=fine, in_specs=in_specs, out_specs=out_specs, check_vma=False)
```

time: 160 us -> 152 us (0.950); the launches traced: 159 us -> 153 us
  Pallas kernels: 52.7 us -> 46.4 us
  waiting for transfers between devices: 44.1 us -> 39.5 us
  starting transfers between devices: 22.7 us -> 25.6 us
    ppermute x9, waiting for transfers between devices: 14.4 us -> 0.02 us  [swap(): lax.ppermute(piece, axis, [(i, i ^ d) for i in range(4)])]
    all_to_all x1, waiting for transfers between devices: 4.51 us -> 12.8 us  [shards(): parts = lax.all_to_all(terms, ('zl', 'r'), 0, 0, tiled=True)]
    pallas_call x1, Pallas kernels: 4.89 us -> 1.87 us  [weights(): pl.pallas_call(weights_kernel, in_specs=[pl.BlockSpec(memory_space=pltpu....]
    pallas_call x1, Pallas kernels: 32.1 us -> 30 us  [attend(): pl.pallas_call(attend_kernel, in_specs=[vmem], out_specs=vmem, out_shape=...]
    ppermute x1 -> x2, waiting for transfers between devices: 2.33 us -> 4.14 us  [the longest x1 2.29 us: shards(): got = lax.ppermute(other, 'core', [(0, 1), (1, 0)])]
    unnamed x24 -> x28, local copies, waits for them, and re-layouts: 2.49 us -> 3.64 us
    ppermute x1 -> x2, starting transfers between devices: 3.06 us -> 3.99 us  [the longest x1 3.53 us: shards(): share_qkv = lax.ppermute(share[:, :768], ('zl', 'core', 'x'), flip)]
    pallas_call x1 -> x2, Pallas kernels: 6.8 us -> 7.07 us  [the longest x1 6.12 us: project(): pl.pallas_call(project_kernel, in_specs=[hbm] * 6, out_specs=[vmem] * 2,...]
  transfers between devices with their start and end apart: 12 -> 13, of which waited for: 7 -> 4; matrix products, arithmetic and copies ran while one was open for 0% -> 0% of each run, Pallas kernels for 25% -> 24%
where the time goes in v3:
time: 152 us; the launch traced here: 153 us
  Pallas kernels  46.4 us (31%)
  waiting for transfers between devices  39.5 us (26%)
  blocking collectives  35.2 us (23%)
  starting transfers between devices  25.6 us (17%)
  local copies, waits for them, and re-layouts  3.65 us (2%)
  other arithmetic  1.68 us (1%)
    all_to_all x1, blocking collectives, shards(): recv = lax.all_to_all(send, ('x', 'r'), 0, 0, tiled=True)  35.2 us
    pallas_call x1, Pallas kernels, attend(): pl.pallas_call(attend_kernel, in_specs=[vmem], out_specs=vmem, out_shape=...  30 us
    all_to_all x1, waiting for transfers between devices, shards(): back = lax.all_to_all(done, 'r', 0, 0, tiled=True)  22.5 us
    all_to_all x1, waiting for transfers between devices, shards(): parts = lax.all_to_all(terms, ('zl', 'r'), 0, 0, tiled=True)  12.8 us
    ppermute x9, starting transfers between devices, swap(): lax.ppermute(piece, axis, [(i, i ^ d) for i in range(4)])  12.2 us
    pallas_call x1, Pallas kernels, unproject(): pl.pallas_call(unproject_kernel, in_specs=[pl.BlockSpec(memory_space=pltp...  6.69 us
    pallas_call x1, Pallas kernels, project(): pl.pallas_call(project_kernel, in_specs=[hbm] * 6, out_specs=[vmem] * 2,...  6.12 us
    all_to_all x1, starting transfers between devices, shards(): parts = lax.all_to_all(terms, ('zl', 'r'), 0, 0, tiled=True)  5.82 us
  transfers between devices with their start and end apart: 13, of which 4 were waited for; matrix products, arithmetic and copies ran while one was open for 0% of the time, Pallas kernels for 24%

profile of v3, /device:TPU:1, one launch (start us, length us, event | category | flops | bytes accessed | tf_op | source)
XLA Modules:
  0.0 153.0 jit_solution(11681276891697949752)
XLA Ops:
  0.6 6.1 %project.1 = (bf16[32,208,128]{2,1,0:T(8,128)(2,1)}, bf16[128,2048]{1,0:T(8,128)(2,1)}) custom-call(bf16[128,1024]{1,0:T(8,128)(2,1)} %bitcast.9, bf16[128,1024]{1,0:T(8,128)(2,1)} %bitcast.8, f32[1,1024]{1,0:T(1,128)} %bitcast.11, s32[1,128]{1,0:T(1,128)} %ids_hbm.1, bf16[1024,3072]{1,0:T(8,128)(2,1)} %wqkv_hbm.3, bf16[1024,1024]{1,0:T(8,128)(2,1)} %wo_hbm.3), custom_call_target="tpu_custom_call" | custom-call | tf_op jit(solution)/shard_map/project/pallas_call | solution.py:111
  6.8 35.2 %all_to_all.15.recv_ref = bf16[32,208,128]{2,1,0:T(8,128)(2,1)S(1)} all-to-all(bf16[32,208,128]{2,1,0:T(8,128)(2,1)} %get-tuple-element.23), channel_id=1, replica_groups=mesh['zl'=2,'core'=2,'x'=4,'r'=8] {'x','r'}, dimensions={0} | all-to-all | bytes 3407872 | tf_op jit(solution)/shard_map/all_to_all | solution.py:454
  42.0 0.7 collective-permute-start.2
  42.7 1.1 collective-permute-start.1
  43.8 1.5 collective-permute-start
  45.2 30.0 %attend.1 = bf16[8,4,192,128]{3,2,1,0:T(8,128)(2,1)} custom-call(bf16[32,208,128]{2,1,0:T(8,128)(2,1)S(1)} %all_to_all.15.recv_ref), custom_call_target="tpu_custom_call" | custom-call | flops 24999999488 | bytes 4000000 | tf_op jit(solution)/shard_map/attend/pallas_call | solution.py:288
  75.2 0.8 copy-done.2
  76.0 3.6 %all-to-all-start.1 = ((bf16[8,4,192,128]{3,2,1,0:T(8,128)(2,1)}), bf16[8,4,192,128]{3,2,1,0:T(8,128)(2,1)S(1)}, u32[]{:S(2)}, u32[]{:S(2)}) async-start(bf16[8,4,192,128]{3,2,1,0:T(8,128)(2,1)} %attend.1), calls=%async_computation.1 | async-start | bytes 3145728 | tf_op jit(solution)/shard_map/all_to_all | solution.py:458
  79.6 0.1 pad_add_fusion.me_ref
  79.7 22.5 %all-to-all-done.1.recv_ref = bf16[8,4,192,128]{3,2,1,0:T(8,128)(2,1)S(1)} async-done(((bf16[8,4,192,128]{3,2,1,0:T(8,128)(2,1)}), bf16[8,4,192,128]{3,2,1,0:T(8,128)(2,1)S(1)}, u32[]{:S(2)}, u32[]{:S(2)}) %all-to-all-start.1) | async-done | bytes 1572896 | tf_op jit(solution)/shard_map/all_to_all | solution.py:458
  102.2 1.0 repack.1
  103.2 0.0 copy-start.9
  103.3 1.4 copy-done.3
  104.6 1.9 %weights.1 = (bf16[16,32,1024]{2,1,0:T(8,128)(2,1)S(1)}, bf16[16,32,1024]{2,1,0:T(8,128)(2,1)S(1)}) custom-call(s32[2]{0:T(128)S(1)} %pad_add_fusion.me_ref, bf16[128,1024]{1,0:T(8,128)(2,1)S(1)} %get-tuple-element.28.c0, bf16[128,1024]{1,0:T(8,128)(2,1)S(1)} %get-tuple-element.29.c1, bf16[128,1024]{1,0:T(8,128)(2,1)S(1)} %get-tuple-element.30.c2, ...), custom_call_target="tpu_custom_call" | custom-call | flops 2000000000 | bytes 4000000 | tf_op jit(solution)/shard_map/weights/pallas_call | solution.py:412
  106.6 0.5 collective-permute-start.6
  107.0 2.3 %collective-permute-done.6 = bf16[16,32,1024]{2,1,0:T(8,128)(2,1)S(1)} collective-permute-done((bf16[16,32,1024]{2,1,0:T(8,128)(2,1)S(1)}, bf16[16,32,1024]{2,1,0:T(8,128)(2,1)S(1)}, u32[]{:S(2)}, u32[]{:S(2)}) %collective-permute-start.6) | collective-permute-done | bytes 1048608 | tf_op jit(solution)/shard_map/ppermute | solution.py:461
  109.3 1.4 add_convert_fusion
  110.7 5.8 %all-to-all-start.2 = ((bf16[16,32,1024]{2,1,0:T(8,128)(2,1)}), bf16[16,32,1024]{2,1,0:T(8,128)(2,1)S(1)}, u32[]{:S(2)}, u32[]{:S(2)}) async-start(bf16[16,32,1024]{2,1,0:T(8,128)(2,1)} %add_convert_fusion), calls=%async_computation.2 | async-start | bytes 2097152 | tf_op jit(solution)/shard_map/all_to_all | solution.py:464
  116.6 0.1 collective-permute-start.3
  116.7 0.1 collective-permute-start.4
  116.8 3.7 %collective-permute-start.5 = (bf16[128,1024]{1,0:T(8,128)(2,1)S(1)}, bf16[128,1024]{1,0:T(8,128)(2,1)S(1)}, u32[]{:S(2)}, u32[]{:S(2)}) collective-permute-start(bf16[128,1024]{1,0:T(8,128)(2,1)S(1)} %copy-done.6), channel_id=1, source_target_pairs={{0,24},{8,16},{16,8},{24,0},{1,25},{9,17},{17,9},{25,1},{2,26},{10... | collective-permute-start | bytes 786440 | tf_op jit(solution)/shard_map/ppermute | solution.py:446
  120.5 12.8 %all-to-all-done.2 = bf16[16,32,1024]{2,1,0:T(8,128)(2,1)S(1)} async-done(((bf16[16,32,1024]{2,1,0:T(8,128)(2,1)}), bf16[16,32,1024]{2,1,0:T(8,128)(2,1)S(1)}, u32[]{:S(2)}, u32[]{:S(2)}) %all-to-all-start.2) | async-done | bytes 1048608 | tf_op jit(solution)/shard_map/all_to_all | solution.py:464
  133.3 0.2 convert_reduce_fusion
  133.5 3.5 %collective-permute-start.7 = (bf16[32,768]{1,0:T(8,128)(2,1)S(1)}, bf16[32,768]{1,0:T(8,128)(2,1)S(1)}, u32[]{:S(2)}, u32[]{:S(2)}) collective-permute-start(bf16[32,768]{1,0:T(8,128)(2,1)S(1)} %slice.8), channel_id=1, source_target_pairs={{0,0},{8,32},{16,64},{24,96},{32,8},{40,40},{48,72},{56,104},{64,1... | collective-permute-start | bytes 147464 | tf_op jit(solution)/shard_map/ppermute | solution.py:469
  137.1 1.9 %collective-permute-done.7 = bf16[32,768]{1,0:T(8,128)(2,1)S(1)} collective-permute-done((bf16[32,768]{1,0:T(8,128)(2,1)S(1)}, bf16[32,768]{1,0:T(8,128)(2,1)S(1)}, u32[]{:S(2)}, u32[]{:S(2)}) %collective-permute-start.7) | collective-permute-done | bytes 49184 | tf_op jit(solution)/shard_map/ppermute | solution.py:469
  138.9 4.6 %collective-permute-start.10 = (bf16[32,1024]{1,0:T(8,128)(2,1)S(1)}, bf16[32,1024]{1,0:T(8,128)(2,1)S(1)}, u32[]{:S(2)}, u32[]{:S(2)}) collective-permute-start(bf16[32,1024]{1,0:T(8,128)(2,1)S(1)} %pad_maximum_fusion.a_ref), channel_id=1, source_target_pairs={{0,96},{32,64},{64,32},{96,0},{1,97},{33,65},{65,33},{97,1},{2,98}... | collective-permute-start | bytes 196616 | tf_op jit(solution)/shard_map/ppermute | solution.py:446
  143.5 0.5 collective-permute-start.8
  144.0 0.2 copy-done.11
  144.2 0.5 copy-done.12
  144.7 0.7 copy-done.13
  145.4 6.7 %unproject.1 = (bf16[128,1024]{1,0:T(8,128)(2,1)}, bf16[128,1024]{1,0:T(8,128)(2,1)}) custom-call(s32[2]{0:T(128)} %copy-done, bf16[128,1024]{1,0:T(8,128)(2,1)} %copy-done.4, bf16[128,1024]{1,0:T(8,128)(2,1)} %copy-done.11, bf16[128,1024]{1,0:T(8,128)(2,1)} %copy-done.12, bf16[128,1024]{1,0:T(8,128)(2,1)} %copy-done.13, bf16[128,1024]{1,0:T(8,128)(2,1)} %bitcast.10, ...), custom_call_target="tpu_custom_call" | custom-call | flops 7000000000 | bytes 10000000 | tf_op jit(solution)/shard_map/unproject/pallas_call | solution.py:345
  152.1 0.8 assemble.1
  (36 shorter events, 0.1 us)
Async XLA Ops:
  6.8 35.2 %copy-start.1 = (bf16[128,2048]{1,0:T(8,128)(2,1)S(1)}, bf16[128,2048]{1,0:T(8,128)(2,1)}, u32[]{:S(2)}) copy-start(bf16[128,2048]{1,0:T(8,128)(2,1)} %get-tuple-element.34.b0) | copy-start | bytes 1572868
  42.0 33.2 %collective-permute-start.2 = (bf16[128,2048]{1,0:T(8,128)(2,1)S(1)}, bf16[128,2048]{1,0:T(8,128)(2,1)S(1)}, u32[]{:S(2)}, u32[]{:S(2)}) collective-permute-start(bf16[128,2048]{1,0:T(8,128)(2,1)S(1)} %copy-done.1), channel_id=1, source_target_pairs={{0,24},{8,16},{16,8},{24,0},{1,25},{9,17},{17,9},{25,1},{2,26},{10... | collective-permute-start | bytes 1572872 | tf_op jit(solution)/shard_map/ppermute | solution.py:446
  42.7 32.5 %collective-permute-start.1 = (bf16[128,2048]{1,0:T(8,128)(2,1)S(1)}, bf16[128,2048]{1,0:T(8,128)(2,1)S(1)}, u32[]{:S(2)}, u32[]{:S(2)}) collective-permute-start(bf16[128,2048]{1,0:T(8,128)(2,1)S(1)} %copy-done.1), channel_id=1, source_target_pairs={{0,16},{8,24},{16,0},{24,8},{1,17},{9,25},{17,1},{25,9},{2,18},{10... | collective-permute-start | bytes 1572872 | tf_op jit(solution)/shard_map/ppermute | solution.py:446
  43.8 31.5 %collective-permute-start = (bf16[128,2048]{1,0:T(8,128)(2,1)S(1)}, bf16[128,2048]{1,0:T(8,128)(2,1)S(1)}, u32[]{:S(2)}, u32[]{:S(2)}) collective-permute-start(bf16[128,2048]{1,0:T(8,128)(2,1)S(1)} %copy-done.1), channel_id=1, source_target_pairs={{0,8},{8,0},{16,24},{24,16},{1,9},{9,1},{17,25},{25,17},{2,10},{10... | collective-permute-start | bytes 1572872 | tf_op jit(solution)/shard_map/ppermute | solution.py:446
  75.2 0.8 copy-start.2
  76.0 26.2 %all-to-all-start.1 = ((bf16[8,4,192,128]{3,2,1,0:T(8,128)(2,1)}), bf16[8,4,192,128]{3,2,1,0:T(8,128)(2,1)S(1)}, u32[]{:S(2)}, u32[]{:S(2)}) async-start(bf16[8,4,192,128]{3,2,1,0:T(8,128)(2,1)} %attend.1), calls=%async_computation.1 | async-start | bytes 3145728 | tf_op jit(solution)/shard_map/all_to_all | solution.py:458
  79.7 26.8 %copy-start = (s32[2]{0:T(128)}, s32[2]{0:T(128)S(1)}, u32[]{:S(2)}) copy-start(s32[2]{0:T(128)S(1)} %pad_add_fusion.me_ref) | copy-start | bytes 28
  103.2 3.3 %copy-start.4 = (bf16[128,1024]{1,0:T(8,128)(2,1)}, bf16[128,1024]{1,0:T(8,128)(2,1)S(1)}, u32[]{:S(2)}) copy-start(bf16[128,1024]{1,0:T(8,128)(2,1)S(1)} %get-tuple-element.28.c0) | copy-start | bytes 786436
  103.2 3.3 %copy-start.5 = (bf16[128,1024]{1,0:T(8,128)(2,1)}, bf16[128,1024]{1,0:T(8,128)(2,1)S(1)}, u32[]{:S(2)}) copy-start(bf16[128,1024]{1,0:T(8,128)(2,1)S(1)} %get-tuple-element.31.c3) | copy-start | bytes 786436
  103.2 3.3 %copy-start.7 = (bf16[128,1024]{1,0:T(8,128)(2,1)}, bf16[128,1024]{1,0:T(8,128)(2,1)S(1)}, u32[]{:S(2)}) copy-start(bf16[128,1024]{1,0:T(8,128)(2,1)S(1)} %get-tuple-element.30.c2) | copy-start | bytes 786436
  103.2 3.3 %copy-start.9 = (bf16[128,1024]{1,0:T(8,128)(2,1)}, bf16[128,1024]{1,0:T(8,128)(2,1)S(1)}, u32[]{:S(2)}) copy-start(bf16[128,1024]{1,0:T(8,128)(2,1)S(1)} %get-tuple-element.29.c1) | copy-start | bytes 786436
  103.3 1.4 copy-start.3
  106.6 2.8 %collective-permute-start.6 = (bf16[16,32,1024]{2,1,0:T(8,128)(2,1)S(1)}, bf16[16,32,1024]{2,1,0:T(8,128)(2,1)S(1)}, u32[]{:S(2)}, u32[]{:S(2)}) collective-permute-start(bf16[16,32,1024]{2,1,0:T(8,128)(2,1)S(1)} %get-tuple-element.39), channel_id=1, source_target_pairs={{0,32},{32,0},{1,33},{33,1},{2,34},{34,2},{3,35},{35,3},{4,36},{36... | collective-permute-start | bytes 3145736 | tf_op jit(solution)/shard_map/ppermute | solution.py:461
  109.3 7.2 %copy-start.10 = (bf16[128,1024]{1,0:T(8,128)(2,1)S(1)}, bf16[128,1024]{1,0:T(8,128)(2,1)}, u32[]{:S(2)}) copy-start(bf16[128,1024]{1,0:T(8,128)(2,1)} %copy-done.9) | copy-start | bytes 786436
  109.3 7.4 %copy-start.8 = (bf16[128,1024]{1,0:T(8,128)(2,1)S(1)}, bf16[128,1024]{1,0:T(8,128)(2,1)}, u32[]{:S(2)}) copy-start(bf16[128,1024]{1,0:T(8,128)(2,1)} %copy-done.7) | copy-start | bytes 786436
  109.3 7.4 %copy-start.6 = (bf16[128,1024]{1,0:T(8,128)(2,1)S(1)}, bf16[128,1024]{1,0:T(8,128)(2,1)}, u32[]{:S(2)}) copy-start(bf16[128,1024]{1,0:T(8,128)(2,1)} %copy-done.5) | copy-start | bytes 786436
  110.7 22.6 %all-to-all-start.2 = ((bf16[16,32,1024]{2,1,0:T(8,128)(2,1)}), bf16[16,32,1024]{2,1,0:T(8,128)(2,1)S(1)}, u32[]{:S(2)}, u32[]{:S(2)}) async-start(bf16[16,32,1024]{2,1,0:T(8,128)(2,1)} %add_convert_fusion), calls=%async_computation.2 | async-start | bytes 2097152 | tf_op jit(solution)/shard_map/all_to_all | solution.py:464
  116.6 26.9 %collective-permute-start.3 = (bf16[128,1024]{1,0:T(8,128)(2,1)S(1)}, bf16[128,1024]{1,0:T(8,128)(2,1)S(1)}, u32[]{:S(2)}, u32[]{:S(2)}) collective-permute-start(bf16[128,1024]{1,0:T(8,128)(2,1)S(1)} %copy-done.10), channel_id=1, source_target_pairs={{0,8},{8,0},{16,24},{24,16},{1,9},{9,1},{17,25},{25,17},{2,10},{10... | collective-permute-start | bytes 786440 | tf_op jit(solution)/shard_map/ppermute | solution.py:446
  116.7 27.3 %collective-permute-start.4 = (bf16[128,1024]{1,0:T(8,128)(2,1)S(1)}, bf16[128,1024]{1,0:T(8,128)(2,1)S(1)}, u32[]{:S(2)}, u32[]{:S(2)}) collective-permute-start(bf16[128,1024]{1,0:T(8,128)(2,1)S(1)} %copy-done.8), channel_id=1, source_target_pairs={{0,16},{8,24},{16,0},{24,8},{1,17},{9,25},{17,1},{25,9},{2,18},{10... | collective-permute-start | bytes 786440 | tf_op jit(solution)/shard_map/ppermute | solution.py:446
  116.8 27.2 %collective-permute-start.5 = (bf16[128,1024]{1,0:T(8,128)(2,1)S(1)}, bf16[128,1024]{1,0:T(8,128)(2,1)S(1)}, u32[]{:S(2)}, u32[]{:S(2)}) collective-permute-start(bf16[128,1024]{1,0:T(8,128)(2,1)S(1)} %copy-done.6), channel_id=1, source_target_pairs={{0,24},{8,16},{16,8},{24,0},{1,25},{9,17},{17,9},{25,1},{2,26},{10... | collective-permute-start | bytes 786440 | tf_op jit(solution)/shard_map/ppermute | solution.py:446
  133.5 5.4 %collective-permute-start.7 = (bf16[32,768]{1,0:T(8,128)(2,1)S(1)}, bf16[32,768]{1,0:T(8,128)(2,1)S(1)}, u32[]{:S(2)}, u32[]{:S(2)}) collective-permute-start(bf16[32,768]{1,0:T(8,128)(2,1)S(1)} %slice.8), channel_id=1, source_target_pairs={{0,0},{8,32},{16,64},{24,96},{32,8},{40,40},{48,72},{56,104},{64,1... | collective-permute-start | bytes 147464 | tf_op jit(solution)/shard_map/ppermute | solution.py:469
  138.9 13.2 %collective-permute-start.10 = (bf16[32,1024]{1,0:T(8,128)(2,1)S(1)}, bf16[32,1024]{1,0:T(8,128)(2,1)S(1)}, u32[]{:S(2)}, u32[]{:S(2)}) collective-permute-start(bf16[32,1024]{1,0:T(8,128)(2,1)S(1)} %pad_maximum_fusion.a_ref), channel_id=1, source_target_pairs={{0,96},{32,64},{64,32},{96,0},{1,97},{33,65},{65,33},{97,1},{2,98}... | collective-permute-start | bytes 196616 | tf_op jit(solution)/shard_map/ppermute | solution.py:446
  143.5 8.6 %collective-permute-start.9 = (bf16[32,1024]{1,0:T(8,128)(2,1)S(1)}, bf16[32,1024]{1,0:T(8,128)(2,1)S(1)}, u32[]{:S(2)}, u32[]{:S(2)}) collective-permute-start(bf16[32,1024]{1,0:T(8,128)(2,1)S(1)} %pad_maximum_fusion.a_ref), channel_id=1, source_target_pairs={{0,64},{32,96},{64,0},{96,32},{1,65},{33,97},{65,1},{97,33},{2,66}... | collective-permute-start | bytes 196616 | tf_op jit(solution)/shard_map/ppermute | solution.py:446
  143.5 0.7 copy-start.11
  143.5 8.6 %collective-permute-start.8 = (bf16[32,1024]{1,0:T(8,128)(2,1)S(1)}, bf16[32,1024]{1,0:T(8,128)(2,1)S(1)}, u32[]{:S(2)}, u32[]{:S(2)}) collective-permute-start(bf16[32,1024]{1,0:T(8,128)(2,1)S(1)} %pad_maximum_fusion.a_ref), channel_id=1, source_target_pairs={{0,32},{32,0},{64,96},{96,64},{1,33},{33,1},{65,97},{97,65},{2,34}... | collective-permute-start | bytes 196616 | tf_op jit(solution)/shard_map/ppermute | solution.py:446
  144.0 0.7 copy-start.12
  144.7 0.7 copy-start.13

commit v4 on v3

--- a/solution.py
+++ b/solution.py
@@ -450,11 +450,12 @@
     x, cot = patches[0], grad_out[0]
     gain_row = gain[None]
     me = jnp.stack([lax.axis_index("x"), lax.axis_index("core")]).astype(jnp.int32)
+    me_grp = lax.axis_index(("zl", "core")).astype(jnp.int32)[None]
     send, both = project(x, cot, gain_row, image_ids, w_qkv, w_out)
     recv = lax.all_to_all(send, ("x", "r"), 0, 0, tiled=True)
     recv, both = lax.optimization_barrier((recv, both))
     both = [swap(both, "x", d) for d in range(N_X)]
-    done, both = lax.optimization_barrier((attend(recv), both))
+    done, both, me, me_grp = lax.optimization_barrier((attend(recv), both, me, me_grp))
     back = lax.all_to_all(done, "r", 0, 0, tiled=True)
     cols = repack(me, back)
     own, other = weights(me, cols, both)
@@ -469,7 +470,7 @@
     share_qkv = lax.ppermute(share[:, :768], ("zl", "core", "x"), flip)
     share = jnp.concatenate([share_qkv, share[:, 768:]], axis=1)
     shares = [swap(share, ("zl", "core"), d) for d in range(N_GRP)]
-    grad_qkv, grad_w_out = assemble(lax.axis_index(("zl", "core")).astype(jnp.int32)[None], shares)
+    grad_qkv, grad_w_out = assemble(me_grp, shares)
     return out[None], grad_x[None], grad_qkv, grad_w_out
 
 

time: 152 us -> 146 us (0.961)
  blocking collectives: 35.2 us -> 21.8 us
  starting transfers between devices: 25.6 us -> 36.9 us
  Pallas kernels: 46.4 us -> 42.8 us
  local copies, waits for them, and re-layouts: 3.65 us -> 1.41 us
    all_to_all x1, blocking collectives: 35.2 us -> 21.8 us  [shards(): back = lax.all_to_all(done, 'r', 0, 0, tiled=True)]
    all_to_all x1, starting transfers between devices: 3.58 us -> 11.3 us  [shards(): recv = lax.all_to_all(send, ('x', 'r'), 0, 0, tiled=True)]
    ppermute x1, starting transfers between devices: 0.47 us -> 5.43 us  [shards(): got = lax.ppermute(other, 'core', [(0, 1), (1, 0)])]
    pallas_call x1, Pallas kernels: 30 us -> 26.4 us  [attend(): pl.pallas_call(attend_kernel, in_specs=[vmem], out_specs=vmem, out_shape=...]
    unnamed x28 -> x12, local copies, waits for them, and re-layouts: 3.64 us -> 1.4 us
    all_to_all x1, starting transfers between devices: 5.82 us -> 4.11 us  [shards(): parts = lax.all_to_all(terms, ('zl', 'r'), 0, 0, tiled=True)]
  transfers between devices with their start and end apart: 13 -> 13, of which waited for: 4 -> 4; matrix products, arithmetic and copies ran while one was open for 0% -> 0% of each run, Pallas kernels for 24% -> 23%
where the time goes in v4:
time: 146 us
  Pallas kernels  42.8 us (29%)
  waiting for transfers between devices  40.3 us (28%)
  starting transfers between devices  36.9 us (25%)
  blocking collectives  21.8 us (15%)
  other arithmetic  1.68 us (1%)
    pallas_call x1, Pallas kernels, attend(): pl.pallas_call(attend_kernel, in_specs=[vmem], out_specs=vmem, out_shape=...  26.4 us
    all_to_all x1, waiting for transfers between devices, shards(): recv = lax.all_to_all(send, ('x', 'r'), 0, 0, tiled=True)  23.6 us
    all_to_all x1, blocking collectives, shards(): back = lax.all_to_all(done, 'r', 0, 0, tiled=True)  21.8 us
    all_to_all x1, waiting for transfers between devices, shards(): parts = lax.all_to_all(terms, ('zl', 'r'), 0, 0, tiled=True)  12.8 us
    ppermute x9, starting transfers between devices, swap(): lax.ppermute(piece, axis, [(i, i ^ d) for i in range(4)])  11.8 us
    all_to_all x1, starting transfers between devices, shards(): recv = lax.all_to_all(send, ('x', 'r'), 0, 0, tiled=True)  11.3 us
    pallas_call x1, Pallas kernels, unproject(): pl.pallas_call(unproject_kernel, in_specs=[pl.BlockSpec(memory_space=pltp...  6.7 us
    pallas_call x1, Pallas kernels, project(): pl.pallas_call(project_kernel, in_specs=[hbm] * 6, out_specs=[vmem] * 2,...  6.12 us
  transfers between devices with their start and end apart: 13, of which 4 were waited for; matrix products, arithmetic and copies ran while one was open for 0% of the time, Pallas kernels for 23%

profile of v4, /device:TPU:1, one launch (start us, length us, event | category | flops | bytes accessed | tf_op | source)
XLA Modules:
  0.0 145.7 jit_solution(603524014988360328)
XLA Ops:
  0.6 6.1 %project.1 = (bf16[32,208,128]{2,1,0:T(8,128)(2,1)}, bf16[128,2048]{1,0:T(8,128)(2,1)}) custom-call(bf16[128,1024]{1,0:T(8,128)(2,1)} %bitcast.9, bf16[128,1024]{1,0:T(8,128)(2,1)} %bitcast.8, f32[1,1024]{1,0:T(1,128)} %bitcast.11, s32[1,128]{1,0:T(1,128)} %ids_hbm.1, bf16[1024,3072]{1,0:T(8,128)(2,1)} %wqkv_hbm.3, bf16[1024,1024]{1,0:T(8,128)(2,1)} %wo_hbm.3), custom_call_target="tpu_custom_call" | custom-call | tf_op jit(solution)/shard_map/project/pallas_call | solution.py:111
  6.8 11.3 %all-to-all-start = ((bf16[32,208,128]{2,1,0:T(8,128)(2,1)}), bf16[32,208,128]{2,1,0:T(8,128)(2,1)S(1)}, u32[]{:S(2)}, u32[]{:S(2)}) async-start(bf16[32,208,128]{2,1,0:T(8,128)(2,1)} %get-tuple-element.25), calls=%async_computation | async-start | bytes 3407872 | tf_op jit(solution)/shard_map/all_to_all | solution.py:455
  18.1 0.1 pad_add_fusion.me_ref
  18.2 23.6 %all-to-all-done.recv_ref = bf16[32,208,128]{2,1,0:T(8,128)(2,1)S(1)} async-done(((bf16[32,208,128]{2,1,0:T(8,128)(2,1)}), bf16[32,208,128]{2,1,0:T(8,128)(2,1)S(1)}, u32[]{:S(2)}, u32[]{:S(2)}) %all-to-all-start) | async-done | bytes 1703968 | tf_op jit(solution)/shard_map/all_to_all | solution.py:455
  41.8 0.8 collective-permute-start.1
  42.6 2.5 %collective-permute-start = (bf16[128,2048]{1,0:T(8,128)(2,1)S(1)}, bf16[128,2048]{1,0:T(8,128)(2,1)S(1)}, u32[]{:S(2)}, u32[]{:S(2)}) collective-permute-start(bf16[128,2048]{1,0:T(8,128)(2,1)S(1)} %copy-done.1), channel_id=1, source_target_pairs={{0,8},{8,0},{16,24},{24,16},{1,9},{9,1},{17,25},{25,17},{2,10},{10... | collective-permute-start | bytes 1572872 | tf_op jit(solution)/shard_map/ppermute | solution.py:446
  45.1 26.4 %attend.1 = bf16[8,4,192,128]{3,2,1,0:T(8,128)(2,1)S(1)} custom-call(bf16[32,208,128]{2,1,0:T(8,128)(2,1)S(1)} %all-to-all-done.recv_ref), custom_call_target="tpu_custom_call" | custom-call | flops 24999999488 | bytes 4000000 | tf_op jit(solution)/shard_map/attend/pallas_call | solution.py:288
  71.5 0.0 collective-permute-done.2.b3
  71.5 0.0 collective-permute-done.b1
  71.5 21.8 %all_to_all.15.recv_ref = bf16[8,4,192,128]{3,2,1,0:T(8,128)(2,1)S(1)} all-to-all(bf16[8,4,192,128]{3,2,1,0:T(8,128)(2,1)S(1)} %attend.1), channel_id=1, replica_groups=mesh['zl'=2,'core'=2,'x'=4,'r'=8] {'r'}, dimensions={0} | all-to-all | bytes 3145728 | tf_op jit(solution)/shard_map/all_to_all | solution.py:459
  93.3 1.0 repack.1
  94.2 0.0 copy-start.2
  94.2 1.8 %weights.1 = (bf16[16,32,1024]{2,1,0:T(8,128)(2,1)S(1)}, bf16[16,32,1024]{2,1,0:T(8,128)(2,1)S(1)}) custom-call(s32[2]{0:T(128)S(1)} %pad_add_fusion.me_ref, bf16[128,1024]{1,0:T(8,128)(2,1)S(1)} %get-tuple-element.31.c0, bf16[128,1024]{1,0:T(8,128)(2,1)S(1)} %get-tuple-element.32.c1, bf16[128,1024]{1,0:T(8,128)(2,1)S(1)} %get-tuple-element.33.c2, ...), custom_call_target="tpu_custom_call" | custom-call | flops 2000000000 | bytes 4000000 | tf_op jit(solution)/shard_map/weights/pallas_call | solution.py:412
  96.1 5.4 %collective-permute-start.6 = (bf16[16,32,1024]{2,1,0:T(8,128)(2,1)S(1)}, bf16[16,32,1024]{2,1,0:T(8,128)(2,1)S(1)}, u32[]{:S(2)}, u32[]{:S(2)}) collective-permute-start(bf16[16,32,1024]{2,1,0:T(8,128)(2,1)S(1)} %get-tuple-element.43), channel_id=1, source_target_pairs={{0,32},{32,0},{1,33},{33,1},{2,34},{34,2},{3,35},{35,3},{4,36},{36... | collective-permute-start | bytes 3145736 | tf_op jit(solution)/shard_map/ppermute | solution.py:462
  101.5 2.3 %collective-permute-done.6 = bf16[16,32,1024]{2,1,0:T(8,128)(2,1)S(1)} collective-permute-done((bf16[16,32,1024]{2,1,0:T(8,128)(2,1)S(1)}, bf16[16,32,1024]{2,1,0:T(8,128)(2,1)S(1)}, u32[]{:S(2)}, u32[]{:S(2)}) %collective-permute-start.6) | collective-permute-done | bytes 1048608 | tf_op jit(solution)/shard_map/ppermute | solution.py:462
  103.8 1.4 add_convert_fusion
  105.2 4.1 %all-to-all-start.2 = ((bf16[16,32,1024]{2,1,0:T(8,128)(2,1)}), bf16[16,32,1024]{2,1,0:T(8,128)(2,1)S(1)}, u32[]{:S(2)}, u32[]{:S(2)}) async-start(bf16[16,32,1024]{2,1,0:T(8,128)(2,1)} %add_convert_fusion), calls=%async_computation.2 | async-start | bytes 2097152 | tf_op jit(solution)/shard_map/all_to_all | solution.py:465
  109.3 0.7 collective-permute-start.3
  110.0 2.9 %collective-permute-start.4 = (bf16[128,1024]{1,0:T(8,128)(2,1)S(1)}, bf16[128,1024]{1,0:T(8,128)(2,1)S(1)}, u32[]{:S(2)}, u32[]{:S(2)}) collective-permute-start(bf16[128,1024]{1,0:T(8,128)(2,1)S(1)} %get-tuple-element.33.c2), channel_id=1, source_target_pairs={{0,16},{8,24},{16,0},{24,8},{1,17},{9,25},{17,1},{25,9},{2,18},{10... | collective-permute-start | bytes 786440 | tf_op jit(solution)/shard_map/ppermute | solution.py:446
  112.9 0.4 collective-permute-start.5
  113.3 12.8 %all-to-all-done.2 = bf16[16,32,1024]{2,1,0:T(8,128)(2,1)S(1)} async-done(((bf16[16,32,1024]{2,1,0:T(8,128)(2,1)}), bf16[16,32,1024]{2,1,0:T(8,128)(2,1)S(1)}, u32[]{:S(2)}, u32[]{:S(2)}) %all-to-all-start.2) | async-done | bytes 1048608 | tf_op jit(solution)/shard_map/all_to_all | solution.py:465
  126.1 0.2 convert_reduce_fusion
  126.3 4.3 %collective-permute-start.7 = (bf16[32,768]{1,0:T(8,128)(2,1)S(1)}, bf16[32,768]{1,0:T(8,128)(2,1)S(1)}, u32[]{:S(2)}, u32[]{:S(2)}) collective-permute-start(bf16[32,768]{1,0:T(8,128)(2,1)S(1)} %slice.8), channel_id=1, source_target_pairs={{0,0},{8,32},{16,64},{24,96},{32,8},{40,40},{48,72},{56,104},{64,1... | collective-permute-start | bytes 147464 | tf_op jit(solution)/shard_map/ppermute | solution.py:470
  130.6 1.6 %collective-permute-done.7 = bf16[32,768]{1,0:T(8,128)(2,1)S(1)} collective-permute-done((bf16[32,768]{1,0:T(8,128)(2,1)S(1)}, bf16[32,768]{1,0:T(8,128)(2,1)S(1)}, u32[]{:S(2)}, u32[]{:S(2)}) %collective-permute-start.7) | collective-permute-done | bytes 49184 | tf_op jit(solution)/shard_map/ppermute | solution.py:470
  132.2 4.1 %collective-permute-start.10 = (bf16[32,1024]{1,0:T(8,128)(2,1)S(1)}, bf16[32,1024]{1,0:T(8,128)(2,1)S(1)}, u32[]{:S(2)}, u32[]{:S(2)}) collective-permute-start(bf16[32,1024]{1,0:T(8,128)(2,1)S(1)} %pad_maximum_fusion.a_ref), channel_id=1, source_target_pairs={{0,96},{32,64},{64,32},{96,0},{1,97},{33,65},{65,33},{97,1},{2,98}... | collective-permute-start | bytes 196616 | tf_op jit(solution)/shard_map/ppermute | solution.py:446
  136.3 0.0 collective-permute-start.9
  136.3 0.5 collective-permute-start.8
  136.8 0.2 copy-done.3
  137.0 0.5 copy-done.4
  137.5 0.7 copy-done.5
  138.1 6.7 %unproject.1 = (bf16[128,1024]{1,0:T(8,128)(2,1)}, bf16[128,1024]{1,0:T(8,128)(2,1)}) custom-call(s32[2]{0:T(128)} %copy-done, bf16[128,1024]{1,0:T(8,128)(2,1)} %copy-done.2, bf16[128,1024]{1,0:T(8,128)(2,1)} %copy-done.3, bf16[128,1024]{1,0:T(8,128)(2,1)} %copy-done.4, bf16[128,1024]{1,0:T(8,128)(2,1)} %copy-done.5, bf16[128,1024]{1,0:T(8,128)(2,1)} %bitcast.10, ...), custom_call_target="tpu_custom_call" | custom-call | flops 7000000000 | bytes 10000000 | tf_op jit(solution)/shard_map/unproject/pallas_call | solution.py:345
  144.9 0.8 assemble.1
  (20 shorter events, 0.1 us)
Async XLA Ops:
  6.8 35.1 %copy-start.1 = (bf16[128,2048]{1,0:T(8,128)(2,1)S(1)}, bf16[128,2048]{1,0:T(8,128)(2,1)}, u32[]{:S(2)}) copy-start(bf16[128,2048]{1,0:T(8,128)(2,1)} %get-tuple-element.38.b0) | copy-start | bytes 1572868
  6.8 35.1 %all-to-all-start = ((bf16[32,208,128]{2,1,0:T(8,128)(2,1)}), bf16[32,208,128]{2,1,0:T(8,128)(2,1)S(1)}, u32[]{:S(2)}, u32[]{:S(2)}) async-start(bf16[32,208,128]{2,1,0:T(8,128)(2,1)} %get-tuple-element.25), calls=%async_computation | async-start | bytes 3407872 | tf_op jit(solution)/shard_map/all_to_all | solution.py:455
  18.2 76.0 %copy-start = (s32[2]{0:T(128)}, s32[2]{0:T(128)S(1)}, u32[]{:S(2)}) copy-start(s32[2]{0:T(128)S(1)} %pad_add_fusion.me_ref) | copy-start | bytes 28
  41.8 29.6 %collective-permute-start.2 = (bf16[128,2048]{1,0:T(8,128)(2,1)S(1)}, bf16[128,2048]{1,0:T(8,128)(2,1)S(1)}, u32[]{:S(2)}, u32[]{:S(2)}) collective-permute-start(bf16[128,2048]{1,0:T(8,128)(2,1)S(1)} %copy-done.1), channel_id=1, source_target_pairs={{0,24},{8,16},{16,8},{24,0},{1,25},{9,17},{17,9},{25,1},{2,26},{10... | collective-permute-start | bytes 1572872 | tf_op jit(solution)/shard_map/ppermute | solution.py:446
  41.8 29.6 %collective-permute-start.1 = (bf16[128,2048]{1,0:T(8,128)(2,1)S(1)}, bf16[128,2048]{1,0:T(8,128)(2,1)S(1)}, u32[]{:S(2)}, u32[]{:S(2)}) collective-permute-start(bf16[128,2048]{1,0:T(8,128)(2,1)S(1)} %copy-done.1), channel_id=1, source_target_pairs={{0,16},{8,24},{16,0},{24,8},{1,17},{9,25},{17,1},{25,9},{2,18},{10... | collective-permute-start | bytes 1572872 | tf_op jit(solution)/shard_map/ppermute | solution.py:446
  42.6 28.9 %collective-permute-start = (bf16[128,2048]{1,0:T(8,128)(2,1)S(1)}, bf16[128,2048]{1,0:T(8,128)(2,1)S(1)}, u32[]{:S(2)}, u32[]{:S(2)}) collective-permute-start(bf16[128,2048]{1,0:T(8,128)(2,1)S(1)} %copy-done.1), channel_id=1, source_target_pairs={{0,8},{8,0},{16,24},{24,16},{1,9},{9,1},{17,25},{25,17},{2,10},{10... | collective-permute-start | bytes 1572872 | tf_op jit(solution)/shard_map/ppermute | solution.py:446
  94.2 1.9 %copy-start.2 = (bf16[128,1024]{1,0:T(8,128)(2,1)}, bf16[128,1024]{1,0:T(8,128)(2,1)S(1)}, u32[]{:S(2)}) copy-start(bf16[128,1024]{1,0:T(8,128)(2,1)S(1)} %get-tuple-element.31.c0) | copy-start | bytes 786436
  96.1 7.7 %collective-permute-start.6 = (bf16[16,32,1024]{2,1,0:T(8,128)(2,1)S(1)}, bf16[16,32,1024]{2,1,0:T(8,128)(2,1)S(1)}, u32[]{:S(2)}, u32[]{:S(2)}) collective-permute-start(bf16[16,32,1024]{2,1,0:T(8,128)(2,1)S(1)} %get-tuple-element.43), channel_id=1, source_target_pairs={{0,32},{32,0},{1,33},{33,1},{2,34},{34,2},{3,35},{35,3},{4,36},{36... | collective-permute-start | bytes 3145736 | tf_op jit(solution)/shard_map/ppermute | solution.py:462
  105.2 20.8 %all-to-all-start.2 = ((bf16[16,32,1024]{2,1,0:T(8,128)(2,1)}), bf16[16,32,1024]{2,1,0:T(8,128)(2,1)S(1)}, u32[]{:S(2)}, u32[]{:S(2)}) async-start(bf16[16,32,1024]{2,1,0:T(8,128)(2,1)} %add_convert_fusion), calls=%async_computation.2 | async-start | bytes 2097152 | tf_op jit(solution)/shard_map/all_to_all | solution.py:465
  109.3 26.9 %collective-permute-start.3 = (bf16[128,1024]{1,0:T(8,128)(2,1)S(1)}, bf16[128,1024]{1,0:T(8,128)(2,1)S(1)}, u32[]{:S(2)}, u32[]{:S(2)}) collective-permute-start(bf16[128,1024]{1,0:T(8,128)(2,1)S(1)} %get-tuple-element.32.c1), channel_id=1, source_target_pairs={{0,8},{8,0},{16,24},{24,16},{1,9},{9,1},{17,25},{25,17},{2,10},{10... | collective-permute-start | bytes 786440 | tf_op jit(solution)/shard_map/ppermute | solution.py:446
  110.0 26.7 %collective-permute-start.4 = (bf16[128,1024]{1,0:T(8,128)(2,1)S(1)}, bf16[128,1024]{1,0:T(8,128)(2,1)S(1)}, u32[]{:S(2)}, u32[]{:S(2)}) collective-permute-start(bf16[128,1024]{1,0:T(8,128)(2,1)S(1)} %get-tuple-element.33.c2), channel_id=1, source_target_pairs={{0,16},{8,24},{16,0},{24,8},{1,17},{9,25},{17,1},{25,9},{2,18},{10... | collective-permute-start | bytes 786440 | tf_op jit(solution)/shard_map/ppermute | solution.py:446
  112.9 23.8 %collective-permute-start.5 = (bf16[128,1024]{1,0:T(8,128)(2,1)S(1)}, bf16[128,1024]{1,0:T(8,128)(2,1)S(1)}, u32[]{:S(2)}, u32[]{:S(2)}) collective-permute-start(bf16[128,1024]{1,0:T(8,128)(2,1)S(1)} %get-tuple-element.34.c3), channel_id=1, source_target_pairs={{0,24},{8,16},{16,8},{24,0},{1,25},{9,17},{17,9},{25,1},{2,26},{10... | collective-permute-start | bytes 786440 | tf_op jit(solution)/shard_map/ppermute | solution.py:446
  126.3 5.9 %collective-permute-start.7 = (bf16[32,768]{1,0:T(8,128)(2,1)S(1)}, bf16[32,768]{1,0:T(8,128)(2,1)S(1)}, u32[]{:S(2)}, u32[]{:S(2)}) collective-permute-start(bf16[32,768]{1,0:T(8,128)(2,1)S(1)} %slice.8), channel_id=1, source_target_pairs={{0,0},{8,32},{16,64},{24,96},{32,8},{40,40},{48,72},{56,104},{64,1... | collective-permute-start | bytes 147464 | tf_op jit(solution)/shard_map/ppermute | solution.py:470
  132.2 12.7 %collective-permute-start.10 = (bf16[32,1024]{1,0:T(8,128)(2,1)S(1)}, bf16[32,1024]{1,0:T(8,128)(2,1)S(1)}, u32[]{:S(2)}, u32[]{:S(2)}) collective-permute-start(bf16[32,1024]{1,0:T(8,128)(2,1)S(1)} %pad_maximum_fusion.a_ref), channel_id=1, source_target_pairs={{0,96},{32,64},{64,32},{96,0},{1,97},{33,65},{65,33},{97,1},{2,98}... | collective-permute-start | bytes 196616 | tf_op jit(solution)/shard_map/ppermute | solution.py:446
  136.3 8.6 %collective-permute-start.9 = (bf16[32,1024]{1,0:T(8,128)(2,1)S(1)}, bf16[32,1024]{1,0:T(8,128)(2,1)S(1)}, u32[]{:S(2)}, u32[]{:S(2)}) collective-permute-start(bf16[32,1024]{1,0:T(8,128)(2,1)S(1)} %pad_maximum_fusion.a_ref), channel_id=1, source_target_pairs={{0,64},{32,96},{64,0},{96,32},{1,65},{33,97},{65,1},{97,33},{2,66}... | collective-permute-start | bytes 196616 | tf_op jit(solution)/shard_map/ppermute | solution.py:446
  136.3 0.7 copy-start.3
  136.3 8.6 %collective-permute-start.8 = (bf16[32,1024]{1,0:T(8,128)(2,1)S(1)}, bf16[32,1024]{1,0:T(8,128)(2,1)S(1)}, u32[]{:S(2)}, u32[]{:S(2)}) collective-permute-start(bf16[32,1024]{1,0:T(8,128)(2,1)S(1)} %pad_maximum_fusion.a_ref), channel_id=1, source_target_pairs={{0,32},{32,0},{64,96},{96,64},{1,33},{33,1},{65,97},{97,65},{2,34}... | collective-permute-start | bytes 196616 | tf_op jit(solution)/shard_map/ppermute | solution.py:446
  136.8 0.7 copy-start.4
  137.4 0.7 copy-start.5

commit v5 on v4

--- a/solution.py
+++ b/solution.py
@@ -353,7 +353,7 @@
             *FETCHED,
             pltpu.SemaphoreType.DMA((2,)),
         ],
-        compiler_params=pltpu.CompilerParams(vmem_limit_bytes=56 * MIB),
+        compiler_params=pltpu.CompilerParams(vmem_limit_bytes=52 * MIB),
         cost_estimate=pl.CostEstimate(flops=7 * 10**9, bytes_accessed=10**7, transcendentals=0),
         name="unproject",
     )(me, *pieces, x, gain, w_qkv, w_out)

time: 146 us -> 145 us (level)
  starting transfers between devices: 36.9 us -> 35.3 us
  blocking collectives: 21.8 us -> 23.4 us
    ppermute x1, starting transfers between devices: 5.43 us -> 3.7 us  [shards(): got = lax.ppermute(other, 'core', [(0, 1), (1, 0)])]
    all_to_all x1, blocking collectives: 21.8 us -> 23.4 us  [shards(): back = lax.all_to_all(done, 'r', 0, 0, tiled=True)]
where the time goes in v5:
time: 145 us; the launch traced here: 144 us
  Pallas kernels  42.6 us (29%)
  waiting for transfers between devices  40.3 us (28%)
  starting transfers between devices  35.3 us (24%)
  blocking collectives  23.4 us (16%)
  other arithmetic  1.68 us (1%)
    pallas_call x1, Pallas kernels, attend(): pl.pallas_call(attend_kernel, in_specs=[vmem], out_specs=vmem, out_shape=...  26.8 us
    all_to_all x1, waiting for transfers between devices, shards(): recv = lax.all_to_all(send, ('x', 'r'), 0, 0, tiled=True)  23.6 us
    all_to_all x1, blocking collectives, shards(): back = lax.all_to_all(done, 'r', 0, 0, tiled=True)  23.4 us
    all_to_all x1, waiting for transfers between devices, shards(): parts = lax.all_to_all(terms, ('zl', 'r'), 0, 0, tiled=True)  12.8 us
    ppermute x9, starting transfers between devices, swap(): lax.ppermute(piece, axis, [(i, i ^ d) for i in range(4)])  11.8 us
    all_to_all x1, starting transfers between devices, shards(): recv = lax.all_to_all(send, ('x', 'r'), 0, 0, tiled=True)  11.3 us
    pallas_call x1, Pallas kernels, project(): pl.pallas_call(project_kernel, in_specs=[hbm] * 6, out_specs=[vmem] * 2,...  6.1 us
    pallas_call x1, Pallas kernels, unproject(): pl.pallas_call(unproject_kernel, in_specs=[pl.BlockSpec(memory_space=pltp...  6.02 us
  transfers between devices with their start and end apart: 13, of which 4 were waited for; matrix products, arithmetic and copies ran while one was open for 0% of the time, Pallas kernels for 23%

profile of v5, /device:TPU:1, one launch (start us, length us, event | category | flops | bytes accessed | tf_op | source)
XLA Modules:
  0.0 144.2 jit_solution(12351298806290108750)
XLA Ops:
  0.6 6.1 %project.1 = (bf16[32,208,128]{2,1,0:T(8,128)(2,1)}, bf16[128,2048]{1,0:T(8,128)(2,1)}) custom-call(bf16[128,1024]{1,0:T(8,128)(2,1)} %bitcast.8, bf16[128,1024]{1,0:T(8,128)(2,1)} %bitcast.12, f32[1,1024]{1,0:T(1,128)} %bitcast.10, s32[1,128]{1,0:T(1,128)} %ids_hbm.1, bf16[1024,3072]{1,0:T(8,128)(2,1)} %wqkv_hbm.3, bf16[1024,1024]{1,0:T(8,128)(2,1)} %wo_hbm.3), custom_call_target="tpu_custom_call" | custom-call | tf_op jit(solution)/shard_map/project/pallas_call | solution.py:111
  6.7 11.3 %all-to-all-start = ((bf16[32,208,128]{2,1,0:T(8,128)(2,1)}), bf16[32,208,128]{2,1,0:T(8,128)(2,1)S(1)}, u32[]{:S(2)}, u32[]{:S(2)}) async-start(bf16[32,208,128]{2,1,0:T(8,128)(2,1)} %get-tuple-element.25), calls=%async_computation | async-start | bytes 3407872 | tf_op jit(solution)/shard_map/all_to_all | solution.py:455
  18.1 0.1 pad_add_fusion.me_ref
  18.2 23.6 %all-to-all-done.recv_ref = bf16[32,208,128]{2,1,0:T(8,128)(2,1)S(1)} async-done(((bf16[32,208,128]{2,1,0:T(8,128)(2,1)}), bf16[32,208,128]{2,1,0:T(8,128)(2,1)S(1)}, u32[]{:S(2)}, u32[]{:S(2)}) %all-to-all-start) | async-done | bytes 1703968 | tf_op jit(solution)/shard_map/all_to_all | solution.py:455
  41.8 0.8 collective-permute-start.1
  42.6 2.5 %collective-permute-start = (bf16[128,2048]{1,0:T(8,128)(2,1)S(1)}, bf16[128,2048]{1,0:T(8,128)(2,1)S(1)}, u32[]{:S(2)}, u32[]{:S(2)}) collective-permute-start(bf16[128,2048]{1,0:T(8,128)(2,1)S(1)} %copy-done.2), channel_id=1, source_target_pairs={{0,8},{8,0},{16,24},{24,16},{1,9},{9,1},{17,25},{25,17},{2,10},{10... | collective-permute-start | bytes 1572872 | tf_op jit(solution)/shard_map/ppermute | solution.py:446
  45.1 26.8 %attend.1 = bf16[8,4,192,128]{3,2,1,0:T(8,128)(2,1)S(1)} custom-call(bf16[32,208,128]{2,1,0:T(8,128)(2,1)S(1)} %all-to-all-done.recv_ref), custom_call_target="tpu_custom_call" | custom-call | flops 24999999488 | bytes 4000000 | tf_op jit(solution)/shard_map/attend/pallas_call | solution.py:288
  71.9 0.0 collective-permute-done.2.b3
  71.9 0.0 collective-permute-done.1.b2
  71.9 23.4 %all_to_all.15.recv_ref = bf16[8,4,192,128]{3,2,1,0:T(8,128)(2,1)S(1)} all-to-all(bf16[8,4,192,128]{3,2,1,0:T(8,128)(2,1)S(1)} %attend.1), channel_id=1, replica_groups=mesh['zl'=2,'core'=2,'x'=4,'r'=8] {'r'}, dimensions={0} | all-to-all | bytes 3145728 | tf_op jit(solution)/shard_map/all_to_all | solution.py:459
  95.3 1.0 repack.1
  96.3 1.9 %weights.1 = (bf16[16,32,1024]{2,1,0:T(8,128)(2,1)S(1)}, bf16[16,32,1024]{2,1,0:T(8,128)(2,1)S(1)}) custom-call(s32[2]{0:T(128)S(1)} %pad_add_fusion.me_ref, bf16[128,1024]{1,0:T(8,128)(2,1)S(1)} %get-tuple-element.31.c0, bf16[128,1024]{1,0:T(8,128)(2,1)S(1)} %get-tuple-element.32.c1, bf16[128,1024]{1,0:T(8,128)(2,1)S(1)} %get-tuple-element.33.c2, ...), custom_call_target="tpu_custom_call" | custom-call | flops 2000000000 | bytes 4000000 | tf_op jit(solution)/shard_map/weights/pallas_call | solution.py:412
  98.2 3.7 %collective-permute-start.6 = (bf16[16,32,1024]{2,1,0:T(8,128)(2,1)S(1)}, bf16[16,32,1024]{2,1,0:T(8,128)(2,1)S(1)}, u32[]{:S(2)}, u32[]{:S(2)}) collective-permute-start(bf16[16,32,1024]{2,1,0:T(8,128)(2,1)S(1)} %get-tuple-element.43), channel_id=1, source_target_pairs={{0,32},{32,0},{1,33},{33,1},{2,34},{34,2},{3,35},{35,3},{4,36},{36... | collective-permute-start | bytes 3145736 | tf_op jit(solution)/shard_map/ppermute | solution.py:462
  101.9 2.3 %collective-permute-done.6 = bf16[16,32,1024]{2,1,0:T(8,128)(2,1)S(1)} collective-permute-done((bf16[16,32,1024]{2,1,0:T(8,128)(2,1)S(1)}, bf16[16,32,1024]{2,1,0:T(8,128)(2,1)S(1)}, u32[]{:S(2)}, u32[]{:S(2)}) %collective-permute-start.6) | collective-permute-done | bytes 1048608 | tf_op jit(solution)/shard_map/ppermute | solution.py:462
  104.2 1.4 add_convert_fusion
  105.6 4.2 %all-to-all-start.2 = ((bf16[16,32,1024]{2,1,0:T(8,128)(2,1)}), bf16[16,32,1024]{2,1,0:T(8,128)(2,1)S(1)}, u32[]{:S(2)}, u32[]{:S(2)}) async-start(bf16[16,32,1024]{2,1,0:T(8,128)(2,1)} %add_convert_fusion), calls=%async_computation.2 | async-start | bytes 2097152 | tf_op jit(solution)/shard_map/all_to_all | solution.py:465
  109.8 0.7 collective-permute-start.3
  110.5 2.9 %collective-permute-start.4 = (bf16[128,1024]{1,0:T(8,128)(2,1)S(1)}, bf16[128,1024]{1,0:T(8,128)(2,1)S(1)}, u32[]{:S(2)}, u32[]{:S(2)}) collective-permute-start(bf16[128,1024]{1,0:T(8,128)(2,1)S(1)} %get-tuple-element.33.c2), channel_id=1, source_target_pairs={{0,16},{8,24},{16,0},{24,8},{1,17},{9,25},{17,1},{25,9},{2,18},{10... | collective-permute-start | bytes 786440 | tf_op jit(solution)/shard_map/ppermute | solution.py:446
  113.4 0.3 collective-permute-start.5
  113.8 12.8 %all-to-all-done.2 = bf16[16,32,1024]{2,1,0:T(8,128)(2,1)S(1)} async-done(((bf16[16,32,1024]{2,1,0:T(8,128)(2,1)}), bf16[16,32,1024]{2,1,0:T(8,128)(2,1)S(1)}, u32[]{:S(2)}, u32[]{:S(2)}) %all-to-all-start.2) | async-done | bytes 1048608 | tf_op jit(solution)/shard_map/all_to_all | solution.py:465
  126.6 0.2 convert_reduce_fusion
  126.8 4.3 %collective-permute-start.7 = (bf16[32,768]{1,0:T(8,128)(2,1)S(1)}, bf16[32,768]{1,0:T(8,128)(2,1)S(1)}, u32[]{:S(2)}, u32[]{:S(2)}) collective-permute-start(bf16[32,768]{1,0:T(8,128)(2,1)S(1)} %slice.8), channel_id=1, source_target_pairs={{0,0},{8,32},{16,64},{24,96},{32,8},{40,40},{48,72},{56,104},{64,1... | collective-permute-start | bytes 147464 | tf_op jit(solution)/shard_map/ppermute | solution.py:470
  131.1 1.6 %collective-permute-done.7 = bf16[32,768]{1,0:T(8,128)(2,1)S(1)} collective-permute-done((bf16[32,768]{1,0:T(8,128)(2,1)S(1)}, bf16[32,768]{1,0:T(8,128)(2,1)S(1)}, u32[]{:S(2)}, u32[]{:S(2)}) %collective-permute-start.7) | collective-permute-done | bytes 49184 | tf_op jit(solution)/shard_map/ppermute | solution.py:470
  132.7 4.1 %collective-permute-start.10 = (bf16[32,1024]{1,0:T(8,128)(2,1)S(1)}, bf16[32,1024]{1,0:T(8,128)(2,1)S(1)}, u32[]{:S(2)}, u32[]{:S(2)}) collective-permute-start(bf16[32,1024]{1,0:T(8,128)(2,1)S(1)} %pad_maximum_fusion.a_ref), channel_id=1, source_target_pairs={{0,96},{32,64},{64,32},{96,0},{1,97},{33,65},{65,33},{97,1},{2,98}... | collective-permute-start | bytes 196616 | tf_op jit(solution)/shard_map/ppermute | solution.py:446
  136.8 0.0 collective-permute-start.9
  136.8 0.0 collective-permute-done.3.c1
  136.8 0.5 collective-permute-start.8
  137.2 0.0 collective-permute-done.4.c2
  137.3 0.0 collective-permute-done.5.c3
  137.3 6.0 %unproject.1 = (bf16[128,1024]{1,0:T(8,128)(2,1)}, bf16[128,1024]{1,0:T(8,128)(2,1)}) custom-call(s32[2]{0:T(128)S(1)} %pad_add_fusion.me_ref, bf16[128,1024]{1,0:T(8,128)(2,1)S(1)} %get-tuple-element.31.c0, bf16[128,1024]{1,0:T(8,128)(2,1)S(1)} %collective-permute-done.3.c1, bf16[128,1024]{1,0:T(8,128)(2,1)S(1)} %collective-permute-done.4.c2, ...), custom_call_target="tpu_custom_call" | custom-call | flops 7000000000 | bytes 10000000 | tf_op jit(solution)/shard_map/unproject/pallas_call | solution.py:345
  143.3 0.0 collective-permute-done.8.b_ref
  143.3 0.8 assemble.1
  (14 shorter events, 0.0 us)
Async XLA Ops:
  6.7 35.1 %copy-start.2 = (bf16[128,2048]{1,0:T(8,128)(2,1)S(1)}, bf16[128,2048]{1,0:T(8,128)(2,1)}, u32[]{:S(2)}) copy-start(bf16[128,2048]{1,0:T(8,128)(2,1)} %get-tuple-element.38.b0) | copy-start | bytes 1572868
  6.7 35.1 %all-to-all-start = ((bf16[32,208,128]{2,1,0:T(8,128)(2,1)}), bf16[32,208,128]{2,1,0:T(8,128)(2,1)S(1)}, u32[]{:S(2)}, u32[]{:S(2)}) async-start(bf16[32,208,128]{2,1,0:T(8,128)(2,1)} %get-tuple-element.25), calls=%async_computation | async-start | bytes 3407872 | tf_op jit(solution)/shard_map/all_to_all | solution.py:455
  41.8 30.1 %collective-permute-start.2 = (bf16[128,2048]{1,0:T(8,128)(2,1)S(1)}, bf16[128,2048]{1,0:T(8,128)(2,1)S(1)}, u32[]{:S(2)}, u32[]{:S(2)}) collective-permute-start(bf16[128,2048]{1,0:T(8,128)(2,1)S(1)} %copy-done.2), channel_id=1, source_target_pairs={{0,24},{8,16},{16,8},{24,0},{1,25},{9,17},{17,9},{25,1},{2,26},{10... | collective-permute-start | bytes 1572872 | tf_op jit(solution)/shard_map/ppermute | solution.py:446
  41.8 30.1 %collective-permute-start.1 = (bf16[128,2048]{1,0:T(8,128)(2,1)S(1)}, bf16[128,2048]{1,0:T(8,128)(2,1)S(1)}, u32[]{:S(2)}, u32[]{:S(2)}) collective-permute-start(bf16[128,2048]{1,0:T(8,128)(2,1)S(1)} %copy-done.2), channel_id=1, source_target_pairs={{0,16},{8,24},{16,0},{24,8},{1,17},{9,25},{17,1},{25,9},{2,18},{10... | collective-permute-start | bytes 1572872 | tf_op jit(solution)/shard_map/ppermute | solution.py:446
  42.6 29.3 %collective-permute-start = (bf16[128,2048]{1,0:T(8,128)(2,1)S(1)}, bf16[128,2048]{1,0:T(8,128)(2,1)S(1)}, u32[]{:S(2)}, u32[]{:S(2)}) collective-permute-start(bf16[128,2048]{1,0:T(8,128)(2,1)S(1)} %copy-done.2), channel_id=1, source_target_pairs={{0,8},{8,0},{16,24},{24,16},{1,9},{9,1},{17,25},{25,17},{2,10},{10... | collective-permute-start | bytes 1572872 | tf_op jit(solution)/shard_map/ppermute | solution.py:446
  98.2 6.0 %collective-permute-start.6 = (bf16[16,32,1024]{2,1,0:T(8,128)(2,1)S(1)}, bf16[16,32,1024]{2,1,0:T(8,128)(2,1)S(1)}, u32[]{:S(2)}, u32[]{:S(2)}) collective-permute-start(bf16[16,32,1024]{2,1,0:T(8,128)(2,1)S(1)} %get-tuple-element.43), channel_id=1, source_target_pairs={{0,32},{32,0},{1,33},{33,1},{2,34},{34,2},{3,35},{35,3},{4,36},{36... | collective-permute-start | bytes 3145736 | tf_op jit(solution)/shard_map/ppermute | solution.py:462
  105.6 31.7 %copy-start = (bf16[1,128,1024]{2,1,0:T(8,128)(2,1)S(1)}, bf16[1,128,1024]{2,1,0:T(8,128)(2,1)}, u32[]{:S(2)}) copy-start(bf16[1,128,1024]{2,1,0:T(8,128)(2,1)} %param.6) | copy-start | bytes 786436
  105.6 31.7 %copy-start.1 = (f32[1024]{0:T(1024)S(1)}, f32[1024]{0:T(1024)}, u32[]{:S(2)}) copy-start(f32[1024]{0:T(1024)} %param.7) | copy-start | bytes 12292
  105.6 21.0 %all-to-all-start.2 = ((bf16[16,32,1024]{2,1,0:T(8,128)(2,1)}), bf16[16,32,1024]{2,1,0:T(8,128)(2,1)S(1)}, u32[]{:S(2)}, u32[]{:S(2)}) async-start(bf16[16,32,1024]{2,1,0:T(8,128)(2,1)} %add_convert_fusion), calls=%async_computation.2 | async-start | bytes 2097152 | tf_op jit(solution)/shard_map/all_to_all | solution.py:465
  109.8 26.9 %collective-permute-start.3 = (bf16[128,1024]{1,0:T(8,128)(2,1)S(1)}, bf16[128,1024]{1,0:T(8,128)(2,1)S(1)}, u32[]{:S(2)}, u32[]{:S(2)}) collective-permute-start(bf16[128,1024]{1,0:T(8,128)(2,1)S(1)} %get-tuple-element.32.c1), channel_id=1, source_target_pairs={{0,8},{8,0},{16,24},{24,16},{1,9},{9,1},{17,25},{25,17},{2,10},{10... | collective-permute-start | bytes 786440 | tf_op jit(solution)/shard_map/ppermute | solution.py:446
  110.5 26.7 %collective-permute-start.4 = (bf16[128,1024]{1,0:T(8,128)(2,1)S(1)}, bf16[128,1024]{1,0:T(8,128)(2,1)S(1)}, u32[]{:S(2)}, u32[]{:S(2)}) collective-permute-start(bf16[128,1024]{1,0:T(8,128)(2,1)S(1)} %get-tuple-element.33.c2), channel_id=1, source_target_pairs={{0,16},{8,24},{16,0},{24,8},{1,17},{9,25},{17,1},{25,9},{2,18},{10... | collective-permute-start | bytes 786440 | tf_op jit(solution)/shard_map/ppermute | solution.py:446
  113.4 23.8 %collective-permute-start.5 = (bf16[128,1024]{1,0:T(8,128)(2,1)S(1)}, bf16[128,1024]{1,0:T(8,128)(2,1)S(1)}, u32[]{:S(2)}, u32[]{:S(2)}) collective-permute-start(bf16[128,1024]{1,0:T(8,128)(2,1)S(1)} %get-tuple-element.34.c3), channel_id=1, source_target_pairs={{0,24},{8,16},{16,8},{24,0},{1,25},{9,17},{17,9},{25,1},{2,26},{10... | collective-permute-start | bytes 786440 | tf_op jit(solution)/shard_map/ppermute | solution.py:446
  126.8 5.9 %collective-permute-start.7 = (bf16[32,768]{1,0:T(8,128)(2,1)S(1)}, bf16[32,768]{1,0:T(8,128)(2,1)S(1)}, u32[]{:S(2)}, u32[]{:S(2)}) collective-permute-start(bf16[32,768]{1,0:T(8,128)(2,1)S(1)} %slice.8), channel_id=1, source_target_pairs={{0,0},{8,32},{16,64},{24,96},{32,8},{40,40},{48,72},{56,104},{64,1... | collective-permute-start | bytes 147464 | tf_op jit(solution)/shard_map/ppermute | solution.py:470
  132.7 10.6 %collective-permute-start.10 = (bf16[32,1024]{1,0:T(8,128)(2,1)S(1)}, bf16[32,1024]{1,0:T(8,128)(2,1)S(1)}, u32[]{:S(2)}, u32[]{:S(2)}) collective-permute-start(bf16[32,1024]{1,0:T(8,128)(2,1)S(1)} %pad_maximum_fusion.a_ref), channel_id=1, source_target_pairs={{0,96},{32,64},{64,32},{96,0},{1,97},{33,65},{65,33},{97,1},{2,98}... | collective-permute-start | bytes 196616 | tf_op jit(solution)/shard_map/ppermute | solution.py:446
  136.8 6.5 %collective-permute-start.9 = (bf16[32,1024]{1,0:T(8,128)(2,1)S(1)}, bf16[32,1024]{1,0:T(8,128)(2,1)S(1)}, u32[]{:S(2)}, u32[]{:S(2)}) collective-permute-start(bf16[32,1024]{1,0:T(8,128)(2,1)S(1)} %pad_maximum_fusion.a_ref), channel_id=1, source_target_pairs={{0,64},{32,96},{64,0},{96,32},{1,65},{33,97},{65,1},{97,33},{2,66}... | collective-permute-start | bytes 196616 | tf_op jit(solution)/shard_map/ppermute | solution.py:446
  136.8 6.6 %collective-permute-start.8 = (bf16[32,1024]{1,0:T(8,128)(2,1)S(1)}, bf16[32,1024]{1,0:T(8,128)(2,1)S(1)}, u32[]{:S(2)}, u32[]{:S(2)}) collective-permute-start(bf16[32,1024]{1,0:T(8,128)(2,1)S(1)} %pad_maximum_fusion.a_ref), channel_id=1, source_target_pairs={{0,32},{32,0},{64,96},{96,64},{1,33},{33,1},{65,97},{97,65},{2,34}... | collective-permute-start | bytes 196616 | tf_op jit(solution)/shard_map/ppermute | solution.py:446

commit v6 on v5

--- a/solution.py
+++ b/solution.py
@@ -136,19 +136,20 @@
         kv = recv_ref[c, :TOK, :].astype(F32)
         idrow = recv_ref[c, OUT_ROWS:, :].astype(F32)[:1]
         idm[pl.ds(c, 1), :] = idrow
-        idcol = jnp.broadcast_to(idrow, (TOK, TOK)).T
+        idcol = jnp.broadcast_to(idrow.astype(BF16), (TOK, TOK)).T.astype(F32)
         extra = jnp.where((feature == idcol) | ((feature > HEADS) & (feature < HEADS + 4)), 1.0, 0.0)
         rows = pl.ds(pl.multiple_of(c * TOK, TOK), TOK)
         kx[rows, :] = jnp.where(lane < HEAD_DIM, kv, extra).astype(BF16)
         vx[rows, :] = jnp.where(lane < HEAD_DIM, jnp.where(lane < 3, 1.0, 0.0), kv).astype(BF16)
-        flipped = kv.T
-        kvt[:TOK, rows] = flipped.astype(BF16)
+        flipped = recv_ref[c, :TOK, :].T
+        kvt[:TOK, rows] = flipped
+        flipped = flipped.astype(F32)
         kvt[TOK:, rows] = jnp.ones((16, TOK), BF16)
         acc[rows, :] = jnp.zeros((TOK, TOK), F32)
         norm = jnp.sum(flipped[:HEAD_DIM] * flipped[:HEAD_DIM], axis=0, keepdims=True)
         return jnp.maximum(largest, norm)
 
-    largest = lax.fori_loop(0, N_CTX, prepare, jnp.zeros((1, TOK), F32), unroll=4)
+    largest = lax.fori_loop(0, N_CTX, prepare, jnp.zeros((1, TOK), F32), unroll=8)
     key_norm = jnp.max(largest)
     for c in range(N_CTX, (SEQ + LARGE) // TOK):
         rows = slice(c * TOK, (c + 1) * TOK)
@@ -175,7 +176,7 @@
         lowest, highest = None, None
         for a in range(Q_SRC):
             both = recv_ref[c0 + a, OUT_ROWS:, :].astype(F32)
-            idcols.append(jnp.broadcast_to(both[8:9], (TOK, TOK)).T[:HALF])
+            idcols.append(jnp.broadcast_to(both[8:9].astype(BF16), (TOK, TOK)).T[:HALF].astype(F32))
             lowest = both if lowest is None else jnp.minimum(lowest, both)
             highest = both if highest is None else jnp.maximum(highest, both)
         idcol = jnp.concatenate(idcols, axis=0)
@@ -189,9 +190,9 @@
         n_middle = (extent + (MIDDLE - 1 - SMALL)) // MIDDLE
         n_small = (jnp.maximum(extent - n_middle * MIDDLE, 0) + (SMALL - 1)) // SMALL
 
-        qdt = qd.T
+        qdt = qd.astype(BF16).T.astype(F32)
         other = jnp.where((feature_q != idcol) & (feature_q < HEADS + 1), MASK, 0.0)
-        qxt_f = jnp.where(lane_q < HEAD_DIM, qd * 0.125, other).T
+        qxt_f = jnp.where(lane_q < HEAD_DIM, qd * 0.125, other).astype(BF16).T.astype(F32)
         norms = jnp.sum(qxt_f[:HEAD_DIM] * qxt_f[:HEAD_DIM], axis=0, keepdims=True)
         small = jnp.max(norms) * key_norm < 1600.0
 
@@ -279,7 +280,7 @@
         send_ref[c % N_R, c // N_R, :TOK, :] = acc[rows, :].astype(BF16)
         return carry
 
-    lax.fori_loop(0, N_CTX, finish, 0, unroll=4)
+    lax.fori_loop(0, N_CTX, finish, 0, unroll=8)
 
 
 def attend(recv):

time: 145 us -> 144 us (level)
  transfers between devices with their start and end apart: 13 -> 13, of which waited for: 4 -> 4; matrix products, arithmetic and copies ran while one was open for 0% -> 0% of each run, Pallas kernels for 23% -> 22%
where the time goes in v6:
time: 144 us; the launch traced here: 143 us
  Pallas kernels  41.5 us (29%)
  waiting for transfers between devices  40.8 us (28%)
  starting transfers between devices  35 us (24%)
  blocking collectives  23.1 us (16%)
  other arithmetic  1.68 us (1%)
    pallas_call x1, Pallas kernels, attend(): pl.pallas_call(attend_kernel, in_specs=[vmem], out_specs=vmem, out_shape=...  25.7 us
    all_to_all x1, waiting for transfers between devices, shards(): recv = lax.all_to_all(send, ('x', 'r'), 0, 0, tiled=True)  23.6 us
    all_to_all x1, blocking collectives, shards(): back = lax.all_to_all(done, 'r', 0, 0, tiled=True)  23.1 us
    all_to_all x1, waiting for transfers between devices, shards(): parts = lax.all_to_all(terms, ('zl', 'r'), 0, 0, tiled=True)  13.1 us
    ppermute x9, starting transfers between devices, swap(): lax.ppermute(piece, axis, [(i, i ^ d) for i in range(4)])  11.7 us
    all_to_all x1, starting transfers between devices, shards(): recv = lax.all_to_all(send, ('x', 'r'), 0, 0, tiled=True)  11.3 us
    pallas_call x1, Pallas kernels, project(): pl.pallas_call(project_kernel, in_specs=[hbm] * 6, out_specs=[vmem] * 2,...  6.1 us
    pallas_call x1, Pallas kernels, unproject(): pl.pallas_call(unproject_kernel, in_specs=[pl.BlockSpec(memory_space=pltp...  6.01 us
  transfers between devices with their start and end apart: 13, of which 4 were waited for; matrix products, arithmetic and copies ran while one was open for 0% of the time, Pallas kernels for 22%

profile of v6, /device:TPU:1, one launch (start us, length us, event | category | flops | bytes accessed | tf_op | source)
XLA Modules:
  0.0 142.9 jit_solution(8354856828719692729)
XLA Ops:
  0.6 6.1 %project.1 = (bf16[32,208,128]{2,1,0:T(8,128)(2,1)}, bf16[128,2048]{1,0:T(8,128)(2,1)}) custom-call(bf16[128,1024]{1,0:T(8,128)(2,1)} %bitcast.8, bf16[128,1024]{1,0:T(8,128)(2,1)} %bitcast.12, f32[1,1024]{1,0:T(1,128)} %bitcast.10, s32[1,128]{1,0:T(1,128)} %ids_hbm.1, bf16[1024,3072]{1,0:T(8,128)(2,1)} %wqkv_hbm.3, bf16[1024,1024]{1,0:T(8,128)(2,1)} %wo_hbm.3), custom_call_target="tpu_custom_call" | custom-call | tf_op jit(solution)/shard_map/project/pallas_call | solution.py:111
  6.7 11.3 %all-to-all-start = ((bf16[32,208,128]{2,1,0:T(8,128)(2,1)}), bf16[32,208,128]{2,1,0:T(8,128)(2,1)S(1)}, u32[]{:S(2)}, u32[]{:S(2)}) async-start(bf16[32,208,128]{2,1,0:T(8,128)(2,1)} %get-tuple-element.25), calls=%async_computation | async-start | bytes 3407872 | tf_op jit(solution)/shard_map/all_to_all | solution.py:456
  18.1 0.1 pad_add_fusion.me_ref
  18.2 23.6 %all-to-all-done.recv_ref = bf16[32,208,128]{2,1,0:T(8,128)(2,1)S(1)} async-done(((bf16[32,208,128]{2,1,0:T(8,128)(2,1)}), bf16[32,208,128]{2,1,0:T(8,128)(2,1)S(1)}, u32[]{:S(2)}, u32[]{:S(2)}) %all-to-all-start) | async-done | bytes 1703968 | tf_op jit(solution)/shard_map/all_to_all | solution.py:456
  41.8 0.8 collective-permute-start.1
  42.6 2.5 %collective-permute-start = (bf16[128,2048]{1,0:T(8,128)(2,1)S(1)}, bf16[128,2048]{1,0:T(8,128)(2,1)S(1)}, u32[]{:S(2)}, u32[]{:S(2)}) collective-permute-start(bf16[128,2048]{1,0:T(8,128)(2,1)S(1)} %copy-done.2), channel_id=1, source_target_pairs={{0,8},{8,0},{16,24},{24,16},{1,9},{9,1},{17,25},{25,17},{2,10},{10... | collective-permute-start | bytes 1572872 | tf_op jit(solution)/shard_map/ppermute | solution.py:447
  45.1 25.7 %attend.1 = bf16[8,4,192,128]{3,2,1,0:T(8,128)(2,1)S(1)} custom-call(bf16[32,208,128]{2,1,0:T(8,128)(2,1)S(1)} %all-to-all-done.recv_ref), custom_call_target="tpu_custom_call" | custom-call | flops 24999999488 | bytes 4000000 | tf_op jit(solution)/shard_map/attend/pallas_call | solution.py:289
  70.8 0.0 collective-permute-done.2.b3
  70.8 0.0 collective-permute-done.b1
  70.8 23.1 %all_to_all.15.recv_ref = bf16[8,4,192,128]{3,2,1,0:T(8,128)(2,1)S(1)} all-to-all(bf16[8,4,192,128]{3,2,1,0:T(8,128)(2,1)S(1)} %attend.1), channel_id=1, replica_groups=mesh['zl'=2,'core'=2,'x'=4,'r'=8] {'r'}, dimensions={0} | all-to-all | bytes 3145728 | tf_op jit(solution)/shard_map/all_to_all | solution.py:460
  94.0 1.0 repack.1
  94.9 1.9 %weights.1 = (bf16[16,32,1024]{2,1,0:T(8,128)(2,1)S(1)}, bf16[16,32,1024]{2,1,0:T(8,128)(2,1)S(1)}) custom-call(s32[2]{0:T(128)S(1)} %pad_add_fusion.me_ref, bf16[128,1024]{1,0:T(8,128)(2,1)S(1)} %get-tuple-element.31.c0, bf16[128,1024]{1,0:T(8,128)(2,1)S(1)} %get-tuple-element.32.c1, bf16[128,1024]{1,0:T(8,128)(2,1)S(1)} %get-tuple-element.33.c2, ...), custom_call_target="tpu_custom_call" | custom-call | flops 2000000000 | bytes 4000000 | tf_op jit(solution)/shard_map/weights/pallas_call | solution.py:413
  96.8 4.0 %collective-permute-start.6 = (bf16[16,32,1024]{2,1,0:T(8,128)(2,1)S(1)}, bf16[16,32,1024]{2,1,0:T(8,128)(2,1)S(1)}, u32[]{:S(2)}, u32[]{:S(2)}) collective-permute-start(bf16[16,32,1024]{2,1,0:T(8,128)(2,1)S(1)} %get-tuple-element.43), channel_id=1, source_target_pairs={{0,32},{32,0},{1,33},{33,1},{2,34},{34,2},{3,35},{35,3},{4,36},{36... | collective-permute-start | bytes 3145736 | tf_op jit(solution)/shard_map/ppermute | solution.py:463
  100.9 2.3 %collective-permute-done.6 = bf16[16,32,1024]{2,1,0:T(8,128)(2,1)S(1)} collective-permute-done((bf16[16,32,1024]{2,1,0:T(8,128)(2,1)S(1)}, bf16[16,32,1024]{2,1,0:T(8,128)(2,1)S(1)}, u32[]{:S(2)}, u32[]{:S(2)}) %collective-permute-start.6) | collective-permute-done | bytes 1048608 | tf_op jit(solution)/shard_map/ppermute | solution.py:463
  103.1 1.4 add_convert_fusion
  104.6 3.8 %all-to-all-start.2 = ((bf16[16,32,1024]{2,1,0:T(8,128)(2,1)}), bf16[16,32,1024]{2,1,0:T(8,128)(2,1)S(1)}, u32[]{:S(2)}, u32[]{:S(2)}) async-start(bf16[16,32,1024]{2,1,0:T(8,128)(2,1)} %add_convert_fusion), calls=%async_computation.2 | async-start | bytes 2097152 | tf_op jit(solution)/shard_map/all_to_all | solution.py:466
  108.3 0.7 collective-permute-start.3
  109.0 2.9 %collective-permute-start.4 = (bf16[128,1024]{1,0:T(8,128)(2,1)S(1)}, bf16[128,1024]{1,0:T(8,128)(2,1)S(1)}, u32[]{:S(2)}, u32[]{:S(2)}) collective-permute-start(bf16[128,1024]{1,0:T(8,128)(2,1)S(1)} %get-tuple-element.33.c2), channel_id=1, source_target_pairs={{0,16},{8,24},{16,0},{24,8},{1,17},{9,25},{17,1},{25,9},{2,18},{10... | collective-permute-start | bytes 786440 | tf_op jit(solution)/shard_map/ppermute | solution.py:447
  111.9 0.3 collective-permute-start.5
  112.3 13.1 %all-to-all-done.2 = bf16[16,32,1024]{2,1,0:T(8,128)(2,1)S(1)} async-done(((bf16[16,32,1024]{2,1,0:T(8,128)(2,1)}), bf16[16,32,1024]{2,1,0:T(8,128)(2,1)S(1)}, u32[]{:S(2)}, u32[]{:S(2)}) %all-to-all-start.2) | async-done | bytes 1048608 | tf_op jit(solution)/shard_map/all_to_all | solution.py:466
  125.4 0.2 convert_reduce_fusion
  125.6 4.1 %collective-permute-start.7 = (bf16[32,768]{1,0:T(8,128)(2,1)S(1)}, bf16[32,768]{1,0:T(8,128)(2,1)S(1)}, u32[]{:S(2)}, u32[]{:S(2)}) collective-permute-start(bf16[32,768]{1,0:T(8,128)(2,1)S(1)} %slice.8), channel_id=1, source_target_pairs={{0,0},{8,32},{16,64},{24,96},{32,8},{40,40},{48,72},{56,104},{64,1... | collective-permute-start | bytes 147464 | tf_op jit(solution)/shard_map/ppermute | solution.py:471
  129.7 1.7 %collective-permute-done.7 = bf16[32,768]{1,0:T(8,128)(2,1)S(1)} collective-permute-done((bf16[32,768]{1,0:T(8,128)(2,1)S(1)}, bf16[32,768]{1,0:T(8,128)(2,1)S(1)}, u32[]{:S(2)}, u32[]{:S(2)}) %collective-permute-start.7) | collective-permute-done | bytes 49184 | tf_op jit(solution)/shard_map/ppermute | solution.py:471
  131.5 4.0 %collective-permute-start.10 = (bf16[32,1024]{1,0:T(8,128)(2,1)S(1)}, bf16[32,1024]{1,0:T(8,128)(2,1)S(1)}, u32[]{:S(2)}, u32[]{:S(2)}) collective-permute-start(bf16[32,1024]{1,0:T(8,128)(2,1)S(1)} %pad_maximum_fusion.a_ref), channel_id=1, source_target_pairs={{0,96},{32,64},{64,32},{96,0},{1,97},{33,65},{65,33},{97,1},{2,98}... | collective-permute-start | bytes 196616 | tf_op jit(solution)/shard_map/ppermute | solution.py:447
  135.5 0.0 collective-permute-start.9
  135.5 0.0 collective-permute-done.3.c1
  135.5 0.5 collective-permute-start.8
  136.0 0.0 collective-permute-done.4.c2
  136.0 0.0 collective-permute-done.5.c3
  136.0 6.0 %unproject.1 = (bf16[128,1024]{1,0:T(8,128)(2,1)}, bf16[128,1024]{1,0:T(8,128)(2,1)}) custom-call(s32[2]{0:T(128)S(1)} %pad_add_fusion.me_ref, bf16[128,1024]{1,0:T(8,128)(2,1)S(1)} %get-tuple-element.31.c0, bf16[128,1024]{1,0:T(8,128)(2,1)S(1)} %collective-permute-done.3.c1, bf16[128,1024]{1,0:T(8,128)(2,1)S(1)} %collective-permute-done.4.c2, ...), custom_call_target="tpu_custom_call" | custom-call | flops 7000000000 | bytes 10000000 | tf_op jit(solution)/shard_map/unproject/pallas_call | solution.py:346
  142.1 0.0 collective-permute-done.8.b_ref
  142.1 0.8 assemble.1
  (14 shorter events, 0.0 us)
Async XLA Ops:
  6.7 35.1 %copy-start.2 = (bf16[128,2048]{1,0:T(8,128)(2,1)S(1)}, bf16[128,2048]{1,0:T(8,128)(2,1)}, u32[]{:S(2)}) copy-start(bf16[128,2048]{1,0:T(8,128)(2,1)} %get-tuple-element.38.b0) | copy-start | bytes 1572868
  6.7 35.1 %all-to-all-start = ((bf16[32,208,128]{2,1,0:T(8,128)(2,1)}), bf16[32,208,128]{2,1,0:T(8,128)(2,1)S(1)}, u32[]{:S(2)}, u32[]{:S(2)}) async-start(bf16[32,208,128]{2,1,0:T(8,128)(2,1)} %get-tuple-element.25), calls=%async_computation | async-start | bytes 3407872 | tf_op jit(solution)/shard_map/all_to_all | solution.py:456
  41.8 29.0 %collective-permute-start.2 = (bf16[128,2048]{1,0:T(8,128)(2,1)S(1)}, bf16[128,2048]{1,0:T(8,128)(2,1)S(1)}, u32[]{:S(2)}, u32[]{:S(2)}) collective-permute-start(bf16[128,2048]{1,0:T(8,128)(2,1)S(1)} %copy-done.2), channel_id=1, source_target_pairs={{0,24},{8,16},{16,8},{24,0},{1,25},{9,17},{17,9},{25,1},{2,26},{10... | collective-permute-start | bytes 1572872 | tf_op jit(solution)/shard_map/ppermute | solution.py:447
  41.8 29.0 %collective-permute-start.1 = (bf16[128,2048]{1,0:T(8,128)(2,1)S(1)}, bf16[128,2048]{1,0:T(8,128)(2,1)S(1)}, u32[]{:S(2)}, u32[]{:S(2)}) collective-permute-start(bf16[128,2048]{1,0:T(8,128)(2,1)S(1)} %copy-done.2), channel_id=1, source_target_pairs={{0,16},{8,24},{16,0},{24,8},{1,17},{9,25},{17,1},{25,9},{2,18},{10... | collective-permute-start | bytes 1572872 | tf_op jit(solution)/shard_map/ppermute | solution.py:447
  42.6 28.3 %collective-permute-start = (bf16[128,2048]{1,0:T(8,128)(2,1)S(1)}, bf16[128,2048]{1,0:T(8,128)(2,1)S(1)}, u32[]{:S(2)}, u32[]{:S(2)}) collective-permute-start(bf16[128,2048]{1,0:T(8,128)(2,1)S(1)} %copy-done.2), channel_id=1, source_target_pairs={{0,8},{8,0},{16,24},{24,16},{1,9},{9,1},{17,25},{25,17},{2,10},{10... | collective-permute-start | bytes 1572872 | tf_op jit(solution)/shard_map/ppermute | solution.py:447
  96.8 6.3 %collective-permute-start.6 = (bf16[16,32,1024]{2,1,0:T(8,128)(2,1)S(1)}, bf16[16,32,1024]{2,1,0:T(8,128)(2,1)S(1)}, u32[]{:S(2)}, u32[]{:S(2)}) collective-permute-start(bf16[16,32,1024]{2,1,0:T(8,128)(2,1)S(1)} %get-tuple-element.43), channel_id=1, source_target_pairs={{0,32},{32,0},{1,33},{33,1},{2,34},{34,2},{3,35},{35,3},{4,36},{36... | collective-permute-start | bytes 3145736 | tf_op jit(solution)/shard_map/ppermute | solution.py:463
  104.5 31.5 %copy-start = (bf16[1,128,1024]{2,1,0:T(8,128)(2,1)S(1)}, bf16[1,128,1024]{2,1,0:T(8,128)(2,1)}, u32[]{:S(2)}) copy-start(bf16[1,128,1024]{2,1,0:T(8,128)(2,1)} %param.6) | copy-start | bytes 786436
  104.5 31.5 %copy-start.1 = (f32[1024]{0:T(1024)S(1)}, f32[1024]{0:T(1024)}, u32[]{:S(2)}) copy-start(f32[1024]{0:T(1024)} %param.7) | copy-start | bytes 12292
  104.6 20.8 %all-to-all-start.2 = ((bf16[16,32,1024]{2,1,0:T(8,128)(2,1)}), bf16[16,32,1024]{2,1,0:T(8,128)(2,1)S(1)}, u32[]{:S(2)}, u32[]{:S(2)}) async-start(bf16[16,32,1024]{2,1,0:T(8,128)(2,1)} %add_convert_fusion), calls=%async_computation.2 | async-start | bytes 2097152 | tf_op jit(solution)/shard_map/all_to_all | solution.py:466
  108.3 27.2 %collective-permute-start.3 = (bf16[128,1024]{1,0:T(8,128)(2,1)S(1)}, bf16[128,1024]{1,0:T(8,128)(2,1)S(1)}, u32[]{:S(2)}, u32[]{:S(2)}) collective-permute-start(bf16[128,1024]{1,0:T(8,128)(2,1)S(1)} %get-tuple-element.32.c1), channel_id=1, source_target_pairs={{0,8},{8,0},{16,24},{24,16},{1,9},{9,1},{17,25},{25,17},{2,10},{10... | collective-permute-start | bytes 786440 | tf_op jit(solution)/shard_map/ppermute | solution.py:447
  109.0 27.0 %collective-permute-start.4 = (bf16[128,1024]{1,0:T(8,128)(2,1)S(1)}, bf16[128,1024]{1,0:T(8,128)(2,1)S(1)}, u32[]{:S(2)}, u32[]{:S(2)}) collective-permute-start(bf16[128,1024]{1,0:T(8,128)(2,1)S(1)} %get-tuple-element.33.c2), channel_id=1, source_target_pairs={{0,16},{8,24},{16,0},{24,8},{1,17},{9,25},{17,1},{25,9},{2,18},{10... | collective-permute-start | bytes 786440 | tf_op jit(solution)/shard_map/ppermute | solution.py:447
  111.9 24.1 %collective-permute-start.5 = (bf16[128,1024]{1,0:T(8,128)(2,1)S(1)}, bf16[128,1024]{1,0:T(8,128)(2,1)S(1)}, u32[]{:S(2)}, u32[]{:S(2)}) collective-permute-start(bf16[128,1024]{1,0:T(8,128)(2,1)S(1)} %get-tuple-element.34.c3), channel_id=1, source_target_pairs={{0,24},{8,16},{16,8},{24,0},{1,25},{9,17},{17,9},{25,1},{2,26},{10... | collective-permute-start | bytes 786440 | tf_op jit(solution)/shard_map/ppermute | solution.py:447
  125.6 5.9 %collective-permute-start.7 = (bf16[32,768]{1,0:T(8,128)(2,1)S(1)}, bf16[32,768]{1,0:T(8,128)(2,1)S(1)}, u32[]{:S(2)}, u32[]{:S(2)}) collective-permute-start(bf16[32,768]{1,0:T(8,128)(2,1)S(1)} %slice.8), channel_id=1, source_target_pairs={{0,0},{8,32},{16,64},{24,96},{32,8},{40,40},{48,72},{56,104},{64,1... | collective-permute-start | bytes 147464 | tf_op jit(solution)/shard_map/ppermute | solution.py:471
  131.5 10.6 %collective-permute-start.10 = (bf16[32,1024]{1,0:T(8,128)(2,1)S(1)}, bf16[32,1024]{1,0:T(8,128)(2,1)S(1)}, u32[]{:S(2)}, u32[]{:S(2)}) collective-permute-start(bf16[32,1024]{1,0:T(8,128)(2,1)S(1)} %pad_maximum_fusion.a_ref), channel_id=1, source_target_pairs={{0,96},{32,64},{64,32},{96,0},{1,97},{33,65},{65,33},{97,1},{2,98}... | collective-permute-start | bytes 196616 | tf_op jit(solution)/shard_map/ppermute | solution.py:447
  135.5 6.5 %collective-permute-start.9 = (bf16[32,1024]{1,0:T(8,128)(2,1)S(1)}, bf16[32,1024]{1,0:T(8,128)(2,1)S(1)}, u32[]{:S(2)}, u32[]{:S(2)}) collective-permute-start(bf16[32,1024]{1,0:T(8,128)(2,1)S(1)} %pad_maximum_fusion.a_ref), channel_id=1, source_target_pairs={{0,64},{32,96},{64,0},{96,32},{1,65},{33,97},{65,1},{97,33},{2,66}... | collective-permute-start | bytes 196616 | tf_op jit(solution)/shard_map/ppermute | solution.py:447
  135.5 6.5 %collective-permute-start.8 = (bf16[32,1024]{1,0:T(8,128)(2,1)S(1)}, bf16[32,1024]{1,0:T(8,128)(2,1)S(1)}, u32[]{:S(2)}, u32[]{:S(2)}) collective-permute-start(bf16[32,1024]{1,0:T(8,128)(2,1)S(1)} %pad_maximum_fusion.a_ref), channel_id=1, source_target_pairs={{0,32},{32,0},{64,96},{96,64},{1,33},{33,1},{65,97},{97,65},{2,34}... | collective-permute-start | bytes 196616 | tf_op jit(solution)/shard_map/ppermute | solution.py:447

commit v7 on v6

--- a/solution.py
+++ b/solution.py
@@ -260,8 +260,12 @@
                 rows = pl.ds(pl.multiple_of(tiles[n].start, TOK), k * SUB)
                 dqt = dqt + dot_nn(kvt[:HEAD_DIM, rows], jnp.concatenate(ds[n:n + k], axis=0))
             added = [
-                acc[rows, :] + dot_nn(jnp.concatenate([a, b], axis=1), right)
-                for rows, a, b in zip(tiles, ds, e)
+                part
+                for n in range(0, len(tiles), 3)
+                for k in [min(3, len(tiles) - n)]
+                for big in [dot_nn(jnp.concatenate([jnp.concatenate(ds[n:n + k], axis=0), jnp.concatenate(e[n:n + k], axis=0)], axis=1), right)]
+                for t in range(k)
+                for part in [acc[tiles[n + t], :] + big[t * SUB:(t + 1) * SUB]]
             ]
             for rows, part in zip(tiles, added):
                 acc[rows, :] = part

time: 144 us -> 143 us (level)
  starting transfers between devices: 35 us -> 36.7 us
where the time goes in v7:
time: 143 us
  Pallas kernels  41.2 us (29%)
  waiting for transfers between devices  40.5 us (28%)
  starting transfers between devices  36.7 us (26%)
  blocking collectives  22 us (15%)
  other arithmetic  1.68 us (1%)
    pallas_call x1, Pallas kernels, attend(): pl.pallas_call(attend_kernel, in_specs=[vmem], out_specs=vmem, out_shape=...  25.4 us
    all_to_all x1, waiting for transfers between devices, shards(): recv = lax.all_to_all(send, ('x', 'r'), 0, 0, tiled=True)  23.6 us
    all_to_all x1, blocking collectives, shards(): back = lax.all_to_all(done, 'r', 0, 0, tiled=True)  22 us
    all_to_all x1, waiting for transfers between devices, shards(): parts = lax.all_to_all(terms, ('zl', 'r'), 0, 0, tiled=True)  12.8 us
    ppermute x9, starting transfers between devices, swap(): lax.ppermute(piece, axis, [(i, i ^ d) for i in range(4)])  11.7 us
    all_to_all x1, starting transfers between devices, shards(): recv = lax.all_to_all(send, ('x', 'r'), 0, 0, tiled=True)  11.3 us
    pallas_call x1, Pallas kernels, project(): pl.pallas_call(project_kernel, in_specs=[hbm] * 6, out_specs=[vmem] * 2,...  6.1 us
    pallas_call x1, Pallas kernels, unproject(): pl.pallas_call(unproject_kernel, in_specs=[pl.BlockSpec(memory_space=pltp...  6 us
  transfers between devices with their start and end apart: 13, of which 4 were waited for; matrix products, arithmetic and copies ran while one was open for 0% of the time, Pallas kernels for 22%

profile of v7, /device:TPU:1, one launch (start us, length us, event | category | flops | bytes accessed | tf_op | source)
XLA Modules:
  0.0 143.0 jit_solution(4661125922155513026)
XLA Ops:
  0.6 6.1 %project.1 = (bf16[32,208,128]{2,1,0:T(8,128)(2,1)}, bf16[128,2048]{1,0:T(8,128)(2,1)}) custom-call(bf16[128,1024]{1,0:T(8,128)(2,1)} %bitcast.8, bf16[128,1024]{1,0:T(8,128)(2,1)} %bitcast.12, f32[1,1024]{1,0:T(1,128)} %bitcast.10, s32[1,128]{1,0:T(1,128)} %ids_hbm.1, bf16[1024,3072]{1,0:T(8,128)(2,1)} %wqkv_hbm.3, bf16[1024,1024]{1,0:T(8,128)(2,1)} %wo_hbm.3), custom_call_target="tpu_custom_call" | custom-call | tf_op jit(solution)/shard_map/project/pallas_call | solution.py:111
  6.7 11.3 %all-to-all-start = ((bf16[32,208,128]{2,1,0:T(8,128)(2,1)}), bf16[32,208,128]{2,1,0:T(8,128)(2,1)S(1)}, u32[]{:S(2)}, u32[]{:S(2)}) async-start(bf16[32,208,128]{2,1,0:T(8,128)(2,1)} %get-tuple-element.25), calls=%async_computation | async-start | bytes 3407872 | tf_op jit(solution)/shard_map/all_to_all | solution.py:460
  18.1 0.1 pad_add_fusion.me_ref
  18.2 23.6 %all-to-all-done.recv_ref = bf16[32,208,128]{2,1,0:T(8,128)(2,1)S(1)} async-done(((bf16[32,208,128]{2,1,0:T(8,128)(2,1)}), bf16[32,208,128]{2,1,0:T(8,128)(2,1)S(1)}, u32[]{:S(2)}, u32[]{:S(2)}) %all-to-all-start) | async-done | bytes 1703968 | tf_op jit(solution)/shard_map/all_to_all | solution.py:460
  41.8 0.0 collective-permute-start.2
  41.8 0.8 collective-permute-start.1
  42.6 2.5 %collective-permute-start = (bf16[128,2048]{1,0:T(8,128)(2,1)S(1)}, bf16[128,2048]{1,0:T(8,128)(2,1)S(1)}, u32[]{:S(2)}, u32[]{:S(2)}) collective-permute-start(bf16[128,2048]{1,0:T(8,128)(2,1)S(1)} %copy-done.2), channel_id=1, source_target_pairs={{0,8},{8,0},{16,24},{24,16},{1,9},{9,1},{17,25},{25,17},{2,10},{10... | collective-permute-start | bytes 1572872 | tf_op jit(solution)/shard_map/ppermute | solution.py:451
  45.1 25.4 %attend.1 = bf16[8,4,192,128]{3,2,1,0:T(8,128)(2,1)S(1)} custom-call(bf16[32,208,128]{2,1,0:T(8,128)(2,1)S(1)} %all-to-all-done.recv_ref), custom_call_target="tpu_custom_call" | custom-call | flops 24999999488 | bytes 4000000 | tf_op jit(solution)/shard_map/attend/pallas_call | solution.py:293
  70.5 0.0 collective-permute-done.2.b3
  70.5 0.0 collective-permute-done.1.b2
  70.5 0.0 collective-permute-done.b1
  70.6 22.0 %all_to_all.15.recv_ref = bf16[8,4,192,128]{3,2,1,0:T(8,128)(2,1)S(1)} all-to-all(bf16[8,4,192,128]{3,2,1,0:T(8,128)(2,1)S(1)} %attend.1), channel_id=1, replica_groups=mesh['zl'=2,'core'=2,'x'=4,'r'=8] {'r'}, dimensions={0} | all-to-all | bytes 3145728 | tf_op jit(solution)/shard_map/all_to_all | solution.py:464
  92.6 1.0 repack.1
  93.6 1.9 %weights.1 = (bf16[16,32,1024]{2,1,0:T(8,128)(2,1)S(1)}, bf16[16,32,1024]{2,1,0:T(8,128)(2,1)S(1)}) custom-call(s32[2]{0:T(128)S(1)} %pad_add_fusion.me_ref, bf16[128,1024]{1,0:T(8,128)(2,1)S(1)} %get-tuple-element.31.c0, bf16[128,1024]{1,0:T(8,128)(2,1)S(1)} %get-tuple-element.32.c1, bf16[128,1024]{1,0:T(8,128)(2,1)S(1)} %get-tuple-element.33.c2, ...), custom_call_target="tpu_custom_call" | custom-call | flops 2000000000 | bytes 4000000 | tf_op jit(solution)/shard_map/weights/pallas_call | solution.py:417
  95.4 5.2 %collective-permute-start.6 = (bf16[16,32,1024]{2,1,0:T(8,128)(2,1)S(1)}, bf16[16,32,1024]{2,1,0:T(8,128)(2,1)S(1)}, u32[]{:S(2)}, u32[]{:S(2)}) collective-permute-start(bf16[16,32,1024]{2,1,0:T(8,128)(2,1)S(1)} %get-tuple-element.43), channel_id=1, source_target_pairs={{0,32},{32,0},{1,33},{33,1},{2,34},{34,2},{3,35},{35,3},{4,36},{36... | collective-permute-start | bytes 3145736 | tf_op jit(solution)/shard_map/ppermute | solution.py:467
  100.6 2.3 %collective-permute-done.6 = bf16[16,32,1024]{2,1,0:T(8,128)(2,1)S(1)} collective-permute-done((bf16[16,32,1024]{2,1,0:T(8,128)(2,1)S(1)}, bf16[16,32,1024]{2,1,0:T(8,128)(2,1)S(1)}, u32[]{:S(2)}, u32[]{:S(2)}) %collective-permute-start.6) | collective-permute-done | bytes 1048608 | tf_op jit(solution)/shard_map/ppermute | solution.py:467
  102.9 1.4 add_convert_fusion
  104.3 4.3 %all-to-all-start.2 = ((bf16[16,32,1024]{2,1,0:T(8,128)(2,1)}), bf16[16,32,1024]{2,1,0:T(8,128)(2,1)S(1)}, u32[]{:S(2)}, u32[]{:S(2)}) async-start(bf16[16,32,1024]{2,1,0:T(8,128)(2,1)} %add_convert_fusion), calls=%async_computation.2 | async-start | bytes 2097152 | tf_op jit(solution)/shard_map/all_to_all | solution.py:470
  108.6 0.8 collective-permute-start.3
  109.4 2.9 %collective-permute-start.4 = (bf16[128,1024]{1,0:T(8,128)(2,1)S(1)}, bf16[128,1024]{1,0:T(8,128)(2,1)S(1)}, u32[]{:S(2)}, u32[]{:S(2)}) collective-permute-start(bf16[128,1024]{1,0:T(8,128)(2,1)S(1)} %get-tuple-element.33.c2), channel_id=1, source_target_pairs={{0,16},{8,24},{16,0},{24,8},{1,17},{9,25},{17,1},{25,9},{2,18},{10... | collective-permute-start | bytes 786440 | tf_op jit(solution)/shard_map/ppermute | solution.py:451
  112.3 0.2 collective-permute-start.5
  112.5 12.8 %all-to-all-done.2 = bf16[16,32,1024]{2,1,0:T(8,128)(2,1)S(1)} async-done(((bf16[16,32,1024]{2,1,0:T(8,128)(2,1)}), bf16[16,32,1024]{2,1,0:T(8,128)(2,1)S(1)}, u32[]{:S(2)}, u32[]{:S(2)}) %all-to-all-start.2) | async-done | bytes 1048608 | tf_op jit(solution)/shard_map/all_to_all | solution.py:470
  125.3 0.2 convert_reduce_fusion
  125.5 4.3 %collective-permute-start.7 = (bf16[32,768]{1,0:T(8,128)(2,1)S(1)}, bf16[32,768]{1,0:T(8,128)(2,1)S(1)}, u32[]{:S(2)}, u32[]{:S(2)}) collective-permute-start(bf16[32,768]{1,0:T(8,128)(2,1)S(1)} %slice.8), channel_id=1, source_target_pairs={{0,0},{8,32},{16,64},{24,96},{32,8},{40,40},{48,72},{56,104},{64,1... | collective-permute-start | bytes 147464 | tf_op jit(solution)/shard_map/ppermute | solution.py:475
  129.8 1.7 %collective-permute-done.7 = bf16[32,768]{1,0:T(8,128)(2,1)S(1)} collective-permute-done((bf16[32,768]{1,0:T(8,128)(2,1)S(1)}, bf16[32,768]{1,0:T(8,128)(2,1)S(1)}, u32[]{:S(2)}, u32[]{:S(2)}) %collective-permute-start.7) | collective-permute-done | bytes 49184 | tf_op jit(solution)/shard_map/ppermute | solution.py:475
  131.6 4.0 %collective-permute-start.10 = (bf16[32,1024]{1,0:T(8,128)(2,1)S(1)}, bf16[32,1024]{1,0:T(8,128)(2,1)S(1)}, u32[]{:S(2)}, u32[]{:S(2)}) collective-permute-start(bf16[32,1024]{1,0:T(8,128)(2,1)S(1)} %pad_maximum_fusion.a_ref), channel_id=1, source_target_pairs={{0,96},{32,64},{64,32},{96,0},{1,97},{33,65},{65,33},{97,1},{2,98}... | collective-permute-start | bytes 196616 | tf_op jit(solution)/shard_map/ppermute | solution.py:451
  135.6 0.0 collective-permute-start.9
  135.6 0.5 collective-permute-start.8
  136.1 6.0 %unproject.1 = (bf16[128,1024]{1,0:T(8,128)(2,1)}, bf16[128,1024]{1,0:T(8,128)(2,1)}) custom-call(s32[2]{0:T(128)S(1)} %pad_add_fusion.me_ref, bf16[128,1024]{1,0:T(8,128)(2,1)S(1)} %get-tuple-element.31.c0, bf16[128,1024]{1,0:T(8,128)(2,1)S(1)} %collective-permute-done.3.c1, bf16[128,1024]{1,0:T(8,128)(2,1)S(1)} %collective-permute-done.4.c2, ...), custom_call_target="tpu_custom_call" | custom-call | flops 7000000000 | bytes 10000000 | tf_op jit(solution)/shard_map/unproject/pallas_call | solution.py:350
  142.1 0.0 collective-permute-done.10.d_ref
  142.1 0.0 collective-permute-done.9.c_ref
  142.2 0.8 assemble.1
  (14 shorter events, 0.0 us)
Async XLA Ops:
  6.7 35.1 %copy-start.2 = (bf16[128,2048]{1,0:T(8,128)(2,1)S(1)}, bf16[128,2048]{1,0:T(8,128)(2,1)}, u32[]{:S(2)}) copy-start(bf16[128,2048]{1,0:T(8,128)(2,1)} %get-tuple-element.38.b0) | copy-start | bytes 1572868
  6.7 35.1 %all-to-all-start = ((bf16[32,208,128]{2,1,0:T(8,128)(2,1)}), bf16[32,208,128]{2,1,0:T(8,128)(2,1)S(1)}, u32[]{:S(2)}, u32[]{:S(2)}) async-start(bf16[32,208,128]{2,1,0:T(8,128)(2,1)} %get-tuple-element.25), calls=%async_computation | async-start | bytes 3407872 | tf_op jit(solution)/shard_map/all_to_all | solution.py:460
  41.8 28.7 %collective-permute-start.2 = (bf16[128,2048]{1,0:T(8,128)(2,1)S(1)}, bf16[128,2048]{1,0:T(8,128)(2,1)S(1)}, u32[]{:S(2)}, u32[]{:S(2)}) collective-permute-start(bf16[128,2048]{1,0:T(8,128)(2,1)S(1)} %copy-done.2), channel_id=1, source_target_pairs={{0,24},{8,16},{16,8},{24,0},{1,25},{9,17},{17,9},{25,1},{2,26},{10... | collective-permute-start | bytes 1572872 | tf_op jit(solution)/shard_map/ppermute | solution.py:451
  41.8 28.7 %collective-permute-start.1 = (bf16[128,2048]{1,0:T(8,128)(2,1)S(1)}, bf16[128,2048]{1,0:T(8,128)(2,1)S(1)}, u32[]{:S(2)}, u32[]{:S(2)}) collective-permute-start(bf16[128,2048]{1,0:T(8,128)(2,1)S(1)} %copy-done.2), channel_id=1, source_target_pairs={{0,16},{8,24},{16,0},{24,8},{1,17},{9,25},{17,1},{25,9},{2,18},{10... | collective-permute-start | bytes 1572872 | tf_op jit(solution)/shard_map/ppermute | solution.py:451
  42.6 28.0 %collective-permute-start = (bf16[128,2048]{1,0:T(8,128)(2,1)S(1)}, bf16[128,2048]{1,0:T(8,128)(2,1)S(1)}, u32[]{:S(2)}, u32[]{:S(2)}) collective-permute-start(bf16[128,2048]{1,0:T(8,128)(2,1)S(1)} %copy-done.2), channel_id=1, source_target_pairs={{0,8},{8,0},{16,24},{24,16},{1,9},{9,1},{17,25},{25,17},{2,10},{10... | collective-permute-start | bytes 1572872 | tf_op jit(solution)/shard_map/ppermute | solution.py:451
  95.4 7.4 %collective-permute-start.6 = (bf16[16,32,1024]{2,1,0:T(8,128)(2,1)S(1)}, bf16[16,32,1024]{2,1,0:T(8,128)(2,1)S(1)}, u32[]{:S(2)}, u32[]{:S(2)}) collective-permute-start(bf16[16,32,1024]{2,1,0:T(8,128)(2,1)S(1)} %get-tuple-element.43), channel_id=1, source_target_pairs={{0,32},{32,0},{1,33},{33,1},{2,34},{34,2},{3,35},{35,3},{4,36},{36... | collective-permute-start | bytes 3145736 | tf_op jit(solution)/shard_map/ppermute | solution.py:467
  104.3 31.8 %copy-start = (bf16[1,128,1024]{2,1,0:T(8,128)(2,1)S(1)}, bf16[1,128,1024]{2,1,0:T(8,128)(2,1)}, u32[]{:S(2)}) copy-start(bf16[1,128,1024]{2,1,0:T(8,128)(2,1)} %param.6) | copy-start | bytes 786436
  104.3 31.8 %copy-start.1 = (f32[1024]{0:T(1024)S(1)}, f32[1024]{0:T(1024)}, u32[]{:S(2)}) copy-start(f32[1024]{0:T(1024)} %param.7) | copy-start | bytes 12292
  104.3 21.0 %all-to-all-start.2 = ((bf16[16,32,1024]{2,1,0:T(8,128)(2,1)}), bf16[16,32,1024]{2,1,0:T(8,128)(2,1)S(1)}, u32[]{:S(2)}, u32[]{:S(2)}) async-start(bf16[16,32,1024]{2,1,0:T(8,128)(2,1)} %add_convert_fusion), calls=%async_computation.2 | async-start | bytes 2097152 | tf_op jit(solution)/shard_map/all_to_all | solution.py:470
  108.6 27.0 %collective-permute-start.3 = (bf16[128,1024]{1,0:T(8,128)(2,1)S(1)}, bf16[128,1024]{1,0:T(8,128)(2,1)S(1)}, u32[]{:S(2)}, u32[]{:S(2)}) collective-permute-start(bf16[128,1024]{1,0:T(8,128)(2,1)S(1)} %get-tuple-element.32.c1), channel_id=1, source_target_pairs={{0,8},{8,0},{16,24},{24,16},{1,9},{9,1},{17,25},{25,17},{2,10},{10... | collective-permute-start | bytes 786440 | tf_op jit(solution)/shard_map/ppermute | solution.py:451
  109.4 26.7 %collective-permute-start.4 = (bf16[128,1024]{1,0:T(8,128)(2,1)S(1)}, bf16[128,1024]{1,0:T(8,128)(2,1)S(1)}, u32[]{:S(2)}, u32[]{:S(2)}) collective-permute-start(bf16[128,1024]{1,0:T(8,128)(2,1)S(1)} %get-tuple-element.33.c2), channel_id=1, source_target_pairs={{0,16},{8,24},{16,0},{24,8},{1,17},{9,25},{17,1},{25,9},{2,18},{10... | collective-permute-start | bytes 786440 | tf_op jit(solution)/shard_map/ppermute | solution.py:451
  112.3 23.8 %collective-permute-start.5 = (bf16[128,1024]{1,0:T(8,128)(2,1)S(1)}, bf16[128,1024]{1,0:T(8,128)(2,1)S(1)}, u32[]{:S(2)}, u32[]{:S(2)}) collective-permute-start(bf16[128,1024]{1,0:T(8,128)(2,1)S(1)} %get-tuple-element.34.c3), channel_id=1, source_target_pairs={{0,24},{8,16},{16,8},{24,0},{1,25},{9,17},{17,9},{25,1},{2,26},{10... | collective-permute-start | bytes 786440 | tf_op jit(solution)/shard_map/ppermute | solution.py:451
  125.5 6.0 %collective-permute-start.7 = (bf16[32,768]{1,0:T(8,128)(2,1)S(1)}, bf16[32,768]{1,0:T(8,128)(2,1)S(1)}, u32[]{:S(2)}, u32[]{:S(2)}) collective-permute-start(bf16[32,768]{1,0:T(8,128)(2,1)S(1)} %slice.8), channel_id=1, source_target_pairs={{0,0},{8,32},{16,64},{24,96},{32,8},{40,40},{48,72},{56,104},{64,1... | collective-permute-start | bytes 147464 | tf_op jit(solution)/shard_map/ppermute | solution.py:475
  131.6 10.5 %collective-permute-start.10 = (bf16[32,1024]{1,0:T(8,128)(2,1)S(1)}, bf16[32,1024]{1,0:T(8,128)(2,1)S(1)}, u32[]{:S(2)}, u32[]{:S(2)}) collective-permute-start(bf16[32,1024]{1,0:T(8,128)(2,1)S(1)} %pad_maximum_fusion.a_ref), channel_id=1, source_target_pairs={{0,96},{32,64},{64,32},{96,0},{1,97},{33,65},{65,33},{97,1},{2,98}... | collective-permute-start | bytes 196616 | tf_op jit(solution)/shard_map/ppermute | solution.py:451
  135.6 6.5 %collective-permute-start.9 = (bf16[32,1024]{1,0:T(8,128)(2,1)S(1)}, bf16[32,1024]{1,0:T(8,128)(2,1)S(1)}, u32[]{:S(2)}, u32[]{:S(2)}) collective-permute-start(bf16[32,1024]{1,0:T(8,128)(2,1)S(1)} %pad_maximum_fusion.a_ref), channel_id=1, source_target_pairs={{0,64},{32,96},{64,0},{96,32},{1,65},{33,97},{65,1},{97,33},{2,66}... | collective-permute-start | bytes 196616 | tf_op jit(solution)/shard_map/ppermute | solution.py:451
  135.6 6.5 %collective-permute-start.8 = (bf16[32,1024]{1,0:T(8,128)(2,1)S(1)}, bf16[32,1024]{1,0:T(8,128)(2,1)S(1)}, u32[]{:S(2)}, u32[]{:S(2)}) collective-permute-start(bf16[32,1024]{1,0:T(8,128)(2,1)S(1)} %pad_maximum_fusion.a_ref), channel_id=1, source_target_pairs={{0,32},{32,0},{64,96},{96,64},{1,33},{33,1},{65,97},{97,65},{2,34}... | collective-permute-start | bytes 196616 | tf_op jit(solution)/shard_map/ppermute | solution.py:451
